TPU v7x, 32 devices: a whole 2x2x4 slice. The times are simulated.
32 devices in a mesh: dp: 2 (over core), graph: 4 (over z), mp: 4 (over y, x).
Axes of the slice: x: 2, y: 2, z: 4, core: 2. Of those that a mesh axis runs over, the one named last changes fastest.
Arguments:
- nodes: bfloat16 [2, 512, 512], P('dp', 'graph'), may hold values from -6 to 6
- edges: bfloat16 [2, 512, 60, 192], P('dp', 'graph', 'mp'), may hold values from -6 to 6
- neighbours: int32 [2, 512, 60], P('dp', 'graph'), may hold values from 0 to 511, as said below
- resmask: int32 [2, 512], P('dp'), may hold values 0 or 1
- node_gain_a: float32 [512], replicated, may hold values from 0.25 to 1.75
- edge_gain_a: float32 [192], replicated, may hold values from 0.25 to 1.75
- message_self: bfloat16 [512, 512], P(None, 'mp'), may hold values from -0.15625 to 0.15625
- message_other: bfloat16 [512, 512], P(None, 'mp'), may hold values from -0.15625 to 0.15625
- message_edge: bfloat16 [192, 512], P(None, 'mp'), may hold values from -0.15625 to 0.15625
- message_out: bfloat16 [512, 512], P('mp'), may hold values from -0.5 to 0.5
- node_gain_b: float32 [512], replicated, may hold values from 0.25 to 1.75
- ffn_in: bfloat16 [512, 2048], P(None, 'mp'), may hold values from -0.25 to 0.25
- ffn_out: bfloat16 [2048, 512], P('mp'), may hold values from -0.25 to 0.25
- node_gain_c: float32 [512], replicated, may hold values from 0.25 to 1.75
- edge_gain_b: float32 [192], replicated, may hold values from 0.25 to 1.75
- update_self: bfloat16 [512, 512], P(None, 'mp'), may hold values from -0.15625 to 0.15625
- update_other: bfloat16 [512, 512], P(None, 'mp'), may hold values from -0.15625 to 0.15625
- update_edge: bfloat16 [192, 512], P(None, 'mp'), may hold values from -0.15625 to 0.15625
- update_out: bfloat16 [512, 192], P('mp'), may hold values from -0.375 to 0.375
- node_cot: bfloat16 [2, 512, 512], P('dp', 'graph'), may hold values from -6 to 6
- edge_cot: bfloat16 [2, 512, 60, 192], P('dp', 'graph', 'mp'), may hold values from -6 to 6
Outputs:
- nodes_out: bfloat16 [2, 512, 512], P('dp', 'graph')
- edges_out: bfloat16 [2, 512, 60, 192], P('dp', 'graph', 'mp')
- grad_nodes: float32 [2, 512, 512], P('dp', 'graph')
- grad_edges: float32 [2, 512, 60, 192], P('dp', 'graph', 'mp')
- grad_node_gain_a: float32 [512], replicated
- grad_edge_gain_a: float32 [192], replicated
- grad_message_self: float32 [512, 512], P(None, 'mp')
- grad_message_other: float32 [512, 512], P(None, 'mp')
- grad_message_edge: float32 [192, 512], P(None, 'mp')
- grad_message_out: float32 [512, 512], P('mp')
- grad_node_gain_b: float32 [512], replicated
- grad_ffn_in: float32 [512, 2048], P(None, 'mp')
- grad_ffn_out: float32 [2048, 512], P('mp')
- grad_node_gain_c: float32 [512], replicated
- grad_edge_gain_b: float32 [192], replicated
- grad_update_self: float32 [512, 512], P(None, 'mp')
- grad_update_other: float32 [512, 512], P(None, 'mp')
- grad_update_edge: float32 [192, 512], P(None, 'mp')
- grad_update_out: float32 [512, 192], P('mp')
Inputs may be any that keep to these rules, and one draw needn't show every extreme that they name: `neighbours`: each row holds 60 different residue numbers of the same complex, none equal to the row's own residue.
All inputs are finite; a program needn't handle non-finite values. No bound on the sum of `resmask` on one device may be relied on, other than what follows from the above.
Results may differ from a plain program's by a relative error of at most 0.02.
Values may be sent and summed in bfloat16 or wider, within the bound.
No kernel may reach another device: no remote copies, remote signals or barrier semaphores. Data moves between devices by JAX's collectives and lax.ppermute only.
A program may use at most 128 MiB of HBM per device.

v0:
```python
import jax
import jax.numpy as jnp
from jax import lax
from jax.sharding import PartitionSpec as P

EPSILON = 1e-05


def normalize(values):
    centre = values - jnp.mean(values, axis=-1, keepdims=True)
    variance = jnp.mean(centre * centre, axis=-1, keepdims=True)
    scale_inv = lax.rsqrt(variance + EPSILON)
    return (centre * scale_inv, scale_inv)


def norm_back(grad_hat, normed, scale_inv):
    return scale_inv * (
        grad_hat
        - jnp.mean(grad_hat, axis=-1, keepdims=True)
        - normed * jnp.mean(grad_hat * normed, axis=-1, keepdims=True)
    )


def gelu_back(preact, grad_out):
    return jax.vjp(jax.nn.gelu, preact)[1](grad_out)[0]


def mixed(form, left, right):
    return jnp.einsum(form, left, right, preferred_element_type=jnp.float32)


def unit_sum(partial_sum):
    return lax.psum(partial_sum, "mp")


def fetch_rows(features, flat_index):
    whole = lax.all_gather(features, "graph", axis=1, tiled=True)
    return jnp.take_along_axis(whole, flat_index[:, :, None], axis=1)


def return_rows(terms, flat_index, total_rows):
    num_cplx = flat_index.shape[0]
    width = terms.shape[-1]
    offsets = flat_index + jnp.arange(num_cplx, dtype=jnp.int32)[:, None] * total_rows
    pooled = jax.ops.segment_sum(
        terms.reshape(-1, width), offsets.reshape(-1), num_segments=num_cplx * total_rows
    )
    pooled = pooled.reshape(num_cplx, total_rows, width)
    return lax.psum_scatter(
        pooled.astype(jnp.bfloat16), "graph", scatter_dimension=1, tiled=True
    ).astype(jnp.float32)


def other_forward(low_rows, weight_other, flat_index, slot_shape):
    taken_rows = fetch_rows(low_rows, flat_index).reshape(slot_shape + (low_rows.shape[2],))
    return (mixed("crkd,dh->crkh", taken_rows, weight_other), taken_rows)


def other_backward(grad_pre, kept_rows, weight_other, flat_index, total_rows):
    grad_weight = mixed("crkd,crkh->dh", kept_rows, grad_pre)
    node_term = return_rows(mixed("crkh,dh->crkd", grad_pre, weight_other), flat_index, total_rows)
    return (grad_weight, node_term)


def local(
    nodes,
    edges,
    neighbours,
    resmask,
    node_gain_a,
    edge_gain_a,
    message_self,
    message_other,
    message_edge,
    message_out,
    node_gain_b,
    ffn_in,
    ffn_out,
    node_gain_c,
    edge_gain_b,
    update_self,
    update_other,
    update_edge,
    update_out,
    node_cot,
    edge_cot,
):
    num_cplx, res_rows, width = nodes.shape
    nbr_count = neighbours.shape[2]
    total_rows = resmask.shape[1]
    msg_self, msg_other, msg_edge = (message_self, message_other, message_edge)
    upd_self, upd_other, upd_edge = (update_self, update_other, update_edge)
    msg_out, upd_out = (message_out, update_out)
    edge_full, cot_full = (
        lax.all_gather(edges, "mp", axis=2, tiled=True),
        lax.all_gather(edge_cot, "mp", axis=2, tiled=True),
    )
    slot_here = neighbours.shape[2]
    slot_shape = (num_cplx, res_rows, slot_here)
    flat_index = neighbours.reshape(num_cplx, res_rows * slot_here)
    weight_mask = jnp.take_along_axis(resmask, flat_index, axis=1).astype(jnp.float32)
    weight_mask = weight_mask.reshape(slot_shape) / nbr_count
    node_full = nodes.astype(jnp.float32)
    hat_one, inv_one = normalize(node_full)
    node_low = (hat_one * node_gain_a).astype(jnp.bfloat16)
    other_msg, other_low = other_forward(node_low, msg_other, flat_index, slot_shape)
    edge_hat, edge_inv = normalize(edge_full.astype(jnp.float32))
    edge_low = (edge_hat * edge_gain_a).astype(jnp.bfloat16)
    edge_lowb = (edge_hat * edge_gain_b).astype(jnp.bfloat16)
    pre_msg = (
        mixed("crd,dh->crh", node_low, msg_self)[:, :, None, :]
        + other_msg
        + mixed("crke,eh->crkh", edge_low, msg_edge)
    )
    act_msg = jax.nn.gelu(pre_msg).astype(jnp.bfloat16)
    pooled_part = jnp.sum(act_msg.astype(jnp.float32) * weight_mask[..., None], axis=2)
    pooled = pooled_part.astype(jnp.bfloat16)
    node_one = node_full + unit_sum(mixed("crh,hd->crd", pooled, msg_out))
    hat_two, inv_two = normalize(node_one)
    ffn_low = (hat_two * node_gain_b).astype(jnp.bfloat16)
    pre_ffn = mixed("crd,df->crf", ffn_low, ffn_in)
    act_ffn = jax.nn.gelu(pre_ffn).astype(jnp.bfloat16)
    node_two = node_one + unit_sum(mixed("crf,fd->crd", act_ffn, ffn_out))
    hat_three, inv_three = normalize(node_two)
    third_low = (hat_three * node_gain_c).astype(jnp.bfloat16)
    other_upd, third_other = other_forward(third_low, upd_other, flat_index, slot_shape)
    pre_upd = (
        mixed("crd,dh->crh", third_low, upd_self)[:, :, None, :]
        + other_upd
        + mixed("crke,eh->crkh", edge_lowb, upd_edge)
    )
    act_upd = jax.nn.gelu(pre_upd).astype(jnp.bfloat16)
    edge_delta = lax.psum_scatter(
        mixed("crkh,he->crke", act_upd, upd_out).astype(jnp.bfloat16),
        "mp",
        scatter_dimension=2,
        tiled=True,
    ).astype(jnp.float32)
    edges_out = (edges.astype(jnp.float32) + edge_delta).astype(jnp.bfloat16)
    nodes_out = node_two.astype(jnp.bfloat16)
    grad_act = mixed("crke,he->crkh", cot_full, upd_out)
    grad_pre = gelu_back(pre_upd, grad_act).astype(jnp.bfloat16)
    grad_upd_self = mixed("crd,crkh->dh", third_low, grad_pre)
    grad_upd_edge = mixed("crke,crkh->eh", edge_lowb, grad_pre)
    grad_upd_other, third_back = other_backward(
        grad_pre, third_other, upd_other, flat_index, total_rows
    )
    third_part = mixed("crkh,dh->crd", grad_pre, upd_self) + third_back
    edgeb_part = mixed("crkh,eh->crke", grad_pre, upd_edge)
    grad_third = unit_sum(third_part)
    grad_gain_c = jnp.sum(grad_third * hat_three, axis=(0, 1))
    grad_two = node_cot.astype(jnp.float32) + norm_back(
        grad_third * node_gain_c, hat_three, inv_three
    )
    grad_two_low = grad_two.astype(jnp.bfloat16)
    grad_lin_out = mixed("crf,crd->fd", act_ffn, grad_two_low)
    grad_act_ffn = mixed("crd,fd->crf", grad_two_low, ffn_out)
    grad_pre_ffn = gelu_back(pre_ffn, grad_act_ffn).astype(jnp.bfloat16)
    grad_lin_in = mixed("crd,crf->df", ffn_low, grad_pre_ffn)
    grad_ffn_low = unit_sum(mixed("crf,df->crd", grad_pre_ffn, ffn_in))
    grad_gain_b = jnp.sum(grad_ffn_low * hat_two, axis=(0, 1))
    grad_one = grad_two + norm_back(grad_ffn_low * node_gain_b, hat_two, inv_two)
    grad_one_low = grad_one.astype(jnp.bfloat16)
    grad_pooled = mixed("crd,hd->crh", grad_one_low, msg_out)
    grad_act_msg = grad_pooled[:, :, None, :] * weight_mask[..., None]
    grad_pre_msg = gelu_back(pre_msg, grad_act_msg).astype(jnp.bfloat16)
    grad_msg_self = mixed("crd,crkh->dh", node_low, grad_pre_msg)
    grad_msg_edge = mixed("crke,crkh->eh", edge_low, grad_pre_msg)
    grad_msg_other, node_back = other_backward(
        grad_pre_msg, other_low, msg_other, flat_index, total_rows
    )
    node_part = mixed("crkh,dh->crd", grad_pre_msg, msg_self) + node_back
    edgea_part = mixed("crkh,eh->crke", grad_pre_msg, msg_edge)
    local_hat, local_inv = normalize(edges.astype(jnp.float32))
    grad_edge_a, grad_edge_b = (
        lax.psum_scatter(
            edgea_part.astype(jnp.bfloat16), "mp", scatter_dimension=2, tiled=True
        ).astype(jnp.float32),
        lax.psum_scatter(
            edgeb_part.astype(jnp.bfloat16), "mp", scatter_dimension=2, tiled=True
        ).astype(jnp.float32),
    )
    gain_a_part = jnp.sum(grad_edge_a * local_hat, axis=(0, 1, 2))
    gain_b_part = jnp.sum(grad_edge_b * local_hat, axis=(0, 1, 2))
    grad_hat_edge = edge_gain_a * grad_edge_a + edge_gain_b * grad_edge_b
    grad_edges = edge_cot.astype(jnp.float32) + norm_back(grad_hat_edge, local_hat, local_inv)
    grad_node_low, grad_gain_ea, grad_gain_eb = unit_sum((node_part, gain_a_part, gain_b_part))
    grad_gain_a = jnp.sum(grad_node_low * hat_one, axis=(0, 1))
    grad_nodes = grad_one + norm_back(grad_node_low * node_gain_a, hat_one, inv_one)
    grad_upd_out = mixed("crkh,crke->he", act_upd, cot_full)
    grad_msg_out = mixed("crh,crd->hd", pooled, grad_one_low)
    summed = lax.psum(
        (
            grad_gain_a,
            grad_gain_ea,
            grad_msg_self,
            grad_msg_other,
            grad_msg_edge,
            grad_msg_out,
            grad_gain_b,
            grad_lin_in,
            grad_lin_out,
            grad_gain_c,
            grad_gain_eb,
            grad_upd_self,
            grad_upd_other,
            grad_upd_edge,
            grad_upd_out,
        ),
        ("dp", "graph"),
    )
    return (
        nodes_out,
        edges_out,
        grad_nodes,
        grad_edges,
        summed[0],
        summed[1],
        summed[2],
        summed[3],
        summed[4],
        summed[5],
        summed[6],
        summed[7],
        summed[8],
        summed[9],
        summed[10],
        summed[11],
        summed[12],
        summed[13],
        summed[14],
    )


def solution(mesh):
    return jax.shard_map(
        local,
        mesh=mesh,
        in_specs=(
            P("dp", "graph", None),
            P("dp", "graph", "mp", None),
            P("dp", "graph", None),
            P("dp", None),
            P(),
            P(),
            P(None, "mp"),
            P(None, "mp"),
            P(None, "mp"),
            P("mp", None),
            P(),
            P(None, "mp"),
            P("mp", None),
            P(),
            P(),
            P(None, "mp"),
            P(None, "mp"),
            P(None, "mp"),
            P("mp", None),
            P("dp", "graph", None),
            P("dp", "graph", "mp", None),
        ),
        out_specs=(
            P("dp", "graph", None),
            P("dp", "graph", "mp", None),
            P("dp", "graph", None),
            P("dp", "graph", "mp", None),
            P(),
            P(),
            P(None, "mp"),
            P(None, "mp"),
            P(None, "mp"),
            P("mp", None),
            P(),
            P(None, "mp"),
            P("mp", None),
            P(),
            P(),
            P(None, "mp"),
            P(None, "mp"),
            P(None, "mp"),
            P("mp", None),
        ),
        check_vma=False,
    )
```

profile of v0, /device:TPU:0, one launch (start us, length us, event | category | flops | bytes accessed | tf_op | source)
XLA Modules:
  0.0 906.2 jit_solution(11914982003806754142)
XLA Ops:
  9.3 45.2 %gather_fusion = s32[7680]{0:T(1024)S(1)} fusion(s32[512]{0:T(512)S(1)} %bitcast.174, s32[8192]{0:T(1024)S(1)} %pad_clamp_fusion), kind=kCustom, calls=%fused_computation.2 | custom fusion | bytes 92160 | tf_op jit(solution)/shard_map/jit(take_along_axis)/gather | solution.py:101
  55.4 17.4 %all_gather.12 = bf16[1,512,512]{2,1,0:T(8,128)(2,1)S(1)} all-gather(bf16[1,128,512]{2,1,0:T(8,128)(2,1)S(1)} %fusion.65), channel_id=1, replica_groups=mesh['dp'=2,'graph'=4,'mp'=4] {'graph'}, dimensions={1}, use_global_device_ids=true | all-gather | bytes 655360 | tf_op jit(solution)/shard_map/all_gather | solution.py:37
  72.7 22.2 %gather_fusion.1 = bf16[7680,512]{1,0:T(8,128)(2,1)} fusion(bf16[512,512]{1,0:T(8,128)(2,1)S(1)} %bitcast.176, s32[8192]{0:T(1024)S(1)} %pad_clamp_fusion.1), kind=kCustom, calls=%fused_computation.clone | custom fusion | bytes 15759360 | tf_op jit(solution)/shard_map/jit(take_along_axis)/gather | solution.py:38
  103.7 11.1 %reshape.595 = bf16[128,60,512]{2,1,0:T(8,128)(2,1)} reshape(bf16[1,7680,512]{2,1,0:T(8,128)(2,1)} %bitcast_select_fusion.1) | data formatting | bytes 15728640 | tf_op jit(solution)/shard_map/reshape.11
  114.8 12.9 %copy.70 = bf16[128,60,512]{0,2,1:T(8,128)(2,1)} copy(bf16[128,60,512]{2,1,0:T(8,128)(2,1)} %reshape.595) | data formatting | bytes 15728640 | tf_op jit(solution)/shard_map/reshape.11
  146.5 44.8 %all-reduce.13.cloned.1.call-done = f32[1,128,512]{2,1,0:T(8,128)} async-done(((f32[1,128,512]{2,1,0:T(8,128)}), f32[1,128,512]{2,1,0:T(8,128)}) %all-reduce.13.cloned.1.call-update) | async-done | bytes 262160 | tf_op jit(solution)/shard_map/psum | solution.py:33
  195.9 42.1 %all-reduce.15.cloned.1.call-done = f32[1,128,512]{2,1,0:T(8,128)} async-done(((f32[1,128,512]{2,1,0:T(8,128)}), f32[1,128,512]{2,1,0:T(8,128)}) %all-reduce.15.cloned.1.call-update) | async-done | bytes 262160 | tf_op jit(solution)/shard_map/psum | solution.py:33
  239.8 15.8 %all_gather.14 = bf16[1,512,512]{2,1,0:T(8,128)(2,1)S(1)} all-gather(bf16[1,128,512]{2,1,0:T(8,128)(2,1)S(1)} %multiply_convert_fusion.2), channel_id=1, replica_groups=mesh['dp'=2,'graph'=4,'mp'=4] {'graph'}, dimensions={1}, use_global_device_ids=true | all-gather | bytes 655360 | tf_op jit(solution)/shard_map/all_gather | solution.py:37
  255.5 22.2 %gather_fusion.2 = bf16[7680,512]{1,0:T(8,128)(2,1)} fusion(bf16[512,512]{1,0:T(8,128)(2,1)S(1)} %bitcast.175, s32[8192]{0:T(1024)S(1)} %pad_clamp_fusion.1), kind=kCustom, calls=%fused_computation.1.clone | custom fusion | bytes 15759360 | tf_op jit(solution)/shard_map/jit(take_along_axis)/gather | solution.py:38
  286.4 11.1 %reshape.600 = bf16[128,60,512]{2,1,0:T(8,128)(2,1)} reshape(bf16[1,7680,512]{2,1,0:T(8,128)(2,1)} %bitcast_select_fusion) | data formatting | bytes 15728640 | tf_op jit(solution)/shard_map/reshape.64
  297.5 12.8 %copy.71 = bf16[128,60,512]{0,2,1:T(8,128)(2,1)} copy(bf16[128,60,512]{2,1,0:T(8,128)(2,1)} %reshape.600) | data formatting | bytes 15728640 | tf_op jit(solution)/shard_map/reshape.64
  334.2 9.3 %fusion.123 = f32[7680,512]{1,0:T(8,128)} fusion(bf16[7680,128]{1,0:T(8,128)(2,1)} %dot_general.119, bf16[512,128]{1,0:T(8,128)(2,1)} %param.39), kind=kOutput, calls=%fused_computation.199 | convolution fusion | flops 1006632960 | bytes 17825792 | tf_op jit(solution)/shard_map/crkh,dh->crkd/dot_general | solution.py:29
  343.5 47.1 %scatter_custom_fusion = f32[512,512]{1,0:T(8,128)} fusion(s32[7680]{0:T(1024)} %reshape.638, f32[7680,512]{1,0:T(8,128)} %fusion.123, f32[]{:T(128)} %constant.63.clone.1), kind=kCustom, calls=%fused_computation.92 | custom fusion | flops 3932160 | bytes 1049088 | tf_op jit(solution)/shard_map/scatter-add | solution.py:45
  392.7 22.5 %reduce-scatter.21.cloned.1.call-done = bf16[1,128,512]{2,1,0:T(8,128)(2,1)} async-done(((bf16[1,512,512]{2,1,0:T(8,128)(2,1)}), bf16[1,128,512]{2,1,0:T(8,128)(2,1)}) %reduce-scatter.21.cloned.1.call-update) | async-done | bytes 131088 | tf_op jit(solution)/shard_map/reduce_scatter | solution.py:49
  417.1 42.7 %all-reduce.17.cloned.1.call-done = f32[1,128,512]{2,1,0:T(8,128)} async-done(((f32[1,128,512]{2,1,0:T(8,128)}), f32[1,128,512]{2,1,0:T(8,128)}) %all-reduce.17.cloned.1.call-update) | async-done | bytes 262160 | tf_op jit(solution)/shard_map/psum | solution.py:33
  468.4 43.0 %all-reduce.19.cloned.1.call-done = f32[1,128,512]{2,1,0:T(8,128)} async-done(((f32[1,128,512]{2,1,0:T(8,128)}), f32[1,128,512]{2,1,0:T(8,128)}) %all-reduce.19.cloned.1.call-update) | async-done | bytes 262160 | tf_op jit(solution)/shard_map/psum | solution.py:33
  528.6 9.3 %fusion.124 = f32[7680,512]{1,0:T(8,128)} fusion(bf16[7680,128]{1,0:T(8,128)(2,1)} %dot_general.127, bf16[512,128]{1,0:T(8,128)(2,1)} %param.30), kind=kOutput, calls=%fused_computation.200 | convolution fusion | flops 1006632960 | bytes 17825792 | tf_op jit(solution)/shard_map/crkh,dh->crkd/dot_general | solution.py:29
  537.8 47.1 %scatter_custom_fusion.1 = f32[512,512]{1,0:T(8,128)} fusion(s32[7680]{0:T(1024)} %reshape.638, f32[7680,512]{1,0:T(8,128)} %fusion.124, f32[]{:T(128)} %constant.63.clone.1), kind=kCustom, calls=%fused_computation.90 | custom fusion | flops 3932160 | bytes 1049088 | tf_op jit(solution)/shard_map/scatter-add | solution.py:45
  587.1 21.7 %reduce-scatter.23.cloned.1.call-done = bf16[1,128,512]{2,1,0:T(8,128)(2,1)} async-done(((bf16[1,512,512]{2,1,0:T(8,128)(2,1)}), bf16[1,128,512]{2,1,0:T(8,128)(2,1)}) %reduce-scatter.23.cloned.1.call-update) | async-done | bytes 131088 | tf_op jit(solution)/shard_map/reduce_scatter | solution.py:49
  656.5 42.5 %reduce-scatter.29.cloned.1.call-done = bf16[1,128,15,192]{1,3,2,0:T(8,128)(2,1)} async-done(((bf16[1,128,60,192]{1,3,2,0:T(8,128)(2,1)}), bf16[1,128,15,192]{1,3,2,0:T(8,128)(2,1)}) %reduce-scatter.29.cloned.1.call-update) | async-done | bytes 737296
  699.1 45.7 %reduce-scatter.27.cloned.1.call-done = bf16[1,128,15,192]{1,3,2,0:T(8,128)(2,1)} async-done(((bf16[1,128,60,192]{1,3,2,0:T(8,128)(2,1)}), bf16[1,128,15,192]{1,3,2,0:T(8,128)(2,1)}) %reduce-scatter.27.cloned.1.call-update) | async-done | bytes 737296
  756.1 16.1 %all-reduce.3 = (f32[512]{0:T(512)}, f32[192]{0:T(256)}, f32[512]{0:T(512)}, f32[512]{0:T(512)}, f32[192]{0:T(256)}) all-reduce(f32[512]{0:T(512)S(1)} %get-tuple-element.28, f32[192]{0:T(256)S(1)} %get-tuple-element.48, f32[512]{0:T(512)S(1)} %copy-done.60, ...), channel_id=1, replica_groups=mesh['dp'=2,'graph'=4,'mp'=4] {'dp','graph'}, use_global_device_ids=true, to_apply=%region_34.36 | all-reduce | flops 1920 | bytes 15360 | tf_op jit(solution)/shard_map/psum | solution.py:192
  772.2 18.0 %reduce-scatter.25.cloned.1.call-done = bf16[1,128,15,192]{1,3,2,0:T(8,128)(2,1)} async-done(((bf16[1,128,60,192]{1,3,2,0:T(8,128)(2,1)}), bf16[1,128,15,192]{1,3,2,0:T(8,128)(2,1)}) %reduce-scatter.25.cloned.1.call-update) | async-done | bytes 737296
  794.1 92.5 %all-reduce.23.cloned.1.call-done = (f32[512,128]{1,0:T(8,128)}, f32[512,128]{1,0:T(8,128)}, f32[192,128]{1,0:T(8,128)}, f32[128,512]{1,0:T(8,128)}, f32[512,512...) async-done(((f32[512,128]{1,0:T(8,128)}, f32[512,128]{1,0:T(8,128)}, ...) | async-done | bytes 3702800 | tf_op jit(solution)/shard_map/psum | solution.py:192
  (274 shorter events, 175.9 us)
Async XLA Ops:
  7.2 186.4 %copy-start = (bf16[512,512]{1,0:T(8,128)(2,1)S(1)}, bf16[512,512]{1,0:T(8,128)(2,1)}, u32[]{:S(2)}) copy-start(bf16[512,512]{1,0:T(8,128)(2,1)} %param.35) | copy-start | bytes 1572868
  7.2 128.1 %all-gather.3.cloned.1.call-start = ((), (), s32[]{:S(2)}) async-start(), calls=%async_computation.5 | async-start | bytes 3686400 | tf_op jit(solution)/shard_map/all_gather | solution.py:95
  7.9 183.3 %all-reduce.13.cloned.1.call-start = ((), (), s32[]{:S(2)}) async-start(), calls=%async_computation.6 | async-start | bytes 524288 | tf_op jit(solution)/shard_map/psum | solution.py:33
  139.2 177.0 %copy-start.38 = (f32[128,60]{0,1:T(8,128)}, f32[128,60]{0,1:T(8,128)S(1)}, u32[]{:S(2)}) copy-start(f32[128,60]{0,1:T(8,128)S(1)} %add_rsqrt_fusion) | copy-start | bytes 92164
  145.5 132.3 %copy-start.40 = (bf16[128,128]{1,0:T(8,128)(2,1)}, bf16[128,128]{1,0:T(8,128)(2,1)S(1)}, u32[]{:S(2)}) copy-start(bf16[128,128]{1,0:T(8,128)(2,1)S(1)} %get-tuple-element.60) | copy-start | bytes 98308
  146.4 91.6 %all-reduce.15.cloned.1.call-start = ((), (), s32[]{:S(2)}) async-start(), calls=%async_computation.7 | async-start | bytes 524288 | tf_op jit(solution)/shard_map/psum | solution.py:33
  192.4 320.9 %copy-start.51 = (f32[128]{0:T(128)}, f32[128]{0:T(128)S(1)}, u32[]{:S(2)}) copy-start(f32[128]{0:T(128)S(1)} %broadcast_multiply_fusion.11) | copy-start | bytes 1540
  192.6 320.7 %copy-start.55 = (f32[128]{0:T(128)}, f32[128]{0:T(128)S(1)}, u32[]{:S(2)}) copy-start(f32[128]{0:T(128)S(1)} %add_rsqrt_fusion.3) | copy-start | bytes 1540
  194.6 125.2 %all-gather.5.cloned.1.call-start = ((), (), s32[]{:S(2)}) async-start(), calls=%async_computation.8 | async-start | bytes 3686400 | tf_op jit(solution)/shard_map/all_gather | solution.py:96
  195.1 220.1 %reduce-scatter.21.cloned.1.call-start = ((), (), s32[]{:S(2)}) async-start(), calls=%async_computation.9 | async-start | bytes 655360 | tf_op jit(solution)/shard_map/reduce_scatter | solution.py:49
  392.7 67.2 %all-reduce.17.cloned.1.call-start = ((), (), s32[]{:S(2)}) async-start(), calls=%async_computation.10 | async-start | bytes 524288 | tf_op jit(solution)/shard_map/psum | solution.py:33
  417.1 94.4 %all-reduce.19.cloned.1.call-start = ((), (), s32[]{:S(2)}) async-start(), calls=%async_computation.11 | async-start | bytes 524288 | tf_op jit(solution)/shard_map/psum | solution.py:33
  468.4 140.4 %reduce-scatter.23.cloned.1.call-start = ((), (), s32[]{:S(2)}) async-start(), calls=%async_computation.12 | async-start | bytes 655360 | tf_op jit(solution)/shard_map/reduce_scatter | solution.py:49
  587.0 66.5 %all-reduce.21.cloned.1.call-start = ((), (), s32[]{:S(2)}) async-start(), calls=%async_computation.13 | async-start | bytes 524288 | tf_op jit(solution)/shard_map/psum | solution.py:33
  610.7 88.4 %reduce-scatter.29.cloned.1.call-start = ((), (), s32[]{:S(2)}) async-start(), calls=%async_computation.16 | async-start | bytes 3686400
  614.9 129.9 %reduce-scatter.27.cloned.1.call-start = ((), (), s32[]{:S(2)}) async-start(), calls=%async_computation.15 | async-start | bytes 3686400
  619.1 171.2 %reduce-scatter.25.cloned.1.call-start = ((), (), s32[]{:S(2)}) async-start(), calls=%async_computation.14 | async-start | bytes 3686400
  624.8 261.8 %all-reduce.23.cloned.1.call-start = ((), (), s32[]{:S(2)}) async-start(), calls=%async_computation.17 | async-start | bytes 7405568 | tf_op jit(solution)/shard_map/psum | solution.py:192
  648.8 96.0 %copy-start.4 = (bf16[1,128,15,192]{1,3,2,0:T(8,128)(2,1)S(1)}, bf16[1,128,15,192]{1,3,2,0:T(8,128)(2,1)}, u32[]{:S(2)}) copy-start(bf16[1,128,15,192]{1,3,2,0:T(8,128)(2,1)} %param.24) | copy-start | bytes 2211844
  648.8 96.0 %copy-start.54 = (f32[192]{0:T(256)S(1)}, f32[192]{0:T(256)}, u32[]{:S(2)}) copy-start(f32[192]{0:T(256)} %param.37) | copy-start | bytes 2308
  648.8 96.0 %copy-start.67 = (f32[192]{0:T(256)S(1)}, f32[192]{0:T(256)}, u32[]{:S(2)}) copy-start(f32[192]{0:T(256)} %param.28) | copy-start | bytes 2308
  648.8 107.3 %copy-start.59 = (f32[512]{0:T(512)S(1)}, f32[512]{0:T(512)}, u32[]{:S(2)}) copy-start(f32[512]{0:T(512)} %get-tuple-element.24) | copy-start | bytes 6148
  648.8 107.3 %copy-start.60 = (f32[512]{0:T(512)S(1)}, f32[512]{0:T(512)}, u32[]{:S(2)}) copy-start(f32[512]{0:T(512)} %get-tuple-element.26) | copy-start | bytes 6148
  648.8 141.5 %copy-start.18 = (bf16[1,128,15,192]{1,3,2,0:T(8,128)(2,1)S(1)}, bf16[1,128,15,192]{1,3,2,0:T(8,128)(2,1)}, u32[]{:S(2)}) copy-start(bf16[1,128,15,192]{1,3,2,0:T(8,128)(2,1)} %param.43) | copy-start | bytes 2211844
  (62 other events, 1075.3 us)
Sparse Core Ops, SparseCore 0:
  9.9 45.0 all-gather.2
  146.5 44.6 all-reduce.12
  195.0 42.9 all-reduce.14
  239.7 42.3 all-gather.4
  392.8 22.3 reduce-scatter.20
  418.6 41.2 all-reduce.16
  468.5 42.9 all-reduce.18
  587.1 21.6 reduce-scatter.22
  612.3 41.1 all-reduce.20
  656.7 42.2 reduce-scatter.28
  702.4 42.2 reduce-scatter.26
  748.0 42.2 reduce-scatter.24
  795.6 90.9 all-reduce.22
where the time goes:
time: 916 us; the launch traced here: 906 us
  waiting for transfers between devices  422 us (46%)
  local copies, waits for them, and re-layouts  171 us (19%)
  other arithmetic  147 us (16%)
  matrix products  92.6 us (10%)
  blocking collectives  58.2 us (6%)
  between operations  15.2 us (2%)
    psum x5, waiting for transfers between devices, unit_sum(): return lax.psum(partial_sum, 'mp')  177 us
    unnamed x16, waiting for transfers between devices  108 us
    scatter-add x2, other arithmetic, return_rows(): jax.ops.segment_sum(terms.reshape(-1, width), offsets.reshape(-1), num_se...  94.2 us
    dot_general x30, matrix products, mixed(): return jnp.einsum(form, left, right, preferred_element_type=jnp.float32)  92.6 us
    psum x1, waiting for transfers between devices, local(): lax.psum((grad_gain_a, grad_gain_ea, grad_msg_self, grad_msg_other, grad_...  92.5 us
    another operation x4, local copies, waits for them, and re-layouts  47.9 us
    gather x2, local copies, waits for them, and re-layouts, local(): jnp.take_along_axis(resmask, flat_index, axis=1).astype(jnp.float32)  45.3 us
    gather x2, local copies, waits for them, and re-layouts, fetch_rows(): return jnp.take_along_axis(whole, flat_index[:, :, None], axis=1)  44.4 us
  transfers between devices with their start and end apart: 13, of which 11 were waited for; matrix products, arithmetic and copies ran while one was open for 24% of the time, Pallas kernels for 0%

commit v1 on v0

v1 whole, which is shorter than its diff:
```python
import functools

import jax
import jax.numpy as jnp
from jax import lax
from jax.experimental import pallas as pl
from jax.experimental.pallas import tpu as pltpu
from jax.sharding import PartitionSpec as P

EPSILON = 1e-05
F32 = jnp.float32
BF16 = jnp.bfloat16
GELU_A = 0.7978845608028654
GELU_B = 0.044715


def dot(left, right):
    return lax.dot_general(left, right, (((1,), (0,)), ((), ())), preferred_element_type=F32)


def dot_nt(left, right):
    return lax.dot_general(left, right, (((1,), (1,)), ((), ())), preferred_element_type=F32)


def dot_tn(left, right):
    return lax.dot_general(left, right, (((0,), (0,)), ((), ())), preferred_element_type=F32)


def normalize(values):
    centre = values - jnp.mean(values, axis=-1, keepdims=True)
    variance = jnp.mean(centre * centre, axis=-1, keepdims=True)
    scale_inv = lax.rsqrt(variance + EPSILON)
    return centre * scale_inv, scale_inv


def norm_back(grad_hat, normed, scale_inv):
    return scale_inv * (
        grad_hat
        - jnp.mean(grad_hat, axis=-1, keepdims=True)
        - normed * jnp.mean(grad_hat * normed, axis=-1, keepdims=True)
    )


def gelu_both(u):
    square = u * u
    th = jnp.tanh(u * (GELU_A + (GELU_A * GELU_B) * square))
    half = 0.5 + 0.5 * th
    slope = half + (0.5 * u) * (1.0 - th * th) * (GELU_A + (3.0 * GELU_A * GELU_B) * square)
    return u * half, slope


def cat(refs, lo, hi):
    return jnp.concatenate([r[lo:hi, :] for r in refs], axis=1)


def edge_prep(et_ref, idx_ref, mask_ref, ga_ref, gb_ref, f_ref, q_ref, oh_ref, oht_ref, mk_ref):
    slots, rows, width = et_ref.shape
    total = mask_ref.shape[0]
    for s in range(slots):
        hat, _ = normalize(et_ref[s].astype(F32))
        f_ref[s] = (hat * ga_ref[...]).astype(BF16)
        q_ref[s] = (hat * gb_ref[...]).astype(BF16)
        idx = idx_ref[s]
        here = lax.broadcasted_iota(jnp.int32, (total, rows), 0)
        oht_ref[:, s * rows : (s + 1) * rows] = (here == idx).astype(F32).astype(BF16)
        eye = lax.broadcasted_iota(jnp.int32, (rows, rows), 0) == lax.broadcasted_iota(
            jnp.int32, (rows, rows), 1
        )
        high = jnp.where(eye, (idx // 64).astype(F32), 0.0).astype(BF16)
        low = jnp.where(eye, (idx % 64).astype(F32), 0.0).astype(BF16)
        ones = jnp.ones((rows, 128), BF16)
        column = (dot(high, ones) * 64.0 + dot(low, ones)).astype(jnp.int32)
        lane = lax.broadcasted_iota(jnp.int32, (rows, 128), 1)
        parts = [
            ((lane + base) == column).astype(F32).astype(BF16) for base in range(0, total, 128)
        ]
        onehot = jnp.concatenate(parts, axis=1)
        oh_ref[s] = onehot
        mk_ref[s] = dot(onehot, mask_ref[...]).astype(BF16)


def message_forward(
    nbr_scale, total_steps, f_ref, oh_ref, mk_ref, nodes_ref, gain_ref, w0, w1, w2, w3, slope_ref, pooled_ref, a_ref, p_ref, ps_ref, acc_ref
):
    step = pl.program_id(0)
    slots, rows, _ = f_ref.shape
    width = nodes_ref.shape[1]
    ws = (w0, w1, w2, w3)

    @pl.when(step == 0)
    def _():
        hat, _ = normalize(nodes_ref[...].astype(F32))
        a = (hat * gain_ref[...]).astype(BF16)
        p_ref[...] = dot(a, cat(ws, width, 2 * width)).astype(BF16)
        own = a[:rows]
        a_ref[...] = own
        ps_ref[...] = dot(own, cat(ws, 0, width))
        acc_ref[...] = jnp.zeros_like(acc_ref)

    we = cat(ws, 2 * width, w0.shape[0])
    for s in range(slots):
        u = dot(oh_ref[s], p_ref[...]) + dot(f_ref[s], we) + ps_ref[...]
        z, slope = gelu_both(u)
        mask = jnp.concatenate([mk_ref[s].astype(F32)] * (u.shape[1] // 128), axis=1)
        acc_ref[...] += z.astype(BF16).astype(F32) * mask
        slope_ref[s] = (slope * mask).astype(BF16)

    @pl.when(step == total_steps - 1)
    def _():
        pooled_ref[...] = (acc_ref[...] * nbr_scale).astype(BF16)


def node_forward(
    s0, s1, s2, s3, nodes_ref, o0, o1, o2, o3, gain_ref, win_ref, wout_ref, s_ref, h1_ref, b_ref, y_ref, slope_ref, part_ref
):
    sums = []
    for p in range(4):
        acc = None
        for k, ref in enumerate((s0, s1, s2, s3)):
            at = (p ^ k) * 128
            term = ref[:, at : at + 128].astype(F32)
            acc = term if acc is None else acc + term
        sums.append(acc.astype(BF16))
    pooled = jnp.concatenate(sums, axis=1)
    s_ref[...] = pooled
    wo = jnp.concatenate([o0[...], o1[...], o2[...], o3[...]], axis=0)
    h1 = nodes_ref[...].astype(F32) + dot(pooled, wo)
    h1_ref[...] = h1
    hat, _ = normalize(h1)
    b = (hat * gain_ref[...]).astype(BF16)
    b_ref[...] = b
    y, slope = gelu_both(dot(b, win_ref[...]))
    y = y.astype(BF16)
    y_ref[...] = y
    slope_ref[...] = slope.astype(BF16)
    part_ref[...] = dot(y, wout_ref[...]).astype(BF16)


def node_close(h1_ref, p0, p1, p2, p3, gain_ref, h2_ref, c_ref, out_ref):
    h2 = h1_ref[...] + (
        (p0[...].astype(F32) + p1[...].astype(F32)) + (p2[...].astype(F32) + p3[...].astype(F32))
    )
    h2_ref[...] = h2
    hat, _ = normalize(h2)
    c_ref[...] = (hat * gain_ref[...]).astype(BF16)
    out_ref[...] = h2.astype(BF16)


def update_kernel(
    total_steps, q_ref, oh_ref, oht_ref, cot_ref, c_ref, w0, w1, w2, w3, o0, o1, o2, o3, w_ref, dv_ref, r_ref, *rest
):
    s_refs, (p_ref, ps_ref, racc_ref, sacc_ref) = rest[:-4], rest[-4:]
    step = pl.program_id(0)
    slots, rows, _ = q_ref.shape
    width = c_ref.shape[1]
    ws = (w0, w1, w2, w3)

    @pl.when(step == 0)
    def _():
        p_ref[...] = dot(c_ref[...], cat(ws, width, 2 * width)).astype(BF16)
        ps_ref[...] = dot(c_ref[:rows, :], cat(ws, 0, width))
        racc_ref[...] = jnp.zeros_like(racc_ref)
        sacc_ref[...] = jnp.zeros_like(sacc_ref)

    we = cat(ws, 2 * width, w0.shape[0])
    wo = jnp.concatenate([o0[...], o1[...], o2[...], o3[...]], axis=0)
    for s in range(slots):
        v = dot(oh_ref[s], p_ref[...]) + dot(q_ref[s], we) + ps_ref[...]
        w, slope = gelu_both(v)
        w_ref[s] = w.astype(BF16)
        dv = (slope * dot_nt(cot_ref[s], wo)).astype(BF16)
        dv_ref[s] = dv
        racc_ref[...] += dv.astype(F32)
    dvs = dv_ref[...].reshape(slots * rows, dv_ref.shape[2])
    sacc_ref[...] += dot(oht_ref[...], dvs)

    @pl.when(step == total_steps - 1)
    def _():
        r_ref[...] = racc_ref[...].astype(BF16)
        for b, ref in enumerate(s_refs):
            n = ref.shape[0]
            ref[...] = sacc_ref[b * n : (b + 1) * n, :].astype(BF16)


def update_edges(
    et_ref, w_ref, dv_ref, q_ref, cot_ref, w0, w1, w2, w3, o0, o1, o2, o3, out_ref, dq_ref, gout_ref, gedge_ref, gacc_ref, eacc_ref
):
    step = pl.program_id(0)
    slots, rows, width_e = et_ref.shape
    we = cat((w0, w1, w2, w3), w0.shape[0] - width_e, w0.shape[0])
    wo = jnp.concatenate([o0[...], o1[...], o2[...], o3[...]], axis=0)

    @pl.when(step == 0)
    def _():
        gacc_ref[...] = jnp.zeros_like(gacc_ref)
        eacc_ref[...] = jnp.zeros_like(eacc_ref)

    for s in range(slots):
        w = w_ref[s]
        dv = dv_ref[s]
        out_ref[s] = (et_ref[s].astype(F32) + dot(w, wo)).astype(BF16)
        dq_ref[s] = dot_nt(dv, we).astype(BF16)
        gacc_ref[...] += dot_tn(cot_ref[s], w)
        eacc_ref[...] += dot_tn(q_ref[s], dv)
    gout_ref[...] = gacc_ref[...].astype(BF16)
    gedge_ref[...] = eacc_ref[...].astype(BF16)


def node_terms(r_ref, s0, s1, s2, s3, w0, w1, w2, w3, sum_ref, part_ref):
    width = w0.shape[0] if False else part_ref.shape[1]
    ws = (w0, w1, w2, w3)
    total = (
        (s0[...].astype(F32) + s1[...].astype(F32)) + (s2[...].astype(F32) + s3[...].astype(F32))
    ).astype(BF16)
    sum_ref[...] = total
    part_ref[...] = (
        dot_nt(r_ref[...], cat(ws, 0, width)) + dot_nt(total, cat(ws, width, 2 * width))
    ).astype(BF16)


def node_terms_one(r_ref, s_ref, w0, w1, w2, w3, part_ref):
    width = part_ref.shape[1]
    ws = (w0, w1, w2, w3)
    part_ref[...] = (
        dot_nt(r_ref[...], cat(ws, 0, width)) + dot_nt(s_ref[...], cat(ws, width, 2 * width))
    ).astype(BF16)


def sum4(refs):
    a, b, c, d = [r[...].astype(F32) for r in refs]
    return (a + b) + (c + d)


def node_backward(
    t0, t1, t2, t3, h2_ref, cot_ref, gain_ref, slope_ref, win_ref, wout_ref, dh2_ref, dr_ref, dp_ref, gain_out, part_ref
):
    dc = sum4((t0, t1, t2, t3))
    hat, inv = normalize(h2_ref[...])
    gain_out[...] = jnp.sum(dc * hat, axis=0, keepdims=True)
    dh2 = cot_ref[...].astype(F32) + norm_back(dc * gain_ref[...], hat, inv)
    dh2_ref[...] = dh2
    dr = dh2.astype(BF16)
    dr_ref[...] = dr
    dp = (slope_ref[...].astype(F32) * dot_nt(dr, wout_ref[...])).astype(BF16)
    dp_ref[...] = dp
    part_ref[...] = dot_nt(dp, win_ref[...]).astype(BF16)


def message_backward(
    nbr_scale, total_steps, t0, t1, t2, t3, h1_ref, dh2_ref, gain_ref, o0, o1, o2, o3, slope_ref, oht_ref,
    dh1_ref, dt_ref, gain_out, du_ref, r_ref, *rest
):
    s_refs, (g_ref, racc_ref, sacc_ref) = rest[:-3], rest[-3:]
    step = pl.program_id(0)
    slots, rows, _ = slope_ref.shape

    @pl.when(step == 0)
    def _():
        db = sum4((t0, t1, t2, t3))
        hat, inv = normalize(h1_ref[...])
        gain_out[...] = jnp.sum(db * hat, axis=0, keepdims=True)
        dh1 = dh2_ref[...] + norm_back(db * gain_ref[...], hat, inv)
        dh1_ref[...] = dh1
        dt = dh1.astype(BF16)
        dt_ref[...] = dt
        wo = jnp.concatenate([o0[...], o1[...], o2[...], o3[...]], axis=0)
        g_ref[...] = dot_nt(dt, wo) * nbr_scale
        racc_ref[...] = jnp.zeros_like(racc_ref)
        sacc_ref[...] = jnp.zeros_like(sacc_ref)

    for s in range(slots):
        du = (slope_ref[s].astype(F32) * g_ref[...]).astype(BF16)
        du_ref[s] = du
        racc_ref[...] += du.astype(F32)
    dus = du_ref[...].reshape(slots * rows, du_ref.shape[2])
    sacc_ref[...] += dot(oht_ref[...], dus)

    @pl.when(step == total_steps - 1)
    def _():
        r_ref[...] = racc_ref[...].astype(BF16)
        for b, ref in enumerate(s_refs):
            n = ref.shape[0]
            ref[...] = sacc_ref[b * n : (b + 1) * n, :].astype(BF16)


def message_edges(
    et_ref, du_ref, dq_ref, f_ref, cot_ref, ga_ref, gb_ref, w0, w1, w2, w3, out_ref, gedge_ref, gains_ref, eacc_ref
):
    step = pl.program_id(0)
    slots, rows, width_e = et_ref.shape
    we = cat((w0, w1, w2, w3), w0.shape[0] - width_e, w0.shape[0])

    @pl.when(step == 0)
    def _():
        eacc_ref[...] = jnp.zeros_like(eacc_ref)
        gains_ref[...] = jnp.zeros_like(gains_ref)

    for s in range(slots):
        du = du_ref[s]
        df = dot_nt(du, we)
        dq = dq_ref[s].astype(F32)
        hat, inv = normalize(et_ref[s].astype(F32))
        gains_ref[0:1, :] += jnp.sum(df * hat, axis=0, keepdims=True)
        gains_ref[1:2, :] += jnp.sum(dq * hat, axis=0, keepdims=True)
        out_ref[s] = cot_ref[s].astype(F32) + norm_back(
            ga_ref[...] * df + gb_ref[...] * dq, hat, inv
        )
        eacc_ref[...] += dot_tn(f_ref[s], du)
    gedge_ref[...] = eacc_ref[...].astype(BF16)


def node_finish(t0, t1, t2, t3, nodes_ref, dh1_ref, gain_ref, gain_out, out_ref):
    da = sum4((t0, t1, t2, t3))
    hat, inv = normalize(nodes_ref[...].astype(F32))
    gain_out[...] = jnp.sum(da * hat, axis=0, keepdims=True)
    out_ref[...] = dh1_ref[...] + norm_back(da * gain_ref[...], hat, inv)


def whole(shape):
    zeros = (0,) * len(shape)
    return pl.BlockSpec(tuple(shape), lambda i: zeros)


def call(body, grid, ins, outs, scratch=(), vmem=48, flops=0, name=None):
    in_specs = [whole(a.shape) if s is None else s for a, s in ins]
    out_specs = [whole(sh) if s is None else s for sh, _, s in outs]
    moved = sum(a.size * a.dtype.itemsize for a, _ in ins)
    moved += sum(jnp.dtype(t).itemsize * int(jnp.prod(jnp.array(sh))) if False else _bytes(sh, t) for sh, t, _ in outs)
    return pl.pallas_call(
        body,
        grid=(grid,),
        in_specs=in_specs,
        out_specs=out_specs,
        out_shape=[jax.ShapeDtypeStruct(sh, t) for sh, t, _ in outs],
        scratch_shapes=list(scratch),
        compiler_params=pltpu.CompilerParams(
            vmem_limit_bytes=vmem << 20, dimension_semantics=("arbitrary",)
        ),
        cost_estimate=pl.CostEstimate(flops=int(flops), bytes_accessed=int(moved), transcendentals=0),
        name=name,
    )(*[a for a, _ in ins])


def _bytes(shape, dtype):
    n = jnp.dtype(dtype).itemsize
    for d in shape:
        n *= d
    return n


def swap(values, axis, bits, size):
    return lax.ppermute(values, axis, [(i, i ^ bits) for i in range(size)])


def partners(values, axis, size):
    return [values] + [swap(values, axis, k, size) for k in range(1, size)]


def local(sizes, *args):
    (
        nodes, edges, neighbours, resmask, node_gain_a, edge_gain_a, message_self, message_other, message_edge,
        message_out, node_gain_b, ffn_in, ffn_out, node_gain_c, edge_gain_b, update_self, update_other, update_edge,
        update_out, node_cot, edge_cot,
    ) = args
    dp, graph, mp = sizes
    at_core, at_graph, at_mp = (lax.axis_index(a) for a in ("dp", "graph", "mp"))
    _, rows, width = nodes.shape
    slots, width_e = edges.shape[2:]
    nbrs = neighbours.shape[2]
    total = resmask.shape[1]
    hidden = message_self.shape[1] * mp
    near = graph <= 4
    vmem = 40 if total <= 1024 else 60
    tile = 3 if slots % 3 == 0 else 1
    steps = slots // tile

    def tiles(*dims):
        return pl.BlockSpec((tile,) + dims, lambda i: (i,) + (0,) * len(dims))

    def gather_rows(values):
        if near:
            return jnp.concatenate(partners(values, "graph", graph), axis=0)
        return lax.all_gather(values, "graph", axis=0, tiled=True)

    def return_rows(blocks):
        if near:
            return [blocks[0]] + [swap(blocks[k], "graph", k, graph) for k in range(1, graph)]
        one = lax.psum_scatter(
            jnp.concatenate(blocks, axis=0), "graph", scatter_dimension=0, tiled=True
        )
        return [one]

    nbr_own = lax.dynamic_slice_in_dim(neighbours[0], at_mp * slots, slots, axis=1).T
    if near:
        nbr_own = ((nbr_own // rows) ^ at_graph) * rows + nbr_own % rows
        mask_row = jnp.concatenate(
            [lax.dynamic_slice_in_dim(resmask[0], (at_graph ^ k) * rows, rows) for k in range(graph)]
        )
    else:
        mask_row = resmask[0]
    mask_lanes = jnp.broadcast_to(mask_row.astype(BF16)[:, None], (total, 128))

    nodes_all = gather_rows(nodes[0])
    wm = partners(jnp.concatenate([message_self, message_other, message_edge], axis=0), "mp", mp)
    wmo = partners(message_out, "mp", mp)
    wu = partners(jnp.concatenate([update_self, update_other, update_edge], axis=0), "mp", mp)
    wuo = partners(update_out, "mp", mp)

    ga_e, gb_e = edge_gain_a[None, :], edge_gain_b[None, :]
    ga_n, gb_n, gc_n = node_gain_a[None, :], node_gain_b[None, :], node_gain_c[None, :]

    et = jnp.swapaxes(edges[0], 0, 1)
    cot = jnp.swapaxes(edge_cot[0], 0, 1)
    slab = (slots, rows)
    edge_spec = tiles(rows, width_e)
    hid_spec = tiles(rows, hidden)
    oht_spec = pl.BlockSpec((total, tile * rows), lambda i: (0, i))

    f, q, oh, oht, mk = call(
        edge_prep, steps,
        [(et, edge_spec), (nbr_own[:, None, :], tiles(1, rows)), (mask_lanes, None), (ga_e, None), (gb_e, None)],
        [
            (slab + (width_e,), BF16, edge_spec), (slab + (width_e,), BF16, edge_spec),
            (slab + (total,), BF16, tiles(rows, total)), ((total, slots * rows), BF16, oht_spec),
            (slab + (128,), BF16, tiles(rows, 128)),
        ],
        vmem=vmem, name="edge_prep",
    )

    slope_m, pooled_part, a_own = call(
        functools.partial(message_forward, 1.0 / nbrs, steps), steps,
        [(f, edge_spec), (oh, tiles(rows, total)), (mk, tiles(rows, 128)), (nodes_all, None), (ga_n, None)]
        + [(w, None) for w in wm],
        [(slab + (hidden,), BF16, hid_spec), ((rows, hidden), BF16, None), ((rows, width), BF16, None)],
        [pltpu.VMEM((total, hidden), BF16), pltpu.VMEM((rows, hidden), F32), pltpu.VMEM((rows, hidden), F32)],
        vmem=vmem, name="message_forward",
    )

    s_parts = partners(pooled_part, "mp", mp)
    ff = ffn_in.shape[1]
    pooled, h1, b, y, slope_f, h2_part = call(
        node_forward, 1,
        [(v, None) for v in s_parts] + [(nodes[0], None)] + [(v, None) for v in wmo]
        + [(gb_n, None), (ffn_in, None), (ffn_out, None)],
        [((rows, hidden), BF16, None), ((rows, width), F32, None), ((rows, width), BF16, None),
         ((rows, ff), BF16, None), ((rows, ff), BF16, None), ((rows, width), BF16, None)],
        vmem=vmem, name="node_forward",
    )
    h2, c_own, nodes_out = call(
        node_close, 1,
        [(h1, None)] + [(v, None) for v in partners(h2_part, "mp", mp)] + [(gc_n, None)],
        [((rows, width), F32, None), ((rows, width), BF16, None), ((rows, width), BF16, None)],
        vmem=vmem, name="node_close",
    )
    c_all = gather_rows(c_own)

    blocks = [((rows, hidden), BF16, None)] * graph
    wu_ins = [(v, None) for v in wu]
    wuo_ins = [(v, None) for v in wuo]
    w_act, dv, r_upd, *s_upd = call(
        functools.partial(update_kernel, steps), steps,
        [(q, edge_spec), (oh, tiles(rows, total)), (oht, oht_spec), (cot, edge_spec), (c_all, None)] + wu_ins + wuo_ins,
        [(slab + (hidden,), BF16, hid_spec), (slab + (hidden,), BF16, hid_spec), ((rows, hidden), BF16, None)] + blocks,
        [pltpu.VMEM((total, hidden), BF16), pltpu.VMEM((rows, hidden), F32), pltpu.VMEM((rows, hidden), F32),
         pltpu.VMEM((total, hidden), F32)],
        vmem=vmem, name="update_forward_backward",
    )
    s_upd_parts = return_rows(s_upd)

    eo, dq, g_out_t, g_edge_u = call(
        update_edges, steps,
        [(et, edge_spec), (w_act, hid_spec), (dv, hid_spec), (q, edge_spec), (cot, edge_spec)] + wu_ins + wuo_ins,
        [(slab + (width_e,), BF16, edge_spec), (slab + (width_e,), BF16, edge_spec),
         ((width_e, hidden), BF16, None), ((width_e, hidden), BF16, None)],
        [pltpu.VMEM((width_e, hidden), F32), pltpu.VMEM((width_e, hidden), F32)],
        vmem=vmem, name="update_edges",
    )
    edges_out = jnp.swapaxes(eo, 0, 1)[None]

    def terms(r, parts, weights, name):
        outs = [((rows, hidden), BF16, None), ((rows, width), BF16, None)]
        if len(parts) == 4:
            return call(
                node_terms, 1, [(r, None)] + [(v, None) for v in parts] + weights, outs, vmem=vmem, name=name
            )
        (part,) = call(
            node_terms_one, 1, [(r, None), (parts[0], None)] + weights, outs[1:], vmem=vmem, name=name
        )
        return parts[0], part

    s_upd_own, dc_part = terms(r_upd, s_upd_parts, wu_ins, "update_node_terms")
    dc_parts = partners(dc_part, "mp", mp)
    dh2, dr, dp_ffn, gain_c, db_part = call(
        node_backward, 1,
        [(v, None) for v in dc_parts]
        + [(h2, None), (node_cot[0], None), (gc_n, None), (slope_f, None), (ffn_in, None), (ffn_out, None)],
        [((rows, width), F32, None), ((rows, width), BF16, None), ((rows, ff), BF16, None), ((1, width), F32, None),
         ((rows, width), BF16, None)],
        vmem=vmem, name="node_backward",
    )
    db_parts = partners(db_part, "mp", mp)
    dh1, dt, gain_b, du, r_msg, *s_msg = call(
        functools.partial(message_backward, 1.0 / nbrs, steps), steps,
        [(v, None) for v in db_parts] + [(h1, None), (dh2, None), (gb_n, None)] + [(v, None) for v in wmo]
        + [(slope_m, hid_spec), (oht, oht_spec)],
        [((rows, width), F32, None), ((rows, width), BF16, None), ((1, width), F32, None),
         (slab + (hidden,), BF16, hid_spec), ((rows, hidden), BF16, None)] + blocks,
        [pltpu.VMEM((rows, hidden), F32), pltpu.VMEM((rows, hidden), F32), pltpu.VMEM((total, hidden), F32)],
        vmem=vmem, name="message_backward",
    )
    s_msg_parts = return_rows(s_msg)
    wm_ins = [(v, None) for v in wm]
    ge, g_edge_m, gains_e = call(
        message_edges, steps,
        [(et, edge_spec), (du, hid_spec), (dq, edge_spec), (f, edge_spec), (cot, edge_spec), (ga_e, None), (gb_e, None)]
        + wm_ins,
        [(slab + (width_e,), F32, edge_spec), ((width_e, hidden), BF16, None), ((2, width_e), F32, None)],
        [pltpu.VMEM((width_e, hidden), F32)],
        vmem=vmem, name="message_edges",
    )
    grad_edges = jnp.swapaxes(ge, 0, 1)[None]
    s_msg_own, da_part = terms(r_msg, s_msg_parts, wm_ins, "message_node_terms")
    da_parts = partners(da_part, "mp", mp)
    gain_a, grad_nodes = call(
        node_finish, 1,
        [(v, None) for v in da_parts] + [(nodes[0], None), (dh1, None), (ga_n, None)],
        [((1, width), F32, None), ((rows, width), F32, None)],
        vmem=vmem, name="node_finish",
    )

    shard = hidden // mp

    def own_units(partial):
        pieces = [partial[:, k * shard : (k + 1) * shard] for k in range(mp)]
        got = [swap(pieces[k], "mp", k, mp) for k in range(1, mp)]
        return sum((v.astype(F32) for v in got), pieces[0].astype(F32)).astype(BF16)

    def product(left, right):
        return lax.dot_general(left, right, (((0,), (0,)), ((), ())), preferred_element_type=F32).astype(BF16)

    def reduce_all(values):
        half = values.shape[0] // dp
        keep = lax.dynamic_slice_in_dim(values, at_core * half, half)
        send = lax.dynamic_slice_in_dim(values, (1 - at_core) * half, half)
        part = keep.astype(F32) + swap(send, "dp", 1, dp).astype(F32)
        if near:
            part = part.astype(BF16)
            got = lax.ppermute(part, "graph", [(0, 1), (3, 2)])
            part = (part.astype(F32) + got.astype(F32)).astype(BF16)
            got = lax.ppermute(part, "graph", [(1, 2), (2, 1)])
            part = (part.astype(F32) + got.astype(F32)).astype(BF16)
            got = lax.ppermute(part, "graph", [(1, 0), (2, 3)])
            done = jnp.where((at_graph == 1) | (at_graph == 2), part, got)
        else:
            done = lax.psum(part, "graph").astype(BF16)
        other = swap(done, "dp", 1, dp)
        first = jnp.where(at_core == 0, done, other)
        second = jnp.where(at_core == 0, other, done)
        return jnp.concatenate([first, second], axis=0).astype(F32)

    upd = reduce_all(
        jnp.concatenate(
            [product(c_own, own_units(r_upd)), product(c_own, own_units(s_upd_own)), own_units(g_edge_u), own_units(g_out_t)],
            axis=0,
        )
    )
    ffn = reduce_all(jnp.concatenate([product(b, dp_ffn), product(y, dr)], axis=0))
    msg = reduce_all(
        jnp.concatenate(
            [product(a_own, own_units(r_msg)), product(a_own, own_units(s_msg_own)), own_units(g_edge_m),
             product(dt, pooled[:, :shard])],
            axis=0,
        )
    )

    gains_e = sum(partners(gains_e, "mp", mp))
    gains = jnp.concatenate([gain_a, gain_b, gain_c, jnp.pad(gains_e, ((0, 0), (0, width - width_e)))], axis=0)
    gains = gains + swap(gains, "dp", 1, dp)
    if near:
        gains = sum(partners(gains, "graph", graph))
    else:
        gains = lax.psum(gains, "graph")

    e0, e1 = 2 * width, 2 * width + width_e
    return (
        nodes_out[None],
        edges_out,
        grad_nodes[None],
        grad_edges,
        gains[0],
        gains[3, :width_e],
        msg[:width],
        msg[width:e0],
        msg[e0:e1],
        msg[e1:].T,
        gains[1],
        ffn[:width],
        ffn[width:],
        gains[2],
        gains[4, :width_e],
        upd[:width],
        upd[width:e0],
        upd[e0:e1],
        upd[e1:].T,
    )


def solution(mesh):
    sizes = (mesh.shape["dp"], mesh.shape["graph"], mesh.shape["mp"])
    rows = P("dp", "graph", None)
    slots = P("dp", "graph", "mp", None)
    cols, tops = P(None, "mp"), P("mp", None)
    return jax.shard_map(
        functools.partial(local, sizes),
        mesh=mesh,
        in_specs=(
            rows, slots, rows, P("dp", None), P(), P(), cols, cols, cols, tops, P(), cols, tops, P(), P(), cols, cols,
            cols, tops, rows, slots,
        ),
        out_specs=(
            rows, slots, rows, slots, P(), P(), cols, cols, cols, tops, P(), cols, tops, P(), P(), cols, cols, cols,
            tops,
        ),
        check_vma=False,
    )
```

time: 916 us -> 271 us (0.30)
  waiting for transfers between devices: 422 us -> 82.3 us
  local copies, waits for them, and re-layouts: 171 us -> 34 us
  other arithmetic: 147 us -> 13.3 us
  starting transfers between devices: 0.78 us -> 97.7 us
  matrix products: 92.6 us -> 3.28 us
  blocking collectives: 58.2 us -> 0 us
  Pallas kernels: 0 us -> 37.2 us
  between operations: 15.2 us -> 2.33 us
    psum x6 -> x0, waiting for transfers between devices: 270 us -> none  [the longest x5 177 us: unit_sum(): return lax.psum(partial_sum, 'mp')]
    unnamed x16 -> x0, waiting for transfers between devices: 108 us -> none
    ppermute x0 -> x82, starting transfers between devices: none -> 97.7 us  [the longest x73 83.2 us: swap(): return lax.ppermute(values, axis, [(i, i ^ bits) for i in range(size)])]
    scatter-add x2 -> x0, other arithmetic: 94.2 us -> none  [return_rows(): jax.ops.segment_sum(terms.reshape(-1, width), offsets.reshape(-1), num_se...]
    gather x4 -> x0, local copies, waits for them, and re-layouts: 89.7 us -> none  [the longest x2 45.3 us: local(): jnp.take_along_axis(resmask, flat_index, axis=1).astype(jnp.float32)]
    dot_general x30 -> x7, matrix products: 92.6 us -> 3.28 us  [product(): lax.dot_general(left, right, (((0,), (0,)), ((), ())), preferred_element_...]
    ppermute x0 -> x82, waiting for transfers between devices: none -> 82.3 us  [the longest x73 49.8 us: swap(): return lax.ppermute(values, axis, [(i, i ^ bits) for i in range(size)])]
    another operation x5 -> x0, local copies, waits for them, and re-layouts: 48 us -> none
  transfers between devices with their start and end apart: 13 -> 82, of which waited for: 11 -> 31; matrix products, arithmetic and copies ran while one was open for 24% -> 12% of each run, Pallas kernels for 0% -> 10%
where the time goes in v1:
time: 271 us; the launch traced here: 270 us
  starting transfers between devices  97.7 us (36%)
  waiting for transfers between devices  82.3 us (30%)
  Pallas kernels  37.2 us (14%)
  local copies, waits for them, and re-layouts  34 us (13%)
  other arithmetic  13.3 us (5%)
  matrix products  3.28 us (1%)
    ppermute x73, starting transfers between devices, swap(): return lax.ppermute(values, axis, [(i, i ^ bits) for i in range(size)])  83.2 us
    ppermute x73, waiting for transfers between devices, swap(): return lax.ppermute(values, axis, [(i, i ^ bits) for i in range(size)])  49.8 us
    pallas_call x12, Pallas kernels, call(): pl.pallas_call(body, grid=(grid,), in_specs=in_specs, out_specs=out_specs...  37.2 us
    unnamed x206, local copies, waits for them, and re-layouts  26.6 us
    ppermute x3, waiting for transfers between devices, reduce_all(): got = lax.ppermute(part, 'graph', [(1, 0), (2, 3)])  22 us
    ppermute x3, waiting for transfers between devices, reduce_all(): got = lax.ppermute(part, 'graph', [(0, 1), (3, 2)])  10.5 us
    ppermute x3, starting transfers between devices, reduce_all(): got = lax.ppermute(part, 'graph', [(0, 1), (3, 2)])  8.58 us
  transfers between devices with their start and end apart: 82, of which 31 were waited for; matrix products, arithmetic and copies ran while one was open for 12% of the time, Pallas kernels for 10%

profile of v1, /device:TPU:0, one launch (start us, length us, event | category | flops | bytes accessed | tf_op | source)
XLA Modules:
  0.0 270.1 jit_solution(16526925296688395821)
XLA Ops:
  0.7 3.1 %collective-permute-start = (bf16[128,512]{1,0:T(8,128)(2,1)}, bf16[128,512]{1,0:T(8,128)(2,1)}, u32[]{:S(2)}, u32[]{:S(2)}) collective-permute-start(bf16[128,512]{1,0:T(8,128)(2,1)} %bitcast.76), channel_id=1, source_target_pairs={{0,4},{4,0},{8,12},{12,8},{1,5},{5,1},{9,13},{13,9},{2,6},{6,2},{1... | collective-permute-start | bytes 393224 | tf_op jit(solution)/shard_map/ppermute | solution.py:352
  3.8 2.6 collective-permute-start.1
  13.4 3.5 %collective-permute-done.1 = bf16[128,512]{1,0:T(8,128)(2,1)S(1)} collective-permute-done((bf16[128,512]{1,0:T(8,128)(2,1)}, bf16[128,512]{1,0:T(8,128)(2,1)S(1)}, u32[]{:S(2)}, u32[]{:S(2)}) %collective-permute-start.1) | collective-permute-done | bytes 131104 | tf_op jit(solution)/shard_map/ppermute | solution.py:352
  20.5 4.0 %edge_prep.1 = (bf16[15,128,192]{2,1,0:T(8,128)(2,1)S(1)}, bf16[15,128,192]{2,1,0:T(8,128)(2,1)S(1)}, bf16[15,128,512]{2,1,0:T(8,128)(2,1)S(1)}, bf16[512,1920]{1,0:T(8,128)(2,1)S(1)}, bf16[15,128,128]{2,1,0:T(8,128)(2,1)S(1)}) custom-call(bf16[15,128,192]{2,1,0:T(8,128)(2,1)S(1)} %bitcast.69, s32[15,1,128]{2,1,0:T(1,128)S(1)} %broadcast_in_dim.36.idx_ref, ...), custom_call_target="tpu_custom_call" | custom-call | bytes 6775808 | tf_op jit(solution)/shard_map/edge_prep/pallas_call | solution.py:329
  29.6 5.0 %message_forward.1 = (bf16[15,128,512]{2,1,0:T(8,128)(2,1)S(1)}, bf16[128,512]{1,0:T(8,128)(2,1)S(1)}, bf16[128,512]{1,0:T(8,128)(2,1)S(1)}) custom-call(bf16[15,128,192]{2,1,0:T(8,128)(2,1)S(1)} %get-tuple-element.70.f_ref, bf16[15,128,512]{2,1,0:T(8,128)(2,1)S(1)} %get-tuple-element.71.oh_ref, bf16[15,128,128]{2,1,0:T(8,128)(2,1)S(1)} %get-tuple-element.72.mk_ref, ...), custom_call_target="tpu_custom_call" | custom-call | bytes 7194624 | tf_op jit(solution)/shard_map/message_forward/pallas_call | solution.py:329
  40.9 3.7 %collective-permute-done.8.s3 = bf16[128,512]{1,0:T(8,128)(2,1)S(1)} collective-permute-done((bf16[128,512]{1,0:T(8,128)(2,1)S(1)}, bf16[128,512]{1,0:T(8,128)(2,1)S(1)}, u32[]{:S(2)}, u32[]{:S(2)}) %collective-permute-start.8) | collective-permute-done | bytes 131104 | tf_op jit(solution)/shard_map/ppermute | solution.py:352
  50.1 2.8 %collective-permute-done.12.p1 = bf16[128,512]{1,0:T(8,128)(2,1)S(1)} collective-permute-done((bf16[128,512]{1,0:T(8,128)(2,1)S(1)}, bf16[128,512]{1,0:T(8,128)(2,1)S(1)}, u32[]{:S(2)}, u32[]{:S(2)}) %collective-permute-start.12) | collective-permute-done | bytes 131104 | tf_op jit(solution)/shard_map/ppermute | solution.py:352
  61.8 6.4 %collective-permute-done.21.o1 = bf16[128,192]{1,0:T(8,128)(2,1)S(1)} collective-permute-done((bf16[128,192]{1,0:T(8,128)(2,1)S(1)}, bf16[128,192]{1,0:T(8,128)(2,1)S(1)}, u32[]{:S(2)}, u32[]{:S(2)}) %collective-permute-start.21) | collective-permute-done | bytes 49184 | tf_op jit(solution)/shard_map/ppermute | solution.py:352
  68.9 2.5 collective-permute-start.16
  80.5 3.2 %collective-permute-done.23.o3 = bf16[128,192]{1,0:T(8,128)(2,1)S(1)} collective-permute-done((bf16[128,192]{1,0:T(8,128)(2,1)}, bf16[128,192]{1,0:T(8,128)(2,1)S(1)}, u32[]{:S(2)}, u32[]{:S(2)}) %collective-permute-start.23) | collective-permute-done | bytes 49184 | tf_op jit(solution)/shard_map/ppermute | solution.py:352
  89.7 8.8 %update_forward_backward.1 = (bf16[15,128,512]{2,1,0:T(8,128)(2,1)S(1)}, bf16[15,128,512]{2,1,0:T(8,128)(2,1)S(1)}, bf16[128,512]{1,0:T(8,128)(2,1)S(1)}, bf16[1...) custom-call(bf16[15,128,192]{2,1,0:T(8,128)(2,1)S(1)} %copy-done.7, ...), custom_call_target="tpu_custom_call" | custom-call | bytes 11960320 | tf_op jit(solution)/shard_map/update_forward_backward/pallas_call | solution.py:329
  104.1 2.7 collective-permute-start.25
  106.8 5.0 %update_edges.1 = (bf16[15,128,192]{2,1,0:T(8,128)(2,1)S(1)}, bf16[15,128,192]{2,1,0:T(8,128)(2,1)S(1)}, bf16[192,512]{1,0:T(8,128)(2,1)S(1)}, bf16[192,512]{1,0:T(8,128)(2,1)S(1)}) custom-call(bf16[15,128,192]{2,1,0:T(8,128)(2,1)S(1)} %bitcast.70, bf16[15,128,512]{2,1,0:T(8,128)(2,1)S(1)} %get-tuple-element.80.w_ref, ...), custom_call_target="tpu_custom_call" | custom-call | bytes 9453568 | tf_op jit(solution)/shard_map/update_edges/pallas_call | solution.py:329
  125.8 2.8 %collective-permute-start.76 = (bf16[192,128]{1,0:T(8,128)(2,1)}, bf16[192,128]{1,0:T(8,128)(2,1)S(1)}, u32[]{:S(2)}, u32[]{:S(2)}) collective-permute-start(bf16[192,128]{1,0:T(8,128)(2,1)} %get-tuple-element.158), channel_id=1, source_target_pairs={{0,3},{1,2},{2,1},{3,0},{4,7},{5,6},{6,5},{7,4},{8,11},{9,10},{10,... | collective-permute-start | bytes 147464 | tf_op jit(solution)/shard_map/ppermute | solution.py:352
  142.2 2.4 collective-permute-done.29.t3
  152.6 2.7 collective-permute-start.78
  155.5 4.4 %message_backward.1 = (f32[128,512]{1,0:T(8,128)S(1)}, bf16[128,512]{1,0:T(8,128)(2,1)S(1)}, f32[1,512]{1,0:T(1,128)S(1)}, bf16[15,128,512]{2,1,0:T(8,128)(2,1)S...) custom-call(bf16[128,512]{1,0:T(8,128)(2,1)S(1)} %get-tuple-element., ...), custom_call_target="tpu_custom_call" | custom-call | bytes 8523776 | tf_op jit(solution)/shard_map/message_backward/pallas_call | solution.py:329
  160.6 3.3 %message_edges.1 = (f32[15,128,192]{2,1,0:T(8,128)S(1)}, bf16[192,512]{1,0:T(8,128)(2,1)S(1)}, f32[2,192]{1,0:T(2,128)S(1)}) custom-call(bf16[15,128,192]{2,1,0:T(8,128)(2,1)S(1)} %bitcast.71, bf16[15,128,512]{2,1,0:T(8,128)(2,1)S(1)} %get-tuple-element.102.du_ref, bf16[15,128,192]{2,1,0:T(8,128)(2,1)S(1)} %copy-done.30, ...), custom_call_target="tpu_custom_call" | custom-call | bytes 7834624 | tf_op jit(solution)/shard_map/message_edges/pallas_call | solution.py:329
  170.0 2.9 %copy.48 = f32[1,128,15,192]{1,3,2,0:T(8,128)} copy(f32[1,128,15,192]{3,1,2,0:T(8,128)} %bitcast.75) | data formatting | bytes 2949120
  188.9 4.6 %collective-permute-done.34.s2 = bf16[128,512]{1,0:T(8,128)(2,1)S(1)} collective-permute-done((bf16[128,512]{1,0:T(8,128)(2,1)S(1)}, bf16[128,512]{1,0:T(8,128)(2,1)S(1)}, u32[]{:S(2)}, u32[]{:S(2)}) %collective-permute-start.34) | collective-permute-done | bytes 131104 | tf_op jit(solution)/shard_map/ppermute | solution.py:352
  219.1 4.6 %collective-permute-start.56 = (bf16[864,128]{1,0:T(8,128)(2,1)S(1)}, bf16[864,128]{1,0:T(8,128)(2,1)S(1)}, u32[]{:S(2)}, u32[]{:S(2)}) collective-permute-start(bf16[864,128]{1,0:T(8,128)(2,1)S(1)} %add_convert_fusion.5), channel_id=1, source_target_pairs={{0,4},{12,8},{1,5},{13,9},{2,6},{14,10},{3,7},{15,11},{16,20},{28,... | collective-permute-start | bytes 663560 | tf_op jit(solution)/shard_map/ppermute | solution.py:548
  229.9 8.4 %collective-permute-done.61 = bf16[512,512]{1,0:T(8,128)(2,1)S(1)} collective-permute-done((bf16[512,512]{1,0:T(8,128)(2,1)S(1)}, bf16[512,512]{1,0:T(8,128)(2,1)S(1)}, u32[]{:S(2)}, u32[]{:S(2)}) %collective-permute-start.61) | collective-permute-done | bytes 524320 | tf_op jit(solution)/shard_map/ppermute | solution.py:548
  240.6 8.7 %collective-permute-done.58 = bf16[864,128]{1,0:T(8,128)(2,1)S(1)} collective-permute-done((bf16[864,128]{1,0:T(8,128)(2,1)S(1)}, bf16[864,128]{1,0:T(8,128)(2,1)S(1)}, u32[]{:S(2)}, u32[]{:S(2)}) %collective-permute-start.58) | collective-permute-done | bytes 221216 | tf_op jit(solution)/shard_map/ppermute | solution.py:552
  252.4 13.3 %collective-permute-done.63 = bf16[512,512]{1,0:T(8,128)(2,1)S(1)} collective-permute-done((bf16[512,512]{1,0:T(8,128)(2,1)S(1)}, bf16[512,512]{1,0:T(8,128)(2,1)S(1)}, u32[]{:S(2)}, u32[]{:S(2)}) %collective-permute-start.63) | collective-permute-done | bytes 524320 | tf_op jit(solution)/shard_map/ppermute | solution.py:552
  (420 shorter events, 156.3 us)
Async XLA Ops:
  0.7 11.7 %collective-permute-start = (bf16[128,512]{1,0:T(8,128)(2,1)}, bf16[128,512]{1,0:T(8,128)(2,1)}, u32[]{:S(2)}, u32[]{:S(2)}) collective-permute-start(bf16[128,512]{1,0:T(8,128)(2,1)} %bitcast.76), channel_id=1, source_target_pairs={{0,4},{4,0},{8,12},{12,8},{1,5},{5,1},{9,13},{13,9},{2,6},{6,2},{1... | collective-permute-start | bytes 393224 | tf_op jit(solution)/shard_map/ppermute | solution.py:352
  3.8 13.2 %collective-permute-start.1 = (bf16[128,512]{1,0:T(8,128)(2,1)}, bf16[128,512]{1,0:T(8,128)(2,1)S(1)}, u32[]{:S(2)}, u32[]{:S(2)}) collective-permute-start(bf16[128,512]{1,0:T(8,128)(2,1)} %bitcast.77), channel_id=1, source_target_pairs={{0,8},{4,12},{8,0},{12,4},{1,9},{5,13},{9,1},{13,5},{2,10},{6,14},... | collective-permute-start | bytes 393224 | tf_op jit(solution)/shard_map/ppermute | solution.py:352
  6.4 19.4 %collective-permute-start.2 = (bf16[128,512]{1,0:T(8,128)(2,1)}, bf16[128,512]{1,0:T(8,128)(2,1)}, u32[]{:S(2)}, u32[]{:S(2)}) collective-permute-start(bf16[128,512]{1,0:T(8,128)(2,1)} %bitcast.78), channel_id=1, source_target_pairs={{0,12},{4,8},{8,4},{12,0},{1,13},{5,9},{9,5},{13,1},{2,14},{6,10},... | collective-permute-start | bytes 393224 | tf_op jit(solution)/shard_map/ppermute | solution.py:352
  9.1 19.5 %collective-permute-start.3 = (bf16[1216,128]{1,0:T(8,128)(2,1)S(1)}, bf16[1216,128]{1,0:T(8,128)(2,1)S(1)}, u32[]{:S(2)}, u32[]{:S(2)}) collective-permute-start(bf16[1216,128]{1,0:T(8,128)(2,1)S(1)} %constant_dynamic-update-slice_fusion.w0), channel_id=1, source_target_pairs={{0,1},{1,0},{2,3},{3,2},{4,5},{5,4},{6,7},{7,6},{8,9},{9,8},{10,11... | collective-permute-start | bytes 933896 | tf_op jit(solution)/shard_map/ppermute | solution.py:352
  10.8 18.7 %collective-permute-start.4 = (bf16[1216,128]{1,0:T(8,128)(2,1)S(1)}, bf16[1216,128]{1,0:T(8,128)(2,1)S(1)}, u32[]{:S(2)}, u32[]{:S(2)}) collective-permute-start(bf16[1216,128]{1,0:T(8,128)(2,1)S(1)} %constant_dynamic-update-slice_fusion.w0), channel_id=1, source_target_pairs={{0,2},{1,3},{2,0},{3,1},{4,6},{5,7},{6,4},{7,5},{8,10},{9,11},{10,... | collective-permute-start | bytes 933896 | tf_op jit(solution)/shard_map/ppermute | solution.py:352
  12.4 17.1 %collective-permute-start.5 = (bf16[1216,128]{1,0:T(8,128)(2,1)S(1)}, bf16[1216,128]{1,0:T(8,128)(2,1)S(1)}, u32[]{:S(2)}, u32[]{:S(2)}) collective-permute-start(bf16[1216,128]{1,0:T(8,128)(2,1)S(1)} %constant_dynamic-update-slice_fusion.w0), channel_id=1, source_target_pairs={{0,3},{1,2},{2,1},{3,0},{4,7},{5,6},{6,5},{7,4},{8,11},{9,10},{10,... | collective-permute-start | bytes 933896 | tf_op jit(solution)/shard_map/ppermute | solution.py:352
  17.0 20.4 %collective-permute-start.10 = (bf16[128,512]{1,0:T(8,128)(2,1)}, bf16[128,512]{1,0:T(8,128)(2,1)}, u32[]{:S(2)}, u32[]{:S(2)}) collective-permute-start(bf16[128,512]{1,0:T(8,128)(2,1)} %o0.5), channel_id=1, source_target_pairs={{0,2},{1,3},{2,0},{3,1},{4,6},{5,7},{6,4},{7,5},{8,10},{9,11},{10,... | collective-permute-start | bytes 393224 | tf_op jit(solution)/shard_map/ppermute | solution.py:352
  25.8 12.5 %collective-permute-start.11 = (bf16[128,512]{1,0:T(8,128)(2,1)S(1)}, bf16[128,512]{1,0:T(8,128)(2,1)S(1)}, u32[]{:S(2)}, u32[]{:S(2)}) collective-permute-start(bf16[128,512]{1,0:T(8,128)(2,1)S(1)} %copy-done.34), channel_id=1, source_target_pairs={{0,3},{1,2},{2,1},{3,0},{4,7},{5,6},{6,5},{7,4},{8,11},{9,10},{10,... | collective-permute-start | bytes 393224 | tf_op jit(solution)/shard_map/ppermute | solution.py:352
  57.2 14.2 %collective-permute-start.15 = (bf16[128,512]{1,0:T(8,128)(2,1)S(1)}, bf16[128,512]{1,0:T(8,128)(2,1)S(1)}, u32[]{:S(2)}, u32[]{:S(2)}) collective-permute-start(bf16[128,512]{1,0:T(8,128)(2,1)S(1)} %get-tuple-element.79), channel_id=1, source_target_pairs={{0,4},{4,0},{8,12},{12,8},{1,5},{5,1},{9,13},{13,9},{2,6},{6,2},{1... | collective-permute-start | bytes 393224 | tf_op jit(solution)/shard_map/ppermute | solution.py:352
  57.2 26.5 %collective-permute-start.18 = (bf16[1216,128]{1,0:T(8,128)(2,1)S(1)}, bf16[1216,128]{1,0:T(8,128)(2,1)}, u32[]{:S(2)}, u32[]{:S(2)}) collective-permute-start(bf16[1216,128]{1,0:T(8,128)(2,1)S(1)} %constant_dynamic-update-slice_fusion.3.w0), channel_id=1, source_target_pairs={{0,1},{1,0},{2,3},{3,2},{4,5},{5,4},{6,7},{7,6},{8,9},{9,8},{10,11... | collective-permute-start | bytes 933896 | tf_op jit(solution)/shard_map/ppermute | solution.py:352
  58.0 25.7 %collective-permute-start.19 = (bf16[1216,128]{1,0:T(8,128)(2,1)S(1)}, bf16[1216,128]{1,0:T(8,128)(2,1)}, u32[]{:S(2)}, u32[]{:S(2)}) collective-permute-start(bf16[1216,128]{1,0:T(8,128)(2,1)S(1)} %constant_dynamic-update-slice_fusion.3.w0), channel_id=1, source_target_pairs={{0,2},{1,3},{2,0},{3,1},{4,6},{5,7},{6,4},{7,5},{8,10},{9,11},{10,... | collective-permute-start | bytes 933896 | tf_op jit(solution)/shard_map/ppermute | solution.py:352
  59.5 24.2 %collective-permute-start.20 = (bf16[1216,128]{1,0:T(8,128)(2,1)S(1)}, bf16[1216,128]{1,0:T(8,128)(2,1)}, u32[]{:S(2)}, u32[]{:S(2)}) collective-permute-start(bf16[1216,128]{1,0:T(8,128)(2,1)S(1)} %constant_dynamic-update-slice_fusion.3.w0), channel_id=1, source_target_pairs={{0,3},{1,2},{2,1},{3,0},{4,7},{5,6},{6,5},{7,4},{8,11},{9,10},{10,... | collective-permute-start | bytes 933896 | tf_op jit(solution)/shard_map/ppermute | solution.py:352
  99.2 18.2 %collective-permute-start.65 = (bf16[128,128]{1,0:T(8,128)(2,1)}, bf16[128,128]{1,0:T(8,128)(2,1)}, u32[]{:S(2)}, u32[]{:S(2)}) collective-permute-start(bf16[128,128]{1,0:T(8,128)(2,1)} %get-tuple-element.163), channel_id=1, source_target_pairs={{0,1},{1,0},{2,3},{3,2},{4,5},{5,4},{6,7},{7,6},{8,9},{9,8},{10,11... | collective-permute-start | bytes 98312 | tf_op jit(solution)/shard_map/ppermute | solution.py:352
  99.6 17.8 %collective-permute-start.66 = (bf16[128,128]{1,0:T(8,128)(2,1)}, bf16[128,128]{1,0:T(8,128)(2,1)}, u32[]{:S(2)}, u32[]{:S(2)}) collective-permute-start(bf16[128,128]{1,0:T(8,128)(2,1)} %get-tuple-element.165), channel_id=1, source_target_pairs={{0,2},{1,3},{2,0},{3,1},{4,6},{5,7},{6,4},{7,5},{8,10},{9,11},{10,... | collective-permute-start | bytes 98312 | tf_op jit(solution)/shard_map/ppermute | solution.py:352
  100.8 18.3 %collective-permute-start.67 = (bf16[128,128]{1,0:T(8,128)(2,1)}, bf16[128,128]{1,0:T(8,128)(2,1)}, u32[]{:S(2)}, u32[]{:S(2)}) collective-permute-start(bf16[128,128]{1,0:T(8,128)(2,1)} %get-tuple-element.164), channel_id=1, source_target_pairs={{0,3},{1,2},{2,1},{3,0},{4,7},{5,6},{6,5},{7,4},{8,11},{9,10},{10,... | collective-permute-start | bytes 98312 | tf_op jit(solution)/shard_map/ppermute | solution.py:352
  102.7 23.1 %collective-permute-start.24 = (bf16[128,512]{1,0:T(8,128)(2,1)}, bf16[128,512]{1,0:T(8,128)(2,1)}, u32[]{:S(2)}, u32[]{:S(2)}) collective-permute-start(bf16[128,512]{1,0:T(8,128)(2,1)} %get-tuple-element.85), channel_id=1, source_target_pairs={{0,4},{4,0},{8,12},{12,8},{1,5},{5,1},{9,13},{13,9},{2,6},{6,2},{1... | collective-permute-start | bytes 393224 | tf_op jit(solution)/shard_map/ppermute | solution.py:352
  104.1 24.5 %collective-permute-start.25 = (bf16[128,512]{1,0:T(8,128)(2,1)}, bf16[128,512]{1,0:T(8,128)(2,1)}, u32[]{:S(2)}, u32[]{:S(2)}) collective-permute-start(bf16[128,512]{1,0:T(8,128)(2,1)} %get-tuple-element.86), channel_id=1, source_target_pairs={{0,8},{4,12},{8,0},{12,4},{1,9},{5,13},{9,1},{13,5},{2,10},{6,14},... | collective-permute-start | bytes 393224 | tf_op jit(solution)/shard_map/ppermute | solution.py:352
  122.4 11.9 %collective-permute-start.74 = (bf16[192,128]{1,0:T(8,128)(2,1)}, bf16[192,128]{1,0:T(8,128)(2,1)S(1)}, u32[]{:S(2)}, u32[]{:S(2)}) collective-permute-start(bf16[192,128]{1,0:T(8,128)(2,1)} %get-tuple-element.157), channel_id=1, source_target_pairs={{0,1},{1,0},{2,3},{3,2},{4,5},{5,4},{6,7},{7,6},{8,9},{9,8},{10,11... | collective-permute-start | bytes 147464 | tf_op jit(solution)/shard_map/ppermute | solution.py:352
  124.7 11.5 %collective-permute-start.75 = (bf16[192,128]{1,0:T(8,128)(2,1)}, bf16[192,128]{1,0:T(8,128)(2,1)S(1)}, u32[]{:S(2)}, u32[]{:S(2)}) collective-permute-start(bf16[192,128]{1,0:T(8,128)(2,1)} %get-tuple-element.159), channel_id=1, source_target_pairs={{0,2},{1,3},{2,0},{3,1},{4,6},{5,7},{6,4},{7,5},{8,10},{9,11},{10,... | collective-permute-start | bytes 147464 | tf_op jit(solution)/shard_map/ppermute | solution.py:352
  151.9 71.8 %collective-permute-start.60 = (bf16[512,512]{1,0:T(8,128)(2,1)}, bf16[512,512]{1,0:T(8,128)(2,1)}, u32[]{:S(2)}, u32[]{:S(2)}) collective-permute-start(bf16[512,512]{1,0:T(8,128)(2,1)} %fusion), channel_id=1, source_target_pairs={{0,16},{16,0},{1,17},{17,1},{2,18},{18,2},{3,19},{19,3},{4,20},{20... | collective-permute-start | bytes 1572872 | tf_op jit(solution)/shard_map/ppermute | solution.py:352
  152.6 45.1 %collective-permute-start.78 = (bf16[704,128]{1,0:T(8,128)(2,1)}, bf16[704,128]{1,0:T(8,128)(2,1)}, u32[]{:S(2)}, u32[]{:S(2)}) collective-permute-start(bf16[704,128]{1,0:T(8,128)(2,1)} %add_convert_fusion.8), channel_id=1, source_target_pairs={{0,4},{12,8},{1,5},{13,9},{2,6},{14,10},{3,7},{15,11},{16,20},{28,... | collective-permute-start | bytes 540680 | tf_op jit(solution)/shard_map/ppermute | solution.py:548
  202.3 15.3 %collective-permute-start.79 = (bf16[704,128]{1,0:T(8,128)(2,1)S(1)}, bf16[704,128]{1,0:T(8,128)(2,1)S(1)}, u32[]{:S(2)}, u32[]{:S(2)}) collective-permute-start(bf16[704,128]{1,0:T(8,128)(2,1)S(1)} %add_convert_fusion.7), channel_id=1, source_target_pairs={{4,8},{8,4},{5,9},{9,5},{6,10},{10,6},{7,11},{11,7},{20,24},{24,20... | collective-permute-start | bytes 540680 | tf_op jit(solution)/shard_map/ppermute | solution.py:550
  225.5 12.7 %collective-permute-start.61 = (bf16[512,512]{1,0:T(8,128)(2,1)S(1)}, bf16[512,512]{1,0:T(8,128)(2,1)S(1)}, u32[]{:S(2)}, u32[]{:S(2)}) collective-permute-start(bf16[512,512]{1,0:T(8,128)(2,1)S(1)} %add_convert_fusion.2), channel_id=1, source_target_pairs={{0,4},{12,8},{1,5},{13,9},{2,6},{14,10},{3,7},{15,11},{16,20},{28,... | collective-permute-start | bytes 1572872 | tf_op jit(solution)/shard_map/ppermute | solution.py:548
  249.5 16.2 %collective-permute-start.63 = (bf16[512,512]{1,0:T(8,128)(2,1)S(1)}, bf16[512,512]{1,0:T(8,128)(2,1)S(1)}, u32[]{:S(2)}, u32[]{:S(2)}) collective-permute-start(bf16[512,512]{1,0:T(8,128)(2,1)S(1)} %add_convert_fusion), channel_id=1, source_target_pairs={{4,0},{8,12},{5,1},{9,13},{6,2},{10,14},{7,3},{11,15},{20,16},{24,... | collective-permute-start | bytes 1572872 | tf_op jit(solution)/shard_map/ppermute | solution.py:552
  (156 other events, 1491.2 us)

commit v2 on v0

v2 whole, which is shorter than its diff:
```python
import functools

import jax
import jax.numpy as jnp
from jax import lax
from jax.experimental import pallas as pl
from jax.experimental.pallas import tpu as pltpu
from jax.sharding import PartitionSpec as P

EPSILON = 1e-05
F32 = jnp.float32
BF16 = jnp.bfloat16
GELU_A = 0.7978845608028654
GELU_B = 0.044715


def dot(left, right):
    return lax.dot_general(left, right, (((1,), (0,)), ((), ())), preferred_element_type=F32)


def dot_nt(left, right):
    return lax.dot_general(left, right, (((1,), (1,)), ((), ())), preferred_element_type=F32)


def dot_tn(left, right):
    return lax.dot_general(left, right, (((0,), (0,)), ((), ())), preferred_element_type=F32)


def normalize(values, axis=-1):
    centre = values - jnp.mean(values, axis=axis, keepdims=True)
    variance = jnp.mean(centre * centre, axis=axis, keepdims=True)
    scale_inv = lax.rsqrt(variance + EPSILON)
    return centre * scale_inv, scale_inv


def norm_back(grad_hat, normed, scale_inv, axis=-1):
    return scale_inv * (
        grad_hat
        - jnp.mean(grad_hat, axis=axis, keepdims=True)
        - normed * jnp.mean(grad_hat * normed, axis=axis, keepdims=True)
    )


def gelu_both(u):
    poly = GELU_A + (GELU_A * GELU_B) * (u * u)
    half = 0.5 + 0.5 * jnp.tanh(u * poly)
    value = u * half
    return value, half + (value * (1.0 - half)) * (6.0 * poly - 4.0 * GELU_A)


def stack(refs, lo, hi):
    return jnp.concatenate([r[:, lo:hi] for r in refs], axis=0)


def rows_of(refs):
    return refs[0][...] if len(refs) == 1 else jnp.concatenate([r[...] for r in refs], axis=0)


def sum_of(refs, lo=None, hi=None):
    parts = [r[...].astype(F32) if lo is None else r[:, lo:hi].astype(F32) for r in refs]
    while len(parts) > 1:
        parts = [sum(parts[i : i + 2]) if i + 1 < len(parts) else parts[i] for i in range(0, len(parts), 2)]
    return parts[0]


def spread(row, count):
    return jnp.concatenate([row[:, i * 128 : i * 128 + 128] for i in range(count)], axis=0)


def by_core(first, second):
    core = lax.axis_index("dp")
    pl.when(core == 0)(first)
    pl.when(core != 0)(second)


def onehot(idx, total):
    here = lax.broadcasted_iota(jnp.int32, (total, idx.shape[1]), 0)
    return (here == idx).astype(F32).astype(BF16)


def lanes(refs):
    return jnp.concatenate([refs[s] for s in range(refs.shape[0])], axis=1)


def edge_prep(graph, near, et_ref, nbr_ref, res_ref, ga_ref, gb_ref, f_ref, q_ref, idx_ref, mask_ref, gains_ref):
    rows = et_ref.shape[2]
    slots, total = idx_ref.shape[0], mask_ref.shape[1]

    @pl.when(pl.program_id(0) == 0)
    def _():
        at_graph, at_mp = lax.axis_index("graph"), lax.axis_index("mp")
        for s in range(slots):
            nbr = nbr_ref[at_mp * slots + s]
            if near:
                idx_ref[s] = ((nbr // rows) ^ at_graph) * rows + lax.rem(nbr, rows)
            else:
                moved = nbr + (total - at_graph * rows)
                idx_ref[s] = jnp.where(moved >= total, moved - total, moved)
        for k in range(graph):
            block = (at_graph ^ k) if near else lax.rem(at_graph + k, graph)
            mask_ref[:, k * rows : (k + 1) * rows] = res_ref[:, pl.ds(pl.multiple_of(block * rows, rows), rows)]
        for i, ref in enumerate((ga_ref, gb_ref)):
            gains_ref[i] = jnp.broadcast_to(ref[...], (rows, ref.shape[1])).T

    for s in range(et_ref.shape[0]):
        hat, _ = normalize(et_ref[s].astype(F32), 0)
        f_ref[s] = (hat * gains_ref[0]).astype(BF16)
        q_ref[s] = (hat * gains_ref[1]).astype(BF16)


def node_close(h1_ref, p0, p1, p2, p3, gain_ref, h2_ref, c_ref, out_ref):
    h2 = h1_ref[...] + sum_of((p0, p1, p2, p3))
    h2_ref[...] = h2
    hat, _ = normalize(h2)
    c_ref[...] = (hat * gain_ref[...]).astype(BF16)
    out_ref[...] = h2.astype(BF16)


def node_backward(
    t0, t1, t2, t3, h2_ref, cot_ref, gain_ref, slope_ref, win_ref, wout_ref,
    dh2_ref, dr_ref, dp_ref, gain_out, share_ref, part_ref,
):
    width = h2_ref.shape[1]
    dc = sum_of((t0, t1, t2, t3), 0, width)
    share_ref[...] = sum_of((t0, t1, t2, t3), width, width + 128).astype(BF16)
    hat, inv = normalize(h2_ref[...])
    gain_out[...] = jnp.sum(dc * hat, axis=0, keepdims=True)
    dh2 = cot_ref[...].astype(F32) + norm_back(dc * gain_ref[...], hat, inv)
    dh2_ref[...] = dh2
    dr = dh2.astype(BF16)
    dr_ref[...] = dr
    dp = (slope_ref[...].astype(F32) * dot_nt(dr, wout_ref[...])).astype(BF16)
    dp_ref[...] = dp
    part_ref[...] = dot_nt(dp, win_ref[...]).astype(BF16)


def pack_weights(ms, mo, me, mout, us, uo, ue, uout_t, front_ref, back_ref, mine_ref, first_ref, second_ref, half_ref):
    side = me.shape[0]
    gap = jnp.zeros((ms.shape[1], 256 - side), BF16)

    def turned(ref):
        return ref[...].astype(F32).T.astype(BF16)

    front = jnp.concatenate([turned(mo), turned(me), gap, turned(ue), gap], axis=1)
    back = jnp.concatenate([turned(ms), mout[...]], axis=1)
    out = jnp.concatenate([turned(uout_t), gap], axis=1)
    first = jnp.concatenate([turned(uo), out[:, :128]], axis=1)
    second = jnp.concatenate([turned(us), out[:, 128:]], axis=1)
    front_ref[...] = front
    back_ref[...] = back
    first_ref[...] = first
    second_ref[...] = second

    def keep_front():
        mine_ref[...] = front
        half_ref[...] = first

    def keep_back():
        mine_ref[...] = back
        half_ref[...] = second

    by_core(keep_front, keep_back)


def message_forward(nbr_scale, steps, parts, f_ref, idx_ref, mask_ref, gain_ref, front_ref, back_ref, *rest):
    node_refs, got, swapped = rest[:parts], rest[parts : parts + 3], rest[parts + 3 : parts + 6]
    slope_ref, pooled_ref, a_ref, fronts_ref, backs_ref, lhs_ref, rhs_ref, ps_ref, acc_ref = rest[parts + 6 :]
    step = pl.program_id(0)
    slots, side, rows = f_ref.shape
    total, width = a_ref.shape
    hidden = ps_ref.shape[0]

    @pl.when(step == 0)
    def _():
        fronts_ref[:rows, :] = front_ref[...]
        backs_ref[:rows, :] = back_ref[...]

        def place(front_of, back_of):
            for k in range(3):
                fronts_ref[(k + 1) * rows : (k + 2) * rows, :] = front_of[k][...]
                backs_ref[(k + 1) * rows : (k + 2) * rows, :] = back_of[k][...]

        by_core(lambda: place(got, swapped), lambda: place(swapped, got))
        block = node_refs[0].shape[0] if parts > 1 else 512
        for at in range(0, total, block):
            ref = node_refs[at // block] if parts > 1 else node_refs[0].at[at : at + block]
            hat, _ = normalize(ref[...].astype(F32))
            a = (hat * gain_ref[...]).astype(BF16)
            a_ref[at : at + block, :] = a
            lhs_ref[:hidden, at : at + block] = dot_nt(fronts_ref[:, :width], a).astype(BF16)
        lhs_ref[:hidden, total:] = fronts_ref[:, width : width + side]
        top = lax.broadcasted_iota(jnp.int32, (16, total), 0) == 0
        lhs_ref[hidden:, :total] = jnp.where(top, mask_ref[...].astype(F32), 0.0).astype(BF16)
        lhs_ref[hidden:, total:] = jnp.zeros((16, side), BF16)
        ps_ref[...] = dot_nt(backs_ref[:, :width], a_ref[:rows, :])
        acc_ref[...] = jnp.zeros_like(acc_ref)

    for s in range(slots):
        rhs_ref[:total, s * rows : (s + 1) * rows] = onehot(idx_ref[s], total)
        rhs_ref[total:, s * rows : (s + 1) * rows] = f_ref[s]
    u_all = dot(lhs_ref[...], rhs_ref[...])
    for s in range(slots):
        u = u_all[:hidden, s * rows : (s + 1) * rows] + ps_ref[...]
        mask = u_all[hidden : hidden + 1, s * rows : (s + 1) * rows]
        z, slope = gelu_both(u)
        acc_ref[...] += z * mask
        slope_ref[s] = (slope * mask).astype(BF16)

    @pl.when(step == steps - 1)
    def _():
        pooled_ref[...] = (acc_ref[...] * nbr_scale).T.astype(BF16)


def node_forward(
    s0, s1, s2, s3, nodes_ref, backs_ref, gain_ref, win_ref, wout_ref, s_ref, h1_ref, b_ref, y_ref, slope_ref, part_ref
):
    width = nodes_ref.shape[1]
    sums = []
    for p in range(4):
        sums.append(sum(
            ref[:, (p ^ k) * 128 : (p ^ k) * 128 + 128].astype(F32) for k, ref in enumerate((s0, s1, s2, s3))
        ).astype(BF16))
    pooled = jnp.concatenate(sums, axis=1)
    s_ref[...] = pooled
    h1 = nodes_ref[...].astype(F32) + dot(pooled, backs_ref[:, width : 2 * width])
    h1_ref[...] = h1
    hat, _ = normalize(h1)
    b = (hat * gain_ref[...]).astype(BF16)
    b_ref[...] = b
    y, slope = gelu_both(dot(b, win_ref[...]))
    y = y.astype(BF16)
    y_ref[...] = y
    slope_ref[...] = slope.astype(BF16)
    part_ref[...] = dot(y, wout_ref[...]).astype(BF16)


def update_nodes(steps, parts, outs, q_ref, cot_ref, idx_ref, fronts_ref, *rest):
    node_refs, (first_ref, second_ref) = rest[:parts], rest[parts : parts + 2]
    got, swapped = rest[parts + 2 : parts + 5], rest[parts + 5 : parts + 8]
    w_ref, dv_ref, r_ref, firsts_ref, seconds_ref = rest[parts + 8 : parts + 13]
    s_refs = rest[parts + 13 : parts + 13 + outs]
    lhs_ref, rhs_ref, ps_ref, wo_ref, racc_ref, sacc_ref = rest[parts + 13 + outs :]
    step = pl.program_id(0)
    slots, side, rows = q_ref.shape
    total = rhs_ref.shape[0] - side
    width = node_refs[0].shape[1]

    @pl.when(step == 0)
    def _():
        firsts_ref[:rows, :] = first_ref[...]
        seconds_ref[:rows, :] = second_ref[...]

        def place(first_of, second_of):
            for k in range(3):
                firsts_ref[(k + 1) * rows : (k + 2) * rows, :] = first_of[k][...]
                seconds_ref[(k + 1) * rows : (k + 2) * rows, :] = second_of[k][...]

        by_core(lambda: place(got, swapped), lambda: place(swapped, got))
        block = node_refs[0].shape[0] if parts > 1 else 512
        for at in range(0, total, block):
            ref = node_refs[at // block] if parts > 1 else node_refs[0].at[at : at + block]
            lhs_ref[:, at : at + block] = dot_nt(firsts_ref[:, :width], ref[...]).astype(BF16)
        lhs_ref[:, total:] = fronts_ref[:, width + 256 : width + 256 + side]
        wo_ref[...] = jnp.concatenate([firsts_ref[:, width:], seconds_ref[:, width : width + side - 128]], axis=1)
        ps_ref[...] = dot_nt(seconds_ref[:, :width], node_refs[0][:rows, :])
        racc_ref[...] = jnp.zeros_like(racc_ref)
        sacc_ref[...] = jnp.zeros_like(sacc_ref)

    for s in range(slots):
        rhs_ref[:total, s * rows : (s + 1) * rows] = onehot(idx_ref[s], total)
        rhs_ref[total:, s * rows : (s + 1) * rows] = q_ref[s]
    v_all = dot(lhs_ref[...], rhs_ref[...])
    g_all = dot(wo_ref[...], lanes(cot_ref))
    dvs = []
    for s in range(slots):
        w, slope = gelu_both(v_all[:, s * rows : (s + 1) * rows] + ps_ref[...])
        w_ref[s] = w.astype(BF16)
        dv = slope * g_all[:, s * rows : (s + 1) * rows]
        racc_ref[...] += dv
        dv = dv.astype(BF16)
        dv_ref[s] = dv
        dvs.append(dv)
    sacc_ref[...] += dot_nt(rhs_ref[:total, :], jnp.concatenate(dvs, axis=1))

    @pl.when(step == steps - 1)
    def _():
        r_ref[...] = racc_ref[...].T.astype(BF16)
        for b, ref in enumerate(s_refs):
            n = ref.shape[0]
            ref[...] = sacc_ref[b * n : (b + 1) * n, :].astype(BF16)


def update_edges(
    steps, et_ref, w_ref, dv_ref, q_ref, cot_ref, r_ref, fronts_ref, firsts_ref, seconds_ref,
    out_ref, dq_ref, x0, x1, x2, x3, ue_ref, uo_ref, gout_ref, gedge_ref,
):
    step = pl.program_id(0)
    slots, side, rows = et_ref.shape
    width = r_ref.shape[1]

    @pl.when(step == 0)
    def _():
        ue_ref[...] = fronts_ref[:, width + 256 : width + 256 + side].astype(F32).T.astype(BF16)
        uo = jnp.concatenate([firsts_ref[:, width:], seconds_ref[:, width : width + side - 128]], axis=1)
        uo_ref[...] = uo.astype(F32).T.astype(BF16)
        gout_ref[...] = jnp.zeros_like(gout_ref)
        gedge_ref[...] = jnp.zeros_like(gedge_ref)

    w, dv = lanes(w_ref), lanes(dv_ref)
    o_all = dot(uo_ref[...], w)
    dq_all = dot(ue_ref[...], dv)
    for s in range(slots):
        out_ref[s] = (et_ref[s].astype(F32) + o_all[:, s * rows : (s + 1) * rows]).astype(BF16)
        dq_ref[s] = dq_all[:, s * rows : (s + 1) * rows].astype(BF16)
    gout_ref[...] += dot_nt(lanes(cot_ref), w)
    gedge_ref[...] += dot_nt(lanes(q_ref), dv)

    @pl.when(step == steps - 1)
    def _():
        for k, ref in enumerate((x0, x1, x2, x3)):
            at = slice(k * 128, k * 128 + 128)
            ref[:rows, :] = r_ref[:, at]
            ref[rows : rows + side, :] = gedge_ref[:, at].astype(BF16)
            ref[rows + side :, :] = gout_ref[:, at].astype(BF16)


def update_terms(parts, r_ref, firsts_ref, seconds_ref, *rest):
    s_refs, outs = rest[:parts], rest[parts + 1 :]
    width = r_ref.shape[1]
    total = sum_of(s_refs).astype(BF16)
    term = (dot(r_ref[...], seconds_ref[:, :width]) + dot(total, firsts_ref[:, :width])).astype(BF16)
    for k, ref in enumerate(outs):
        ref[:, :width] = term
        ref[:, width:] = total[:, k * 128 : k * 128 + 128]


def message_terms(parts, r_ref, fronts_ref, backs_ref, nodes_ref, gb_ref, gc_ref, ge_ref, *rest):
    s_refs, outs = rest[:parts], rest[parts:]
    rows, width = r_ref.shape
    total = sum_of(s_refs).astype(BF16)
    term = dot(r_ref[...], backs_ref[:, :width]) + dot(total, fronts_ref[:, :width])
    hat, _ = normalize(nodes_ref[...].astype(F32))
    gain = jnp.sum(term * hat, axis=0, keepdims=True)
    edge = jnp.concatenate([ge_ref[0:2, :], jnp.zeros((2, width - 256), F32)], axis=1)
    gains = jnp.concatenate(
        [gain, gb_ref[...] * 0.25, gc_ref[...] * 0.25, edge, jnp.zeros((11, width), F32)], axis=0
    ).astype(BF16)
    term = term.astype(BF16)
    for k, ref in enumerate(outs):
        ref[:rows, :width] = term
        ref[:rows, width:] = total[:, k * 128 : k * 128 + 128]
        ref[rows:, :width] = gains
        ref[rows:, width:] = jnp.zeros((16, 128), BF16)


def early_grads(b_ref, dp_ref, y_ref, dr_ref, c_ref, share_ref, x0, x1, x2, x3, keep_ref, send_ref):
    rows, width = c_ref.shape
    extra = sum_of((x0, x1, x2, x3)).astype(BF16)
    side = (extra.shape[0] - rows) // 2
    part = (width + side) // 4
    piece = keep_ref.shape[0] // 4

    def put(ref, large, small):
        large = large.astype(BF16)
        small = jnp.concatenate(small, axis=0)
        for i in range(4):
            ref[i * piece : i * piece + 128, :] = large[i * 128 : i * 128 + 128]
            own = jnp.concatenate([small[i * part : (i + 1) * part], jnp.zeros((192 - part, 128), F32)], axis=0)
            ref[i * piece + 128 : (i + 1) * piece, :] = jnp.concatenate(
                [own[j * 48 : j * 48 + 48] for j in range(4)], axis=1
            ).astype(BF16)

    def run(one, two):
        put(one, dot_tn(b_ref[...], dp_ref[...]),
            [dot_tn(c_ref[...], extra[:rows]), extra[rows : rows + side].astype(F32)])
        put(two, dot_tn(y_ref[...], dr_ref[...]),
            [dot_tn(c_ref[...], share_ref[...]), extra[rows + side :].astype(F32)])

    by_core(lambda: run(keep_ref, send_ref), lambda: run(send_ref, keep_ref))


def early_pieces(keep_ref, got_ref, *outs):
    piece = keep_ref.shape[0] // 4
    for k, ref in enumerate(outs):
        at = pl.ds(pl.multiple_of((lax.axis_index("graph") ^ k) * piece, 16), piece)
        ref[...] = (keep_ref[at, :].astype(F32) + got_ref[at, :].astype(F32)).astype(BF16)


def early_total(p0, p1, p2, p3, out_ref):
    out_ref[...] = sum_of((p0, p1, p2, p3)).astype(BF16)


def finish_early(near, *refs):
    mine, theirs = refs[:4], refs[4:8]
    gin_ref, gout_ref, self_ref, edge_ref, other_ref, out_ref, one_ref, two_ref = refs[8:]
    width, side = gin_ref.shape[0], edge_ref.shape[0]
    part = (width + side) // 4

    def run(one, two):
        for pieces, large, small in ((one, gin_ref, one_ref), (two, gout_ref, two_ref)):
            for k, ref in enumerate(pieces):
                i = (lax.axis_index("graph") ^ k) if near else k
                large[pl.ds(pl.multiple_of(i * 128, 128), 128), :] = ref[:128, :].astype(F32)
                own = jnp.concatenate([ref[128:, j * 128 : j * 128 + 128] for j in range(4)], axis=0).astype(F32)
                small[pl.ds(pl.multiple_of(i * part, 16), part), :] = own[:part]

    by_core(lambda: run(mine, theirs), lambda: run(theirs, mine))
    self_ref[...] = one_ref[:width, :]
    edge_ref[...] = one_ref[width:, :]
    other_ref[...] = two_ref[:width, :]
    out_ref[...] = two_ref[width:, :]


def message_backward(nbr_scale, steps, outs, t0, t1, t2, t3, h1_ref, dh2_ref, gain_ref, backs_ref, slope_ref, idx_ref, *rest):
    rest = rest[1:]
    dh1_ref, dt_ref, gain_out, du_ref, r_ref = rest[:5]
    s_refs = rest[5 : 5 + outs]
    g_ref, racc_ref, sacc_ref = rest[5 + outs :]
    step = pl.program_id(0)
    slots, hidden, rows = slope_ref.shape
    total, width = sacc_ref.shape[0], h1_ref.shape[1]

    @pl.when(step == 0)
    def _():
        db = sum_of((t0, t1, t2, t3))
        hat, inv = normalize(h1_ref[...])
        gain_out[...] = jnp.sum(db * hat, axis=0, keepdims=True)
        dh1 = dh2_ref[...] + norm_back(db * gain_ref[...], hat, inv)
        dh1_ref[...] = dh1
        dt = dh1.astype(BF16)
        dt_ref[...] = dt
        g_ref[...] = dot_nt(backs_ref[:, width : 2 * width], dt) * nbr_scale
        racc_ref[...] = jnp.zeros_like(racc_ref)
        sacc_ref[...] = jnp.zeros_like(sacc_ref)

    dus, hots = [], []
    for s in range(slots):
        du = slope_ref[s].astype(F32) * g_ref[...]
        racc_ref[...] += du
        du = du.astype(BF16)
        du_ref[s] = du
        dus.append(du)
        hots.append(onehot(idx_ref[s], total))
    sacc_ref[...] += dot_nt(jnp.concatenate(hots, axis=1), jnp.concatenate(dus, axis=1))

    @pl.when(step == steps - 1)
    def _():
        r_ref[...] = racc_ref[...].T.astype(BF16)
        for b, ref in enumerate(s_refs):
            n = ref.shape[0]
            ref[...] = sacc_ref[b * n : (b + 1) * n, :].astype(BF16)


def message_edges(
    steps, et_ref, du_ref, dq_ref, f_ref, cot_ref, gains_ref, r_ref, fronts_ref, out_ref, ge_ref, m0, m1, m2, m3,
    we_ref, gedge_ref, ga_ref, gb_ref,
):
    step = pl.program_id(0)
    slots, side, rows = et_ref.shape
    width = r_ref.shape[1]

    @pl.when(step == 0)
    def _():
        we_ref[...] = fronts_ref[:, width : width + side].astype(F32).T.astype(BF16)
        gedge_ref[...] = jnp.zeros_like(gedge_ref)
        ga_ref[...] = jnp.zeros_like(ga_ref)
        gb_ref[...] = jnp.zeros_like(gb_ref)

    du = lanes(du_ref)
    df_all = dot(we_ref[...], du)
    gedge_ref[...] += dot_nt(lanes(f_ref), du)
    for s in range(slots):
        df = df_all[:, s * rows : (s + 1) * rows]
        dq = dq_ref[s].astype(F32)
        hat, inv = normalize(et_ref[s].astype(F32), 0)
        ga_ref[...] += df * hat
        gb_ref[...] += dq * hat
        out_ref[s] = cot_ref[s].astype(F32) + norm_back(gains_ref[0] * df + gains_ref[1] * dq, hat, inv, 0)

    @pl.when(step == steps - 1)
    def _():
        lane = lax.broadcasted_iota(jnp.int32, (side, 256), 1)
        row = lax.broadcasted_iota(jnp.int32, (side, 256), 0)

        def laid(ref):
            column = jnp.sum(ref[...], axis=1, keepdims=True)
            return jnp.sum(jnp.where(row == lane, column, 0.0), axis=0, keepdims=True)

        ge_ref[...] = jnp.concatenate([laid(ga_ref), laid(gb_ref), jnp.zeros((6, 256), F32)], axis=0)
        for k, ref in enumerate((m0, m1, m2, m3)):
            at = slice(k * 128, k * 128 + 128)
            ref[:rows, :] = r_ref[:, at]
            ref[rows:, :] = gedge_ref[:, at].astype(BF16)


def late_grads(m0, m1, m2, m3, s_ref, dt_ref, order_ref, share_ref, keep_ref, send_ref):
    rows, width = dt_ref.shape
    total = sum_of((m0, m1, m2, m3))
    share_ref[...] = total[:rows].astype(BF16)
    gout = dot_tn(s_ref[...], dt_ref[...])
    every = jnp.concatenate([total[rows:]] + [gout[:, i * 128 : i * 128 + 128] for i in range(width // 128)], axis=0)
    every = every.astype(BF16)
    half = keep_ref.shape[0]

    def put(one, two):
        one[...] = every[:half]
        two[...] = every[half:]

    by_core(lambda: put(keep_ref, send_ref), lambda: put(send_ref, keep_ref))


def node_finish(t0, t1, t2, t3, nodes_ref, dh1_ref, gain_ref, out_ref, share_ref):
    rows, width = dh1_ref.shape
    every = sum_of((t0, t1, t2, t3))
    hat, inv = normalize(nodes_ref[...].astype(F32))
    out_ref[...] = dh1_ref[...] + norm_back(every[:rows, :width] * gain_ref[...], hat, inv)
    share_ref[:rows, :] = every[:rows, width:].astype(BF16)
    share_ref[rows:, :] = jnp.concatenate(
        [every[rows : rows + 8, i * 128 : i * 128 + 128] for i in range(width // 128)], axis=0
    ).astype(BF16)


def message_grads(parts, a_ref, *rest):
    one, two, out_ref = rest[:parts], rest[parts : 2 * parts], rest[2 * parts]
    rows = a_ref.shape[0] // parts
    width = a_ref.shape[1]
    other = dot_tn(a_ref[...], jnp.concatenate([r[:rows, :] for r in two], axis=0))
    own = dot_tn(a_ref[...], jnp.concatenate([r[:rows, :] for r in one], axis=0))
    out_ref[:width, :] = other.astype(BF16)
    out_ref[width : 2 * width, :] = own.astype(BF16)
    low = 2 * width + one[0].shape[0] - rows
    out_ref[2 * width : low, :] = sum(r[rows:, :].astype(F32) for r in one).astype(BF16)
    out_ref[low:, :] = sum(r[rows:, :].astype(F32) for r in two).astype(BF16)


def finish_late(
    mine_ref, theirs_ref, other_ref, self_ref, edge_ref, out_ref, ga_ref, gb_ref, gc_ref, gea_ref, geb_ref
):
    width, side = other_ref.shape[0], edge_ref.shape[0]
    rows = out_ref.shape[0]
    other_ref[...] = mine_ref[:width, :].astype(F32) + theirs_ref[:width, :].astype(F32)
    self_ref[...] = mine_ref[width : 2 * width, :].astype(F32) + theirs_ref[width : 2 * width, :].astype(F32)
    low = mine_ref.shape[0] - 8 * (width // 128)
    gains = mine_ref[low:, :].astype(F32) + theirs_ref[low:, :].astype(F32)
    for i, ref in enumerate((ga_ref, gb_ref, gc_ref)):
        ref[...] = jnp.concatenate([gains[8 * j + i : 8 * j + i + 1] for j in range(width // 128)], axis=1)
    for i, ref in ((3, gea_ref), (4, geb_ref)):
        ref[...] = jnp.concatenate([gains[i : i + 1], gains[8 + i : 9 + i]], axis=1)[:, :side]

    def run(first, second):
        every = jnp.concatenate([first[2 * width : low, :], second[2 * width : low, :]], axis=0).astype(F32)
        edge_ref[...] = every[:side]
        out_ref[...] = jnp.concatenate(
            [every[side + i * rows : side + (i + 1) * rows] for i in range(width // 128)], axis=1
        )

    by_core(lambda: run(mine_ref, theirs_ref), lambda: run(theirs_ref, mine_ref))


def whole(shape):
    zeros = (0,) * len(shape)
    return pl.BlockSpec(tuple(shape), lambda i: zeros)


def in_bytes(shape, dtype):
    n = jnp.dtype(dtype).itemsize
    for d in shape:
        n *= d
    return n


AFTER = pl.BlockSpec(memory_space=pl.ANY)


def call(name, body, grid, ins, outs, scratch=(), vmem=24):
    ins = [a if isinstance(a, tuple) else (a, whole(a.shape)) for a in ins]
    outs = [o if len(o) == 3 else o + (whole(o[0]),) for o in outs]
    moved = sum(in_bytes(a.shape, a.dtype) for a, _ in ins) + sum(in_bytes(sh, t) for sh, t, _ in outs)
    return pl.pallas_call(
        body,
        grid=(grid,),
        in_specs=[s for _, s in ins],
        out_specs=[s for _, _, s in outs],
        out_shape=[jax.ShapeDtypeStruct(sh, t) for sh, t, _ in outs],
        scratch_shapes=list(scratch),
        compiler_params=pltpu.CompilerParams(vmem_limit_bytes=vmem << 20, dimension_semantics=("arbitrary",)),
        cost_estimate=pl.CostEstimate(flops=0, bytes_accessed=moved, transcendentals=0),
        name=name,
    )(*[a for a, _ in ins])


def swap(values, axis, bits, size):
    return lax.ppermute(values, axis, [(i, i ^ bits) for i in range(size)])


def partners(values, axis, size):
    return [values] + [swap(values, axis, k, size) for k in range(1, size)]


def deal(pieces, axis, size):
    return [pieces[0]] + [swap(pieces[k], axis, k, size) for k in range(1, size)]


def turn(values, start, axis):
    return lax.dynamic_slice_in_dim(
        jnp.concatenate([values, values], axis=axis), start, values.shape[axis], axis=axis
    )


def after(values, *others):
    return lax.optimization_barrier((values,) + others)[0]


def local(sizes, *args):
    (
        nodes, edges, neighbours, resmask, node_gain_a, edge_gain_a, message_self, message_other, message_edge,
        message_out, node_gain_b, ffn_in, ffn_out, node_gain_c, edge_gain_b, update_self, update_other, update_edge,
        update_out, node_cot, edge_cot,
    ) = args
    cores, graph, mp = sizes
    near = graph <= 4
    at_graph = None if near else lax.axis_index("graph")
    _, rows, width = nodes.shape
    slots, side = edges.shape[2:]
    nbrs = neighbours.shape[2]
    total = resmask.shape[1]
    shard = message_self.shape[1]
    hidden = shard * mp
    ff = ffn_in.shape[1]
    vmem = 16 if total <= 1024 else 60
    tile = 3 if slots % 3 == 0 else 1
    steps = slots // tile
    run = functools.partial(call, vmem=vmem)

    def tiles(*dims):
        return pl.BlockSpec((tile,) + dims, lambda i: (i,) + (0,) * len(dims))

    def gather_rows(values):
        if near:
            return partners(values, "graph", graph)
        return [turn(lax.all_gather(values, "graph", axis=0, tiled=True), at_graph * rows, 0)]

    def return_rows(blocks):
        if near:
            return deal(blocks, "graph", graph)
        placed = turn(blocks[0], total - at_graph * rows, 0)
        return [lax.psum_scatter(placed, "graph", scatter_dimension=0, tiled=True)]

    blocks = [((rows, hidden), BF16)] * graph if near else [((total, hidden), BF16)]
    outs = len(blocks)
    node, cot_n = nodes[0], node_cot[0]
    ga_n, gb_n, gc_n = node_gain_a[None, :], node_gain_b[None, :], node_gain_c[None, :]

    front, back, mine, first, second, half = run(
        "pack_weights", pack_weights, 1,
        [pltpu.with_memory_space_constraint(w, pltpu.HBM) for w in (
            message_self, message_other, message_edge, message_out, update_self, update_other, update_edge, update_out.T
        )],
        [((shard, width + 512), BF16)] + [((shard, 2 * width), BF16)] * 2 + [((shard, width + 128), BF16)] * 3,
    )
    got = partners(mine, "mp", mp)[1:]
    nodes_all = gather_rows(node)
    swapped = [swap(v, "dp", 1, cores) for v in got]

    et = jnp.transpose(edges[0], (1, 2, 0))
    cot = jnp.transpose(edge_cot[0], (1, 2, 0))
    edge_spec, hid_spec = tiles(side, rows), tiles(hidden, rows)
    edge_sh, hid_sh = (slots, side, rows), (slots, hidden, rows)

    f, q, idx, mask_row, gains_e = run(
        "edge_prep", functools.partial(edge_prep, graph, near), steps,
        [(et, edge_spec), jnp.transpose(neighbours, (2, 0, 1)), resmask, edge_gain_a[None, :], edge_gain_b[None, :]],
        [(edge_sh, BF16, edge_spec), (edge_sh, BF16, edge_spec), ((slots, 1, rows), jnp.int32), ((1, total), jnp.int32),
         ((2, side, rows), F32)],
    )
    idx = (idx, tiles(1, rows))
    slope_m, pooled_part, a_all, fronts, backs = run(
        "message_forward", functools.partial(message_forward, 1.0 / nbrs, steps, len(nodes_all)), steps,
        [(f, edge_spec), idx, mask_row, ga_n, front, back] + nodes_all + got + swapped,
        [(hid_sh, BF16, hid_spec), ((rows, hidden), BF16), ((total, width), BF16), ((hidden, width + 512), BF16),
         ((hidden, 2 * width), BF16)],
        [pltpu.VMEM((hidden + 16, total + side), BF16), pltpu.VMEM((total + side, tile * rows), BF16),
         pltpu.VMEM((hidden, rows), F32), pltpu.VMEM((hidden, rows), F32)],
    )

    pooled, h1, b, y, slope_f, h2_part = run(
        "node_forward", node_forward, 1,
        partners(pooled_part, "mp", mp) + [node, backs, gb_n, ffn_in, ffn_out],
        [((rows, hidden), BF16), ((rows, width), F32), ((rows, width), BF16), ((rows, ff), BF16), ((rows, ff), BF16),
         ((rows, width), BF16)],
    )
    h2, c_own, nodes_out = run(
        "node_close", node_close, 1, [h1] + partners(h2_part, "mp", mp) + [gc_n],
        [((rows, width), F32), ((rows, width), BF16), ((rows, width), BF16)],
    )
    c_all = gather_rows(c_own)
    late_got = partners(after(half, c_own), "mp", mp)[1:]
    late_swapped = [swap(v, "dp", 1, cores) for v in late_got]

    w_act, dv, r_upd, firsts, seconds, *s_upd = run(
        "update_nodes", functools.partial(update_nodes, steps, len(c_all), outs), steps,
        [(q, edge_spec), (cot, edge_spec), idx, fronts] + c_all + [first, second] + late_got + late_swapped,
        [(hid_sh, BF16, hid_spec), (hid_sh, BF16, hid_spec), ((rows, hidden), BF16)]
        + [((hidden, width + 128), BF16)] * 2 + blocks,
        [pltpu.VMEM((hidden, total + side), BF16), pltpu.VMEM((total + side, tile * rows), BF16),
         pltpu.VMEM((hidden, rows), F32), pltpu.VMEM((hidden, side), BF16), pltpu.VMEM((hidden, rows), F32),
         pltpu.VMEM((total, hidden), F32)],
    )
    s_upd_parts = return_rows(s_upd)
    eo, dq, *extra = run(
        "update_edges", functools.partial(update_edges, steps), steps,
        [(et, edge_spec), (w_act, hid_spec), (dv, hid_spec), (q, edge_spec), (cot, edge_spec), r_upd, fronts, firsts, seconds],
        [(edge_sh, BF16, edge_spec), (edge_sh, BF16, edge_spec)] + [((rows + 2 * side, shard), BF16)] * mp,
        [pltpu.VMEM((side, hidden), BF16), pltpu.VMEM((side, hidden), BF16), pltpu.VMEM((side, hidden), F32),
         pltpu.VMEM((side, hidden), F32)],
    )
    edges_out = jnp.transpose(eo, (2, 0, 1))[None]
    order = extra[0]
    extra = deal(extra, "mp", mp)

    terms = run(
        "update_terms", functools.partial(update_terms, outs), 1, [r_upd, firsts, seconds] + s_upd_parts + [(order, AFTER)],
        [((rows, width + shard), BF16)] * mp,
    )
    dh2, dr, dp_ffn, gain_c, share, db_part = run(
        "node_backward", node_backward, 1, deal(terms, "mp", mp) + [h2, cot_n, gc_n, slope_f, ffn_in, ffn_out],
        [((rows, width), F32), ((rows, width), BF16), ((rows, ff), BF16), ((1, width), F32), ((rows, shard), BF16),
         ((rows, width), BF16)],
    )
    db_parts = partners(db_part, "mp", mp)

    piece = width // 4 + 48
    keep, send = run(
        "early_grads", early_grads, 1, [b, dp_ffn, y, dr, c_own, share] + extra, [((4 * piece, ff), BF16)] * 2,
    )
    got = swap(send, "dp", 1, cores)
    if near:
        early = run("early_pieces", early_pieces, 1, [keep, got], [((piece, ff), BF16)] * 4)
        order = early[0]
        (early,) = run("early_total", early_total, 1, deal(early, "graph", graph), [((piece, ff), BF16)])
        early = partners(early, "graph", graph)
    else:
        order = got
        early = lax.psum(keep.astype(F32) + got.astype(F32), "graph").astype(BF16)
        early = [early[i * piece : (i + 1) * piece] for i in range(4)]

    dh1, dt, gain_b, du, r_msg, *s_msg = run(
        "message_backward", functools.partial(message_backward, 1.0 / nbrs, steps, outs), steps,
        db_parts + [h1, dh2, gb_n, backs, (slope_m, hid_spec), idx, (order, AFTER)],
        [((rows, width), F32), ((rows, width), BF16), ((1, width), F32), (hid_sh, BF16, hid_spec),
         ((rows, hidden), BF16)] + blocks,
        [pltpu.VMEM((hidden, rows), F32), pltpu.VMEM((hidden, rows), F32), pltpu.VMEM((total, hidden), F32)],
    )
    s_msg_parts = return_rows(s_msg)
    ge, gains_edge, *mixed = run(
        "message_edges", functools.partial(message_edges, steps), steps,
        [(et, edge_spec), (du, hid_spec), (dq, edge_spec), (f, edge_spec), (cot, edge_spec), gains_e, r_msg, fronts],
        [(edge_sh, F32, edge_spec), ((8, 256), F32)] + [((rows + side, shard), BF16)] * mp,
        [pltpu.VMEM((side, hidden), BF16), pltpu.VMEM((side, hidden), F32), pltpu.VMEM((side, rows), F32),
         pltpu.VMEM((side, rows), F32)],
    )
    grad_edges = jnp.transpose(ge, (2, 0, 1))[None]
    mixed = deal(mixed, "mp", mp)

    terms = run(
        "message_terms", functools.partial(message_terms, outs), 1,
        [r_msg, fronts, backs, node, gain_b, gain_c, gains_edge] + s_msg_parts,
        [((rows + 16, width + shard), BF16)] * mp,
    )
    order = terms[0]
    terms = deal(terms, "mp", mp)
    half = (side + width) // 2
    first_rows = pl.BlockSpec((rows, shard), lambda i: (0, 0))
    share_r, keep, send = run(
        "late_grads", late_grads, 1, mixed + [(pooled, first_rows), dt, (order, AFTER)],
        [((rows, shard), BF16)] + [((half, shard), BF16)] * 2,
    )
    late = (keep.astype(F32) + swap(send, "dp", 1, cores).astype(F32)).astype(BF16)
    one = jnp.concatenate([share_r, late], axis=0)
    grad_nodes, two = run(
        "node_finish", node_finish, 1, terms + [node, dh1, ga_n],
        [((rows, width), F32), ((rows + width // 16, shard), BF16)],
    )
    if near:
        one, two = partners(one, "graph", graph), partners(two, "graph", graph)
    else:
        one, two = [one], [two]
    parts = len(one)
    (part,) = run(
        "message_grads", functools.partial(message_grads, parts), 1,
        [(a_all, pl.BlockSpec((parts * rows, width), lambda i: (0, 0)))] + one + two,
        [((2 * width + half + width // 16, shard), BF16)],
    )
    if not near:
        part = lax.psum(part, "graph")
    grad_mo, grad_ms, grad_me, grad_mout, gain_a, gain_b, gain_c, gain_ea, gain_eb = run(
        "finish_late", finish_late, 1, [part, swap(part, "dp", 1, cores)],
        [((width, shard), F32), ((width, shard), F32), ((side, shard), F32), ((shard, width), F32), ((1, width), F32),
         ((1, width), F32), ((1, width), F32), ((1, side), F32), ((1, side), F32)],
    )
    grad_in, grad_out, grad_us, grad_ue, grad_uo, grad_uout = run(
        "finish_early", functools.partial(finish_early, near), 1, early + [swap(v, "dp", 1, cores) for v in early],
        [((width, ff), F32), ((ff, width), F32), ((width, shard), F32), ((side, shard), F32), ((width, shard), F32),
         ((side, shard), F32)],
        [pltpu.VMEM((width + side, shard), F32)] * 2,
    )
    return (
        nodes_out[None],
        edges_out,
        grad_nodes[None],
        grad_edges,
        gain_a[0],
        gain_ea[0],
        grad_ms,
        grad_mo,
        grad_me,
        grad_mout,
        gain_b[0],
        grad_in,
        grad_out,
        gain_c[0],
        gain_eb[0],
        grad_us,
        grad_uo,
        grad_ue,
        grad_uout.T,
    )


def solution(mesh):
    sizes = (mesh.shape["dp"], mesh.shape["graph"], mesh.shape["mp"])
    rows = P("dp", "graph", None)
    slots = P("dp", "graph", "mp", None)
    cols, tops = P(None, "mp"), P("mp", None)
    return jax.shard_map(
        functools.partial(local, sizes),
        mesh=mesh,
        in_specs=(
            rows, slots, rows, P("dp", None), P(), P(), cols, cols, cols, tops, P(), cols, tops, P(), P(), cols, cols,
            cols, tops, rows, slots,
        ),
        out_specs=(
            rows, slots, rows, slots, P(), P(), cols, cols, cols, tops, P(), cols, tops, P(), P(), cols, cols, cols,
            tops,
        ),
        check_vma=False,
    )
```

time: 916 us -> 199 us (0.22)
  waiting for transfers between devices: 422 us -> 62.4 us
  local copies, waits for them, and re-layouts: 171 us -> 5.53 us
  other arithmetic: 147 us -> 0.04 us
  matrix products: 92.6 us -> 0 us
  starting transfers between devices: 0.78 us -> 92.2 us
  blocking collectives: 58.2 us -> 0 us
  Pallas kernels: 0 us -> 37 us
  between operations: 15.2 us -> 0.96 us
    psum x6 -> x0, waiting for transfers between devices: 270 us -> none  [the longest x5 177 us: unit_sum(): return lax.psum(partial_sum, 'mp')]
    unnamed x16 -> x0, waiting for transfers between devices: 108 us -> none
    scatter-add x2 -> x0, other arithmetic: 94.2 us -> none  [return_rows(): jax.ops.segment_sum(terms.reshape(-1, width), offsets.reshape(-1), num_se...]
    dot_general x30 -> x0, matrix products: 92.6 us -> none  [mixed(): return jnp.einsum(form, left, right, preferred_element_type=jnp.float32)]
    ppermute x0 -> x64, starting transfers between devices: none -> 92.2 us  [swap(): return lax.ppermute(values, axis, [(i, i ^ bits) for i in range(size)])]
    gather x4 -> x0, local copies, waits for them, and re-layouts: 89.7 us -> none  [the longest x2 45.3 us: local(): jnp.take_along_axis(resmask, flat_index, axis=1).astype(jnp.float32)]
    ppermute x0 -> x64, waiting for transfers between devices: none -> 62.4 us  [swap(): return lax.ppermute(values, axis, [(i, i ^ bits) for i in range(size)])]
    another operation x5 -> x0, local copies, waits for them, and re-layouts: 48 us -> none
  transfers between devices with their start and end apart: 13 -> 64, of which waited for: 11 -> 27; matrix products, arithmetic and copies ran while one was open for 24% -> 0% of each run, Pallas kernels for 0% -> 7%
where the time goes in v2:
time: 199 us; the launch traced here: 198 us
  starting transfers between devices  92.2 us (46%)
  waiting for transfers between devices  62.4 us (31%)
  Pallas kernels  37 us (19%)
  local copies, waits for them, and re-layouts  5.53 us (3%)
    ppermute x64, starting transfers between devices, swap(): return lax.ppermute(values, axis, [(i, i ^ bits) for i in range(size)])  92.2 us
    ppermute x64, waiting for transfers between devices, swap(): return lax.ppermute(values, axis, [(i, i ^ bits) for i in range(size)])  62.4 us
    pallas_call x20, Pallas kernels, call(): pl.pallas_call(body, grid=(grid,), in_specs=[s for _, s in ins], out_spec...  37 us
    unnamed x32, local copies, waits for them, and re-layouts  5.53 us
  transfers between devices with their start and end apart: 64, of which 27 were waited for; matrix products, arithmetic and copies ran while one was open for 0% of the time, Pallas kernels for 7%

profile of v2, /device:TPU:0, one launch (start us, length us, event | category | flops | bytes accessed | tf_op | source)
XLA Modules:
  0.0 198.2 jit_solution(15500992857131425576)
XLA Ops:
  2.2 4.0 %collective-permute-start.5 = (bf16[128,1024]{1,0:T(8,128)(2,1)S(1)}, bf16[128,1024]{1,0:T(8,128)(2,1)S(1)}, u32[]{:S(2)}, u32[]{:S(2)}) collective-permute-start(bf16[128,1024]{1,0:T(8,128)(2,1)S(1)} %get-tuple-element.120), channel_id=1, source_target_pairs={{0,3},{1,2},{2,1},{3,0},{4,7},{5,6},{6,5},{7,4},{8,11},{9,10},{10,... | collective-permute-start | bytes 786440 | tf_op jit(solution)/shard_map/ppermute | solution.py:593
  6.8 4.0 %collective-permute-start.2 = (bf16[128,512]{1,0:T(8,128)(2,1)}, bf16[128,512]{1,0:T(8,128)(2,1)S(1)}, u32[]{:S(2)}, u32[]{:S(2)}) collective-permute-start(bf16[128,512]{1,0:T(8,128)(2,1)} %bitcast.35), channel_id=1, source_target_pairs={{0,12},{4,8},{8,4},{12,0},{1,13},{5,9},{9,5},{13,1},{2,14},{6,10},... | collective-permute-start | bytes 393224 | tf_op jit(solution)/shard_map/ppermute | solution.py:593
  13.3 4.7 %collective-permute-done.4.rest_5_ = bf16[128,1024]{1,0:T(8,128)(2,1)S(1)} collective-permute-done((bf16[128,1024]{1,0:T(8,128)(2,1)S(1)}, bf16[128,1024]{1,0:T(8,128)(2,1)S(1)}, u32[]{:S(2)}, u32[]{:S(2)}) %collective-permute-start.4) | collective-permute-done | bytes 262176 | tf_op jit(solution)/shard_map/ppermute | solution.py:593
  30.1 6.8 %message_forward.1 = (bf16[15,512,128]{2,1,0:T(8,128)(2,1)S(1)}, bf16[128,512]{1,0:T(8,128)(2,1)S(1)}, bf16[512,512]{1,0:T(8,128)(2,1)S(1)}, bf16[512,1024]{1,0:T(8,128)(2,1)S(1)}, bf16[512,1024]{1,0:T(8,128)(2,1)S(1)}) custom-call(bf16[15,192,128]{2,1,0:T(8,128)(2,1)S(1)} %get-tuple-element.115.f_ref, s32[15,1,128]{2,1,0:T(1,128)S(1)} %get-tuple-element.116.idx_ref, ...), custom_call_target="tpu_custom_call" | custom-call | bytes 8089088 | tf_op jit(solution)/shard_map/message_forward/pallas_call | solution.py:579
  40.5 3.5 %collective-permute-done.11.s3 = bf16[128,512]{1,0:T(8,128)(2,1)S(1)} collective-permute-done((bf16[128,512]{1,0:T(8,128)(2,1)S(1)}, bf16[128,512]{1,0:T(8,128)(2,1)S(1)}, u32[]{:S(2)}, u32[]{:S(2)}) %collective-permute-start.11) | collective-permute-done | bytes 131104 | tf_op jit(solution)/shard_map/ppermute | solution.py:593
  49.7 3.5 %collective-permute-done.14.p3 = bf16[128,512]{1,0:T(8,128)(2,1)S(1)} collective-permute-done((bf16[128,512]{1,0:T(8,128)(2,1)S(1)}, bf16[128,512]{1,0:T(8,128)(2,1)S(1)}, u32[]{:S(2)}, u32[]{:S(2)}) %collective-permute-start.14) | collective-permute-done | bytes 131104 | tf_op jit(solution)/shard_map/ppermute | solution.py:593
  58.9 4.8 %collective-permute-start.17 = (bf16[128,512]{1,0:T(8,128)(2,1)S(1)}, bf16[128,512]{1,0:T(8,128)(2,1)S(1)}, u32[]{:S(2)}, u32[]{:S(2)}) collective-permute-start(bf16[128,512]{1,0:T(8,128)(2,1)S(1)} %get-tuple-element.128.rest_0_.c_ref), channel_id=1, source_target_pairs={{0,12},{4,8},{8,4},{12,0},{1,13},{5,9},{9,5},{13,1},{2,14},{6,10},... | collective-permute-start | bytes 393224 | tf_op jit(solution)/shard_map/ppermute | solution.py:593
  67.4 4.4 %collective-permute-start.15 = (bf16[128,512]{1,0:T(8,128)(2,1)S(1)}, bf16[128,512]{1,0:T(8,128)(2,1)S(1)}, u32[]{:S(2)}, u32[]{:S(2)}) collective-permute-start(bf16[128,512]{1,0:T(8,128)(2,1)S(1)} %get-tuple-element.128.rest_0_.c_ref), channel_id=1, source_target_pairs={{0,4},{4,0},{8,12},{12,8},{1,5},{5,1},{9,13},{13,9},{2,6},{6,2},{1... | collective-permute-start | bytes 393224 | tf_op jit(solution)/shard_map/ppermute | solution.py:593
  72.1 3.0 %collective-permute-done.15.rest_1_ = bf16[128,512]{1,0:T(8,128)(2,1)S(1)} collective-permute-done((bf16[128,512]{1,0:T(8,128)(2,1)S(1)}, bf16[128,512]{1,0:T(8,128)(2,1)S(1)}, u32[]{:S(2)}, u32[]{:S(2)}) %collective-permute-start.15) | collective-permute-done | bytes 131104 | tf_op jit(solution)/shard_map/ppermute | solution.py:593
  75.2 8.1 %update_nodes.1 = (bf16[15,512,128]{2,1,0:T(8,128)(2,1)S(1)}, bf16[15,512,128]{2,1,0:T(8,128)(2,1)S(1)}, bf16[128,512]{1,0:T(8,128)(2,1)S(1)}, bf16[512,640]{1,0...) custom-call(bf16[15,192,128]{2,1,0:T(8,128)(2,1)S(1)} %get-tuple-ele, ...), custom_call_target="tpu_custom_call" | custom-call | bytes 10264064 | tf_op jit(solution)/shard_map/update_nodes/pallas_call | solution.py:579
  85.1 3.2 %collective-permute-start.25 = (bf16[128,512]{1,0:T(8,128)(2,1)S(1)}, bf16[128,512]{1,0:T(8,128)(2,1)S(1)}, u32[]{:S(2)}, u32[]{:S(2)}) collective-permute-start(bf16[128,512]{1,0:T(8,128)(2,1)S(1)} %get-tuple-element.141), channel_id=1, source_target_pairs={{0,8},{4,12},{8,0},{12,4},{1,9},{5,13},{9,1},{13,5},{2,10},{6,14},... | collective-permute-start | bytes 393224 | tf_op jit(solution)/shard_map/ppermute | solution.py:593
  88.3 4.1 %update_edges.1 = (bf16[15,192,128]{2,1,0:T(8,128)(2,1)}, bf16[15,192,128]{2,1,0:T(8,128)(2,1)S(1)}, bf16[512,128]{1,0:T(8,128)(2,1)S(1)}, bf16[512,128]{1,0:T(8...) custom-call(bf16[15,192,128]{2,1,0:T(8,128)(2,1)S(1)} %bitcast.30, ...), custom_call_target="tpu_custom_call" | custom-call | bytes 10633216 | tf_op jit(solution)/shard_map/update_edges/pallas_call | solution.py:579
  92.4 5.6 %collective-permute-done.25.rest_2_ = bf16[128,512]{1,0:T(8,128)(2,1)S(1)} collective-permute-done((bf16[128,512]{1,0:T(8,128)(2,1)S(1)}, bf16[128,512]{1,0:T(8,128)(2,1)S(1)}, u32[]{:S(2)}, u32[]{:S(2)}) %collective-permute-start.25) | collective-permute-done | bytes 131104 | tf_op jit(solution)/shard_map/ppermute | solution.py:593
  116.2 3.6 %collective-permute-done.32.t3 = bf16[128,512]{1,0:T(8,128)(2,1)S(1)} collective-permute-done((bf16[128,512]{1,0:T(8,128)(2,1)S(1)}, bf16[128,512]{1,0:T(8,128)(2,1)S(1)}, u32[]{:S(2)}, u32[]{:S(2)}) %collective-permute-start.32) | collective-permute-done | bytes 131104 | tf_op jit(solution)/shard_map/ppermute | solution.py:593
  122.1 3.2 %message_backward.1 = (f32[128,512]{1,0:T(8,128)S(1)}, bf16[128,512]{1,0:T(8,128)(2,1)S(1)}, f32[1,512]{1,0:T(1,128)S(1)}, bf16[15,512,128]{2,1,0:T(8,128)(2,1)S...) custom-call(bf16[128,512]{1,0:T(8,128)(2,1)S(1)} %get-tuple-element., ...), custom_call_target="tpu_custom_call" | custom-call | bytes 7269888 | tf_op jit(solution)/shard_map/message_backward/pallas_call | solution.py:579
  125.3 3.7 %collective-permute-start.37 = (bf16[128,512]{1,0:T(8,128)(2,1)S(1)}, bf16[128,512]{1,0:T(8,128)(2,1)S(1)}, u32[]{:S(2)}, u32[]{:S(2)}) collective-permute-start(bf16[128,512]{1,0:T(8,128)(2,1)S(1)} %get-tuple-element.172), channel_id=1, source_target_pairs={{0,4},{4,0},{8,12},{12,8},{1,5},{5,1},{9,13},{13,9},{2,6},{6,2},{1... | collective-permute-start | bytes 393224 | tf_op jit(solution)/shard_map/ppermute | solution.py:593
  131.9 3.7 %message_edges.1 = (f32[15,192,128]{2,1,0:T(8,128)}, f32[8,256]{1,0:T(8,128)S(1)}, bf16[320,128]{1,0:T(8,128)(2,1)S(1)}, bf16[320,128]{1,0:T(8,128)(2,1)S(1)}, b...) custom-call(bf16[15,192,128]{2,1,0:T(8,128)(2,1)S(1)} %bitcast.31, ...), custom_call_target="tpu_custom_call" | custom-call | bytes 8101888 | tf_op jit(solution)/shard_map/message_edges/pallas_call | solution.py:579
  149.9 4.2 %collective-permute-done.54.p1 = bf16[176,512]{1,0:T(8,128)(2,1)S(1)} collective-permute-done((bf16[176,512]{1,0:T(8,128)(2,1)S(1)}, bf16[176,512]{1,0:T(8,128)(2,1)S(1)}, u32[]{:S(2)}, u32[]{:S(2)}) %collective-permute-start.54) | collective-permute-done | bytes 180256 | tf_op jit(solution)/shard_map/ppermute | solution.py:593
  155.2 2.8 %collective-permute-start.49 = (bf16[480,128]{1,0:T(8,128)(2,1)S(1)}, bf16[480,128]{1,0:T(8,128)(2,1)S(1)}, u32[]{:S(2)}, u32[]{:S(2)}) collective-permute-start(bf16[480,128]{1,0:T(8,128)(2,1)S(1)} %pad_maximum_fusion.rest_0_), channel_id=1, source_target_pairs={{0,12},{4,8},{8,4},{12,0},{1,13},{5,9},{9,5},{13,1},{2,14},{6,10},... | collective-permute-start | bytes 368648 | tf_op jit(solution)/shard_map/ppermute | solution.py:593
  160.7 7.9 %collective-permute-start.52 = (bf16[160,128]{1,0:T(8,128)(2,1)S(1)}, bf16[160,128]{1,0:T(8,128)(2,1)S(1)}, u32[]{:S(2)}, u32[]{:S(2)}) collective-permute-start(bf16[160,128]{1,0:T(8,128)(2,1)S(1)} %get-tuple-element.192.rest_4_), channel_id=1, source_target_pairs={{0,12},{4,8},{8,4},{12,0},{1,13},{5,9},{9,5},{13,1},{2,14},{6,10},... | collective-permute-start | bytes 122888 | tf_op jit(solution)/shard_map/ppermute | solution.py:593
  168.6 4.0 %collective-permute-start.51 = (bf16[160,128]{1,0:T(8,128)(2,1)S(1)}, bf16[160,128]{1,0:T(8,128)(2,1)S(1)}, u32[]{:S(2)}, u32[]{:S(2)}) collective-permute-start(bf16[160,128]{1,0:T(8,128)(2,1)S(1)} %get-tuple-element.192.rest_4_), channel_id=1, source_target_pairs={{0,8},{4,12},{8,0},{12,4},{1,9},{5,13},{9,1},{13,5},{2,10},{6,14},... | collective-permute-start | bytes 122888 | tf_op jit(solution)/shard_map/ppermute | solution.py:593
  176.7 3.4 %collective-permute-start.59 = (bf16[176,512]{1,0:T(8,128)(2,1)S(1)}, bf16[176,512]{1,0:T(8,128)(2,1)S(1)}, u32[]{:S(2)}, u32[]{:S(2)}) collective-permute-start(bf16[176,512]{1,0:T(8,128)(2,1)S(1)} %early_total.1.refs_0_), channel_id=1, source_target_pairs={{0,12},{4,8},{8,4},{12,0},{1,13},{5,9},{9,5},{13,1},{2,14},{6,10},... | collective-permute-start | bytes 540680 | tf_op jit(solution)/shard_map/ppermute | solution.py:593
  182.1 3.9 %collective-permute-done.59.refs_3_ = bf16[176,512]{1,0:T(8,128)(2,1)S(1)} collective-permute-done((bf16[176,512]{1,0:T(8,128)(2,1)S(1)}, bf16[176,512]{1,0:T(8,128)(2,1)S(1)}, u32[]{:S(2)}, u32[]{:S(2)}) %collective-permute-start.59) | collective-permute-done | bytes 180256 | tf_op jit(solution)/shard_map/ppermute | solution.py:593
  186.0 7.7 %collective-permute-done.58.refs_2_ = bf16[176,512]{1,0:T(8,128)(2,1)S(1)} collective-permute-done((bf16[176,512]{1,0:T(8,128)(2,1)S(1)}, bf16[176,512]{1,0:T(8,128)(2,1)S(1)}, u32[]{:S(2)}, u32[]{:S(2)}) %collective-permute-start.58) | collective-permute-done | bytes 180256 | tf_op jit(solution)/shard_map/ppermute | solution.py:593
  (158 shorter events, 89.4 us)
Async XLA Ops:
  2.2 11.1 %collective-permute-start.5 = (bf16[128,1024]{1,0:T(8,128)(2,1)S(1)}, bf16[128,1024]{1,0:T(8,128)(2,1)S(1)}, u32[]{:S(2)}, u32[]{:S(2)}) collective-permute-start(bf16[128,1024]{1,0:T(8,128)(2,1)S(1)} %get-tuple-element.120), channel_id=1, source_target_pairs={{0,3},{1,2},{2,1},{3,0},{4,7},{5,6},{6,5},{7,4},{8,11},{9,10},{10,... | collective-permute-start | bytes 786440 | tf_op jit(solution)/shard_map/ppermute | solution.py:593
  6.1 11.9 %collective-permute-start.4 = (bf16[128,1024]{1,0:T(8,128)(2,1)S(1)}, bf16[128,1024]{1,0:T(8,128)(2,1)S(1)}, u32[]{:S(2)}, u32[]{:S(2)}) collective-permute-start(bf16[128,1024]{1,0:T(8,128)(2,1)S(1)} %get-tuple-element.120), channel_id=1, source_target_pairs={{0,2},{1,3},{2,0},{3,1},{4,6},{5,7},{6,4},{7,5},{8,10},{9,11},{10,... | collective-permute-start | bytes 786440 | tf_op jit(solution)/shard_map/ppermute | solution.py:593
  6.6 11.7 %collective-permute-start.3 = (bf16[128,1024]{1,0:T(8,128)(2,1)S(1)}, bf16[128,1024]{1,0:T(8,128)(2,1)S(1)}, u32[]{:S(2)}, u32[]{:S(2)}) collective-permute-start(bf16[128,1024]{1,0:T(8,128)(2,1)S(1)} %get-tuple-element.120), channel_id=1, source_target_pairs={{0,1},{1,0},{2,3},{3,2},{4,5},{5,4},{6,7},{7,6},{8,9},{9,8},{10,11... | collective-permute-start | bytes 786440 | tf_op jit(solution)/shard_map/ppermute | solution.py:593
  6.8 14.6 %collective-permute-start.2 = (bf16[128,512]{1,0:T(8,128)(2,1)}, bf16[128,512]{1,0:T(8,128)(2,1)S(1)}, u32[]{:S(2)}, u32[]{:S(2)}) collective-permute-start(bf16[128,512]{1,0:T(8,128)(2,1)} %bitcast.35), channel_id=1, source_target_pairs={{0,12},{4,8},{8,4},{12,0},{1,13},{5,9},{9,5},{13,1},{2,14},{6,10},... | collective-permute-start | bytes 393224 | tf_op jit(solution)/shard_map/ppermute | solution.py:593
  13.3 15.2 %collective-permute-start.8 = (bf16[128,1024]{1,0:T(8,128)(2,1)S(1)}, bf16[128,1024]{1,0:T(8,128)(2,1)S(1)}, u32[]{:S(2)}, u32[]{:S(2)}) collective-permute-start(bf16[128,1024]{1,0:T(8,128)(2,1)S(1)} %collective-permute-done.5.rest_6_), channel_id=1, source_target_pairs={{0,16},{16,0},{1,17},{17,1},{2,18},{18,2},{3,19},{19,3},{4,20},{20... | collective-permute-start | bytes 786440 | tf_op jit(solution)/shard_map/ppermute | solution.py:593
  18.1 10.4 %collective-permute-start.7 = (bf16[128,1024]{1,0:T(8,128)(2,1)S(1)}, bf16[128,1024]{1,0:T(8,128)(2,1)S(1)}, u32[]{:S(2)}, u32[]{:S(2)}) collective-permute-start(bf16[128,1024]{1,0:T(8,128)(2,1)S(1)} %collective-permute-done.4.rest_5_), channel_id=1, source_target_pairs={{0,16},{16,0},{1,17},{17,1},{2,18},{18,2},{3,19},{19,3},{4,20},{20... | collective-permute-start | bytes 786440 | tf_op jit(solution)/shard_map/ppermute | solution.py:593
  63.7 11.5 %collective-permute-start.23 = (bf16[128,640]{1,0:T(8,128)(2,1)S(1)}, bf16[128,640]{1,0:T(8,128)(2,1)S(1)}, u32[]{:S(2)}, u32[]{:S(2)}) collective-permute-start(bf16[128,640]{1,0:T(8,128)(2,1)S(1)} %collective-permute-done.20.rest_8_), channel_id=1, source_target_pairs={{0,16},{16,0},{1,17},{17,1},{2,18},{18,2},{3,19},{19,3},{4,20},{20... | collective-permute-start | bytes 491528 | tf_op jit(solution)/shard_map/ppermute | solution.py:593
  85.1 12.8 %collective-permute-start.25 = (bf16[128,512]{1,0:T(8,128)(2,1)S(1)}, bf16[128,512]{1,0:T(8,128)(2,1)S(1)}, u32[]{:S(2)}, u32[]{:S(2)}) collective-permute-start(bf16[128,512]{1,0:T(8,128)(2,1)S(1)} %get-tuple-element.141), channel_id=1, source_target_pairs={{0,8},{4,12},{8,0},{12,4},{1,9},{5,13},{9,1},{13,5},{2,10},{6,14},... | collective-permute-start | bytes 393224 | tf_op jit(solution)/shard_map/ppermute | solution.py:593
  125.3 12.3 %collective-permute-start.37 = (bf16[128,512]{1,0:T(8,128)(2,1)S(1)}, bf16[128,512]{1,0:T(8,128)(2,1)S(1)}, u32[]{:S(2)}, u32[]{:S(2)}) collective-permute-start(bf16[128,512]{1,0:T(8,128)(2,1)S(1)} %get-tuple-element.172), channel_id=1, source_target_pairs={{0,4},{4,0},{8,12},{12,8},{1,5},{5,1},{9,13},{13,9},{2,6},{6,2},{1... | collective-permute-start | bytes 393224 | tf_op jit(solution)/shard_map/ppermute | solution.py:593
  129.0 12.9 %collective-permute-start.38 = (bf16[128,512]{1,0:T(8,128)(2,1)S(1)}, bf16[128,512]{1,0:T(8,128)(2,1)S(1)}, u32[]{:S(2)}, u32[]{:S(2)}) collective-permute-start(bf16[128,512]{1,0:T(8,128)(2,1)S(1)} %get-tuple-element.173), channel_id=1, source_target_pairs={{0,8},{4,12},{8,0},{12,4},{1,9},{5,13},{9,1},{13,5},{2,10},{6,14},... | collective-permute-start | bytes 393224 | tf_op jit(solution)/shard_map/ppermute | solution.py:593
  130.5 11.3 %collective-permute-start.39 = (bf16[128,512]{1,0:T(8,128)(2,1)S(1)}, bf16[128,512]{1,0:T(8,128)(2,1)S(1)}, u32[]{:S(2)}, u32[]{:S(2)}) collective-permute-start(bf16[128,512]{1,0:T(8,128)(2,1)S(1)} %get-tuple-element.174), channel_id=1, source_target_pairs={{0,12},{4,8},{8,4},{12,0},{1,13},{5,9},{9,5},{13,1},{2,14},{6,10},... | collective-permute-start | bytes 393224 | tf_op jit(solution)/shard_map/ppermute | solution.py:593
  143.3 10.8 %collective-permute-start.54 = (bf16[176,512]{1,0:T(8,128)(2,1)S(1)}, bf16[176,512]{1,0:T(8,128)(2,1)S(1)}, u32[]{:S(2)}, u32[]{:S(2)}) collective-permute-start(bf16[176,512]{1,0:T(8,128)(2,1)S(1)} %get-tuple-element.200), channel_id=1, source_target_pairs={{0,4},{4,0},{8,12},{12,8},{1,5},{5,1},{9,13},{13,9},{2,6},{6,2},{1... | collective-permute-start | bytes 540680 | tf_op jit(solution)/shard_map/ppermute | solution.py:593
  144.9 15.7 %collective-permute-start.55 = (bf16[176,512]{1,0:T(8,128)(2,1)S(1)}, bf16[176,512]{1,0:T(8,128)(2,1)S(1)}, u32[]{:S(2)}, u32[]{:S(2)}) collective-permute-start(bf16[176,512]{1,0:T(8,128)(2,1)S(1)} %get-tuple-element.201), channel_id=1, source_target_pairs={{0,8},{4,12},{8,0},{12,4},{1,9},{5,13},{9,1},{13,5},{2,10},{6,14},... | collective-permute-start | bytes 540680 | tf_op jit(solution)/shard_map/ppermute | solution.py:593
  147.6 10.4 %collective-permute-start.41 = (bf16[144,640]{1,0:T(8,128)(2,1)S(1)}, bf16[144,640]{1,0:T(8,128)(2,1)S(1)}, u32[]{:S(2)}, u32[]{:S(2)}) collective-permute-start(bf16[144,640]{1,0:T(8,128)(2,1)S(1)} %get-tuple-element.177), channel_id=1, source_target_pairs={{0,2},{1,3},{2,0},{3,1},{4,6},{5,7},{6,4},{7,5},{8,10},{9,11},{10,... | collective-permute-start | bytes 552968 | tf_op jit(solution)/shard_map/ppermute | solution.py:593
  154.1 14.5 %collective-permute-start.56 = (bf16[176,512]{1,0:T(8,128)(2,1)S(1)}, bf16[176,512]{1,0:T(8,128)(2,1)S(1)}, u32[]{:S(2)}, u32[]{:S(2)}) collective-permute-start(bf16[176,512]{1,0:T(8,128)(2,1)S(1)} %get-tuple-element.202), channel_id=1, source_target_pairs={{0,12},{4,8},{8,4},{12,0},{1,13},{5,9},{9,5},{13,1},{2,14},{6,10},... | collective-permute-start | bytes 540680 | tf_op jit(solution)/shard_map/ppermute | solution.py:593
  155.2 17.4 %collective-permute-start.49 = (bf16[480,128]{1,0:T(8,128)(2,1)S(1)}, bf16[480,128]{1,0:T(8,128)(2,1)S(1)}, u32[]{:S(2)}, u32[]{:S(2)}) collective-permute-start(bf16[480,128]{1,0:T(8,128)(2,1)S(1)} %pad_maximum_fusion.rest_0_), channel_id=1, source_target_pairs={{0,12},{4,8},{8,4},{12,0},{1,13},{5,9},{9,5},{13,1},{2,14},{6,10},... | collective-permute-start | bytes 368648 | tf_op jit(solution)/shard_map/ppermute | solution.py:593
  158.0 18.6 %collective-permute-start.48 = (bf16[480,128]{1,0:T(8,128)(2,1)S(1)}, bf16[480,128]{1,0:T(8,128)(2,1)S(1)}, u32[]{:S(2)}, u32[]{:S(2)}) collective-permute-start(bf16[480,128]{1,0:T(8,128)(2,1)S(1)} %pad_maximum_fusion.rest_0_), channel_id=1, source_target_pairs={{0,8},{4,12},{8,0},{12,4},{1,9},{5,13},{9,1},{13,5},{2,10},{6,14},... | collective-permute-start | bytes 368648 | tf_op jit(solution)/shard_map/ppermute | solution.py:593
  158.0 22.1 %collective-permute-start.47 = (bf16[480,128]{1,0:T(8,128)(2,1)S(1)}, bf16[480,128]{1,0:T(8,128)(2,1)S(1)}, u32[]{:S(2)}, u32[]{:S(2)}) collective-permute-start(bf16[480,128]{1,0:T(8,128)(2,1)S(1)} %pad_maximum_fusion.rest_0_), channel_id=1, source_target_pairs={{0,4},{4,0},{8,12},{12,8},{1,5},{5,1},{9,13},{13,9},{2,6},{6,2},{1... | collective-permute-start | bytes 368648 | tf_op jit(solution)/shard_map/ppermute | solution.py:593
  160.7 19.4 %collective-permute-start.52 = (bf16[160,128]{1,0:T(8,128)(2,1)S(1)}, bf16[160,128]{1,0:T(8,128)(2,1)S(1)}, u32[]{:S(2)}, u32[]{:S(2)}) collective-permute-start(bf16[160,128]{1,0:T(8,128)(2,1)S(1)} %get-tuple-element.192.rest_4_), channel_id=1, source_target_pairs={{0,12},{4,8},{8,4},{12,0},{1,13},{5,9},{9,5},{13,1},{2,14},{6,10},... | collective-permute-start | bytes 122888 | tf_op jit(solution)/shard_map/ppermute | solution.py:593
  168.6 12.5 %collective-permute-start.51 = (bf16[160,128]{1,0:T(8,128)(2,1)S(1)}, bf16[160,128]{1,0:T(8,128)(2,1)S(1)}, u32[]{:S(2)}, u32[]{:S(2)}) collective-permute-start(bf16[160,128]{1,0:T(8,128)(2,1)S(1)} %get-tuple-element.192.rest_4_), channel_id=1, source_target_pairs={{0,8},{4,12},{8,0},{12,4},{1,9},{5,13},{9,1},{13,5},{2,10},{6,14},... | collective-permute-start | bytes 122888 | tf_op jit(solution)/shard_map/ppermute | solution.py:593
  180.1 13.6 %collective-permute-start.58 = (bf16[176,512]{1,0:T(8,128)(2,1)S(1)}, bf16[176,512]{1,0:T(8,128)(2,1)S(1)}, u32[]{:S(2)}, u32[]{:S(2)}) collective-permute-start(bf16[176,512]{1,0:T(8,128)(2,1)S(1)} %early_total.1.refs_0_), channel_id=1, source_target_pairs={{0,8},{4,12},{8,0},{12,4},{1,9},{5,13},{9,1},{13,5},{2,10},{6,14},... | collective-permute-start | bytes 540680 | tf_op jit(solution)/shard_map/ppermute | solution.py:593
  180.1 13.6 %collective-permute-start.57 = (bf16[176,512]{1,0:T(8,128)(2,1)S(1)}, bf16[176,512]{1,0:T(8,128)(2,1)S(1)}, u32[]{:S(2)}, u32[]{:S(2)}) collective-permute-start(bf16[176,512]{1,0:T(8,128)(2,1)S(1)} %early_total.1.refs_0_), channel_id=1, source_target_pairs={{0,4},{4,0},{8,12},{12,8},{1,5},{5,1},{9,13},{13,9},{2,6},{6,2},{1... | collective-permute-start | bytes 540680 | tf_op jit(solution)/shard_map/ppermute | solution.py:593
  181.6 15.6 %collective-permute-start.53 = (bf16[1408,128]{1,0:T(8,128)(2,1)S(1)}, bf16[1408,128]{1,0:T(8,128)(2,1)S(1)}, u32[]{:S(2)}, u32[]{:S(2)}) collective-permute-start(bf16[1408,128]{1,0:T(8,128)(2,1)S(1)} %message_grads.1.mine_ref), channel_id=1, source_target_pairs={{0,16},{16,0},{1,17},{17,1},{2,18},{18,2},{3,19},{19,3},{4,20},{20... | collective-permute-start | bytes 1081352 | tf_op jit(solution)/shard_map/ppermute | solution.py:593
  181.6 12.6 %collective-permute-start.60 = (bf16[176,512]{1,0:T(8,128)(2,1)S(1)}, bf16[176,512]{1,0:T(8,128)(2,1)S(1)}, u32[]{:S(2)}, u32[]{:S(2)}) collective-permute-start(bf16[176,512]{1,0:T(8,128)(2,1)S(1)} %early_total.1.refs_0_), channel_id=1, source_target_pairs={{0,16},{16,0},{1,17},{17,1},{2,18},{18,2},{3,19},{19,3},{4,20},{20... | collective-permute-start | bytes 540680 | tf_op jit(solution)/shard_map/ppermute | solution.py:593
  (56 other events, 473.0 us)

commit v3 on v2

v3 whole, which is shorter than its diff:
```python
import functools

import jax
import jax.numpy as jnp
from jax import lax
from jax.experimental import pallas as pl
from jax.experimental.pallas import tpu as pltpu
from jax.sharding import PartitionSpec as P

EPSILON = 1e-05
F32 = jnp.float32
BF16 = jnp.bfloat16
GELU_A = 0.7978845608028654
GELU_B = 0.044715


def dot(left, right):
    return lax.dot_general(left, right, (((1,), (0,)), ((), ())), preferred_element_type=F32)


def dot_nt(left, right):
    return lax.dot_general(left, right, (((1,), (1,)), ((), ())), preferred_element_type=F32)


def dot_tn(left, right):
    return lax.dot_general(left, right, (((0,), (0,)), ((), ())), preferred_element_type=F32)


def normalize(values, axis=-1):
    centre = values - jnp.mean(values, axis=axis, keepdims=True)
    variance = jnp.mean(centre * centre, axis=axis, keepdims=True)
    scale_inv = lax.rsqrt(variance + EPSILON)
    return centre * scale_inv, scale_inv


def norm_back(grad_hat, normed, scale_inv, axis=-1):
    return scale_inv * (
        grad_hat
        - jnp.mean(grad_hat, axis=axis, keepdims=True)
        - normed * jnp.mean(grad_hat * normed, axis=axis, keepdims=True)
    )


def gelu_both(u):
    poly = GELU_A + (GELU_A * GELU_B) * (u * u)
    half = 0.5 + 0.5 * jnp.tanh(u * poly)
    value = u * half
    return value, half + (value * (1.0 - half)) * (6.0 * poly - 4.0 * GELU_A)


def stack(refs, lo, hi):
    return jnp.concatenate([r[:, lo:hi] for r in refs], axis=0)


def rows_of(refs):
    return refs[0][...] if len(refs) == 1 else jnp.concatenate([r[...] for r in refs], axis=0)


def sum_of(refs, lo=None, hi=None):
    parts = [r[...].astype(F32) if lo is None else r[:, lo:hi].astype(F32) for r in refs]
    while len(parts) > 1:
        parts = [sum(parts[i : i + 2]) if i + 1 < len(parts) else parts[i] for i in range(0, len(parts), 2)]
    return parts[0]


def spread(row, count):
    return jnp.concatenate([row[:, i * 128 : i * 128 + 128] for i in range(count)], axis=0)


def by_core(first, second):
    core = lax.axis_index("dp")
    pl.when(core == 0)(first)
    pl.when(core != 0)(second)


def onehot(idx, total):
    here = lax.broadcasted_iota(jnp.int32, (total, idx.shape[1]), 0)
    return (here == idx).astype(F32).astype(BF16)


CHUNK = 32
GROUP = 8


def groups(slots):
    return [range(at, min(at + GROUP, slots)) for at in range(0, slots, GROUP)]


def lanes(refs):
    return jnp.concatenate([refs[s] for s in range(refs.shape[0])], axis=1)


def edge_prep(
    graph, near, et_ref, nbr_ref, res_ref, ga_ref, gb_ref, na_ref, nb_ref, nc_ref, mix_ref, mask_ref, gains_ref, nodes_ref
):
    slots, side, rows = et_ref.shape
    total = mask_ref.shape[1]
    at_graph, at_mp = lax.axis_index("graph"), lax.axis_index("mp")
    for k in range(graph):
        block = (at_graph ^ k) if near else lax.rem(at_graph + k, graph)
        mask_ref[:, k * rows : (k + 1) * rows] = res_ref[:, pl.ds(pl.multiple_of(block * rows, rows), rows)]
    for i, ref in enumerate((na_ref, nb_ref, nc_ref)):
        nodes_ref[i : i + 1, :] = ref[...]
    for i, ref in enumerate((ga_ref, gb_ref)):
        gains_ref[i] = jnp.broadcast_to(ref[...], (rows, ref.shape[1])).T
    for s in range(slots):
        at = slice(s * rows, (s + 1) * rows)
        hat, _ = normalize(et_ref[s].astype(F32), 0)
        mix_ref[:side, at] = (hat * gains_ref[0]).astype(BF16)
        mix_ref[side + total :, at] = (hat * gains_ref[1]).astype(BF16)
        nbr = nbr_ref[at_mp * slots + s]
        if near:
            idx = ((nbr // rows) ^ at_graph) * rows + lax.rem(nbr, rows)
        else:
            moved = nbr + (total - at_graph * rows)
            idx = jnp.where(moved >= total, moved - total, moved)
        mix_ref[side : side + total, at] = onehot(idx, total)


def node_close(h1_ref, p0, p1, p2, p3, gain_ref, h2_ref, c_ref, out_ref):
    h2 = h1_ref[...] + sum_of((p0, p1, p2, p3))
    h2_ref[...] = h2
    hat, _ = normalize(h2)
    c_ref[...] = (hat * gain_ref[2:3, :]).astype(BF16)
    out_ref[...] = h2.astype(BF16)


def node_backward(
    t0, t1, t2, t3, h2_ref, cot_ref, gain_ref, slope_ref, win_ref, wout_ref,
    dh2_ref, dr_ref, dp_ref, gain_out, share_ref, part_ref,
):
    width = h2_ref.shape[1]
    dc = sum_of((t0, t1, t2, t3), 0, width)
    share_ref[...] = sum_of((t0, t1, t2, t3), width, width + 128).astype(BF16)
    hat, inv = normalize(h2_ref[...])
    gain_out[...] = jnp.sum(dc * hat, axis=0, keepdims=True)
    dh2 = cot_ref[...].astype(F32) + norm_back(dc * gain_ref[2:3, :], hat, inv)
    dh2_ref[...] = dh2
    dr = dh2.astype(BF16)
    dr_ref[...] = dr
    dp = (slope_ref[...].astype(F32) * dot_nt(dr, wout_ref[...])).astype(BF16)
    dp_ref[...] = dp
    part_ref[...] = dot_nt(dp, win_ref[...]).astype(BF16)


def pack_weights(ms, mo, me, mout, us, uo, ue, uout_t, full_ref, half_ref, later_ref):
    wide = ms.shape[0]
    size = half_ref.shape[1]

    def turned(ref):
        return ref[...].astype(F32).T.astype(BF16)

    def filled(parts):
        got = sum(p.shape[1] for p in parts)
        return jnp.concatenate(parts + [jnp.zeros((ms.shape[1], size - got), BF16)], axis=1)

    front = filled([turned(mo), turned(me), turned(ue), turned(uout_t)])
    back = filled([turned(ms), mout[...]])
    full_ref[:, :size] = front
    full_ref[:, size:] = back
    later_ref[:, :wide] = turned(us)
    later_ref[:, wide:] = turned(uo)

    def keep_front():
        half_ref[...] = front

    def keep_back():
        half_ref[...] = back

    by_core(keep_front, keep_back)


def row_prep(parts, *refs):
    node_refs, gain_ref, a_ref = refs[:parts], refs[parts], refs[parts + 1]
    total = a_ref.shape[0]
    block = node_refs[0].shape[0] if parts > 1 else 512
    for at in range(0, total, block):
        ref = node_refs[at // block] if parts > 1 else node_refs[0].at[at : at + block]
        hat, _ = normalize(ref[...].astype(F32))
        a_ref[at : at + block, :] = (hat * gain_ref[0:1, :]).astype(BF16)


def message_forward(
    nbr_scale, slots, mix_ref, mask_ref, a_ref, full_ref, cross_ref, diag_ref, cross_two_ref, diag_two_ref,
    slope_ref, pooled_ref, fronts_ref, backs_ref, lhs_ref, u_ref, ps_ref, acc_ref,
):
    total, width = a_ref.shape
    hidden, rows = ps_ref.shape
    side = (mix_ref.shape[0] - total) // 2
    shard, size = diag_ref.shape

    def place(blocks, front, back):
        for k, ref in enumerate(blocks):
            at = slice(k * shard, (k + 1) * shard)
            fronts_ref[at, :] = ref[:, :size]
            backs_ref[at, :] = ref[:, size:]
        fronts_ref[3 * shard :, :] = front[...]
        backs_ref[3 * shard :, :] = back[...]

    by_core(
        lambda: place((full_ref, cross_ref, cross_two_ref), diag_ref, diag_two_ref),
        lambda: place((full_ref, cross_two_ref, cross_ref), diag_two_ref, diag_ref),
    )
    lhs_ref[:hidden, :side] = fronts_ref[:, width : width + side]
    for at in range(0, total, 512):
        lhs_ref[:hidden, side + at : side + at + 512] = dot_nt(
            fronts_ref[:, :width], a_ref[at : at + 512, :]
        ).astype(BF16)
    top = lax.broadcasted_iota(jnp.int32, (16, total), 0) == 0
    lhs_ref[hidden:, side:] = jnp.where(top, mask_ref[...].astype(F32), 0.0).astype(BF16)
    lhs_ref[hidden:, :side] = jnp.zeros((16, side), BF16)
    ps_ref[...] = dot_nt(backs_ref[:, :width], a_ref[:rows, :])

    def product(group):
        lane = slice(group[0] * rows, (group[-1] + 1) * rows)
        u_ref[:, lane] = dot(lhs_ref[...], mix_ref[: side + total, lane])

    parts = groups(slots)
    product(parts[0])
    for i, group in enumerate(parts):
        if i + 1 < len(parts):
            product(parts[i + 1])
        for low in range(0, hidden, CHUNK):
            at = slice(low, low + CHUNK)
            ps = ps_ref[at, :]
            acc = acc_ref[at, :] if i else None
            for s in group:
                lane = slice(s * rows, (s + 1) * rows)
                z, slope = gelu_both(u_ref[at, lane] + ps)
                mask = u_ref[hidden : hidden + 1, lane]
                z = z * mask
                acc = z if acc is None else acc + z
                slope_ref[at, lane] = (slope * mask).astype(BF16)
            acc_ref[at, :] = acc
    pooled_ref[...] = (acc_ref[...] * nbr_scale).T.astype(BF16)


def node_forward(
    s0, s1, s2, s3, nodes_ref, backs_ref, gain_ref, win_ref, wout_ref, s_ref, h1_ref, b_ref, y_ref, slope_ref, part_ref
):
    width = nodes_ref.shape[1]
    sums = []
    for p in range(4):
        sums.append(sum(
            ref[:, (p ^ k) * 128 : (p ^ k) * 128 + 128].astype(F32) for k, ref in enumerate((s0, s1, s2, s3))
        ).astype(BF16))
    pooled = jnp.concatenate(sums, axis=1)
    s_ref[...] = pooled
    h1 = nodes_ref[...].astype(F32) + dot(pooled, backs_ref[:, width : 2 * width])
    h1_ref[...] = h1
    hat, _ = normalize(h1)
    b = (hat * gain_ref[1:2, :]).astype(BF16)
    b_ref[...] = b
    y, slope = gelu_both(dot(b, win_ref[...]))
    y = y.astype(BF16)
    y_ref[...] = y
    slope_ref[...] = slope.astype(BF16)
    part_ref[...] = dot(y, wout_ref[...]).astype(BF16)


def update_nodes(slots, parts, outs, mix_ref, cot_ref, fronts_ref, *rest):
    node_refs, w_refs = rest[:parts], rest[parts : parts + 4]
    w_ref, dv_ref, r_ref = rest[parts + 4 : parts + 7]
    s_refs = rest[parts + 7 : parts + 7 + outs]
    lhs_ref, v_ref, g_ref, ps_ref, racc_ref = rest[parts + 7 + outs :]
    side, rows = cot_ref.shape[1:]
    total = mix_ref.shape[0] - 2 * side
    width = node_refs[0].shape[1]
    hidden = ps_ref.shape[0]
    other = stack(w_refs, width, 2 * width)
    block = node_refs[0].shape[0] if parts > 1 else 512
    for at in range(0, total, block):
        ref = node_refs[at // block] if parts > 1 else node_refs[0].at[at : at + block]
        lhs_ref[:, at : at + block] = dot_nt(other, ref[...]).astype(BF16)
    lhs_ref[:, total:] = fronts_ref[:, width + side : width + 2 * side]
    wo = fronts_ref[:, width + 2 * side : width + 3 * side]
    ps_ref[...] = dot_nt(stack(w_refs, 0, width), node_refs[0][:rows, :])

    v_all = dot(lhs_ref[...], mix_ref[side:, :])
    g_all = dot(wo, lanes(cot_ref))
    for low in range(0, hidden, CHUNK):
        at = slice(low, low + CHUNK)
        ps = ps_ref[at, :]
        acc = None
        for s in range(slots):
            lane = slice(s * rows, (s + 1) * rows)
            w, slope = gelu_both(v_all[at, lane] + ps)
            w_ref[at, lane] = w.astype(BF16)
            dv = slope * g_all[at, lane]
            acc = dv if acc is None else acc + dv
            dv_ref[at, lane] = dv.astype(BF16)
        racc_ref[at, :] = acc
    r_ref[...] = racc_ref[...].T.astype(BF16)
    back = dot_nt(mix_ref[side : side + total, :], dv_ref[...]).astype(BF16) if total <= 512 else None
    for b, ref in enumerate(s_refs):
        n = ref.shape[0]
        for at in range(0, n, 512):
            m = min(512, n)
            low = b * n + at
            if back is not None:
                ref[at : at + m, :] = back[low : low + m]
            else:
                ref[at : at + m, :] = dot_nt(mix_ref[side + low : side + low + m, :], dv_ref[...]).astype(BF16)


def update_edges(et_ref, w_ref, dv_ref, mix_ref, cot_ref, r_ref, fronts_ref, out_ref, dq_ref, x0, x1, x2, x3):
    slots, side, rows = et_ref.shape
    width = r_ref.shape[1]
    low = mix_ref.shape[0] - side
    ue = fronts_ref[:, width + side : width + 2 * side].astype(F32).T.astype(BF16)
    uo = fronts_ref[:, width + 2 * side : width + 3 * side].astype(F32).T.astype(BF16)
    dq_ref[...] = dot(ue, dv_ref[...]).astype(BF16)
    o_all = dot(uo, w_ref[...])
    for s in range(slots):
        out_ref[s] = (et_ref[s].astype(F32) + o_all[:, s * rows : (s + 1) * rows]).astype(BF16)
    gout = dot_nt(lanes(cot_ref), w_ref[...]).astype(BF16)
    gedge = dot_nt(mix_ref[low:, :], dv_ref[...]).astype(BF16)
    for k, ref in enumerate((x0, x1, x2, x3)):
        at = slice(k * 128, k * 128 + 128)
        ref[:rows, :] = r_ref[:, at]
        ref[rows : rows + side, :] = gedge[:, at]
        ref[rows + side :, :] = gout[:, at]


def update_terms(parts, r_ref, w0, w1, w2, w3, *rest):
    s_refs, outs = rest[:parts], rest[-4:]
    width = r_ref.shape[1]
    total = sum_of(s_refs).astype(BF16)
    ws = (w0, w1, w2, w3)
    term = (dot(r_ref[...], stack(ws, 0, width)) + dot(total, stack(ws, width, 2 * width))).astype(BF16)
    for k, ref in enumerate(outs):
        ref[:, :width] = term
        ref[:, width:] = total[:, k * 128 : k * 128 + 128]


def message_shares(x0, x1, x2, x3, _, r_ref, edge_ref, *s_refs):
    rows = r_ref.shape[0]
    every = sum_of((x0, x1, x2, x3)).astype(BF16)
    n = s_refs[0].shape[0]
    for b, ref in enumerate(s_refs):
        ref[...] = every[b * n : (b + 1) * n]
    low = every.shape[0] - edge_ref.shape[0]
    r_ref[...] = every[low - rows : low]
    edge_ref[...] = every[low:]


def message_terms(parts, r_ref, fronts_ref, backs_ref, nodes_ref, gb_ref, gc_ref, ge_ref, *rest):
    s_refs, (term_ref, share_ref) = rest[:parts], rest[parts:]
    rows, shard = r_ref.shape
    width = nodes_ref.shape[1]
    total = sum_of(s_refs).astype(BF16)
    share_ref[:rows, :] = total
    share_ref[rows:, :] = r_ref[...]
    term = dot(r_ref[...], backs_ref[:shard, :width]) + dot(total, fronts_ref[:shard, :width])
    hat, _ = normalize(nodes_ref[...].astype(F32))
    gain = jnp.sum(term * hat, axis=0, keepdims=True)
    edge = jnp.concatenate([ge_ref[0:2, :], jnp.zeros((2, width - 256), F32)], axis=1)
    gains = [gain, gb_ref[...] * 0.25, gc_ref[...] * 0.25, edge, jnp.zeros((11, width), F32)]
    term_ref[...] = jnp.concatenate([term] + gains, axis=0).astype(BF16)


def early_grads(b_ref, dp_ref, y_ref, dr_ref, c_ref, share_ref, x0, x1, x2, x3, _, __, ___, keep_ref, send_ref):
    rows, width = c_ref.shape
    extra = sum_of((x0, x1, x2, x3)).astype(BF16)
    side = (extra.shape[0] - rows) // 2
    part = (width + side) // 4

    def put(ref, large, small):
        ref[:width, :] = large.astype(BF16)
        small = jnp.concatenate(small, axis=0).astype(BF16)
        ref[width : width + part, :] = jnp.concatenate([small[i * part : (i + 1) * part] for i in range(4)], axis=1)
        ref[width + part :, :] = jnp.zeros_like(ref[width + part :, :])

    def run(one, two):
        put(one, dot_tn(b_ref[...], dp_ref[...]),
            [dot_tn(c_ref[...], extra[:rows]), extra[rows : rows + side].astype(F32)])
        put(two, dot_tn(y_ref[...], dr_ref[...]),
            [dot_tn(c_ref[...], share_ref[...]), extra[rows + side :].astype(F32)])

    by_core(lambda: run(keep_ref, send_ref), lambda: run(send_ref, keep_ref))


def split(total, bit, stay_ref, go_ref):
    half = stay_ref.shape[0]
    own = (lax.axis_index("graph") // bit) % 2

    @pl.when(own == 0)
    def _():
        stay_ref[...] = total[:half]
        go_ref[...] = total[half:]

    @pl.when(own != 0)
    def _():
        stay_ref[...] = total[half:]
        go_ref[...] = total[:half]


def sum_split(bit, one_ref, two_ref, *rest):
    stay_ref, go_ref = rest[-2:]
    split((one_ref[...].astype(F32) + two_ref[...].astype(F32)).astype(BF16), bit, stay_ref, go_ref)


def sum_two(one_ref, two_ref, _, out_ref):
    out_ref[...] = (one_ref[...].astype(F32) + two_ref[...].astype(F32)).astype(BF16)


def join(bit, one, two):
    own = (lax.axis_index("graph") // bit) % 2
    return jnp.where(own == 0, one, two), jnp.where(own == 0, two, one)


def join_two(bit, one_ref, two_ref, _, out_ref):
    half = one_ref.shape[0]
    first, second = join(bit, one_ref[...], two_ref[...])
    out_ref[:half, :] = first
    out_ref[half:, :] = second


def finish_early(bit, m0, m1, t0, t1, gin_ref, gout_ref, self_ref, edge_ref, other_ref, out_ref):
    width, side = gin_ref.shape[0], edge_ref.shape[0]
    part = (width + side) // 4

    def run(one, two):
        for pair, large, top, low in ((one, gin_ref, self_ref, edge_ref), (two, gout_ref, other_ref, out_ref)):
            pair = [r[...] for r in pair]
            if bit:
                clear, full = join(bit, *pair)
                quarter = clear.shape[0] // 2
                pair = [clear[:quarter], full[:quarter], clear[quarter:], full[quarter:]]
            every = jnp.concatenate(pair, axis=0).astype(F32)
            large[...] = every[:width]
            small = jnp.concatenate([every[width : width + part, i * 128 : i * 128 + 128] for i in range(4)], axis=0)
            top[...] = small[:width]
            low[...] = small[width:]

    by_core(lambda: run((m0, m1), (t0, t1)), lambda: run((t0, t1), (m0, m1)))


def message_backward(
    nbr_scale, slots, t0, t1, t2, t3, h1_ref, dh2_ref, gain_ref, backs_ref, slope_ref, mix_ref,
    dh1_ref, dt_ref, gain_out, du_ref, x0, x1, x2, x3, g_ref, racc_ref,
):
    hidden, rows = g_ref.shape
    width = h1_ref.shape[1]
    side = mix_ref.shape[0] - x0.shape[0] + rows
    total = x0.shape[0] - rows - side
    db = sum_of((t0, t1, t2, t3))
    hat, inv = normalize(h1_ref[...])
    gain_out[...] = jnp.sum(db * hat, axis=0, keepdims=True)
    dh1 = dh2_ref[...] + norm_back(db * gain_ref[1:2, :], hat, inv)
    dh1_ref[...] = dh1
    dt = dh1.astype(BF16)
    dt_ref[...] = dt
    g_ref[...] = dot_nt(backs_ref[:, width : 2 * width], dt) * nbr_scale
    for low in range(0, hidden, CHUNK):
        at = slice(low, low + CHUNK)
        g = g_ref[at, :]
        acc = None
        for s in range(slots):
            lane = slice(s * rows, (s + 1) * rows)
            du = slope_ref[at, lane].astype(F32) * g
            acc = du if acc is None else acc + du
            du_ref[at, lane] = du.astype(BF16)
        racc_ref[at, :] = acc
    for low in range(0, total, 512):
        back = dot_nt(mix_ref[side + low : side + low + 512, :], du_ref[...]).astype(BF16)
        for k, ref in enumerate((x0, x1, x2, x3)):
            ref[low : low + 512, :] = back[:, k * 128 : k * 128 + 128]
    gedge = dot_nt(mix_ref[:side, :], du_ref[...]).astype(BF16)
    for k, ref in enumerate((x0, x1, x2, x3)):
        ref[total : total + rows, :] = racc_ref[k * 128 : k * 128 + 128, :].T.astype(BF16)
        ref[total + rows :, :] = gedge[:, k * 128 : k * 128 + 128]


def message_edges(
    et_ref, du_ref, dq_ref, cot_ref, gains_ref, fronts_ref, out_ref, ge_ref, ga_ref, gb_ref
):
    slots, side, rows = et_ref.shape
    width = fronts_ref.shape[0]
    we = fronts_ref[:, width : width + side].astype(F32).T.astype(BF16)
    df_all = dot(we, du_ref[...])
    ga_ref[...] = jnp.zeros_like(ga_ref)
    gb_ref[...] = jnp.zeros_like(gb_ref)
    for s in range(slots):
        df = df_all[:, s * rows : (s + 1) * rows]
        dq = dq_ref[:, s * rows : (s + 1) * rows].astype(F32)
        hat, inv = normalize(et_ref[s].astype(F32), 0)
        ga_ref[...] += df * hat
        gb_ref[...] += dq * hat
        out_ref[s] = cot_ref[s].astype(F32) + norm_back(gains_ref[0] * df + gains_ref[1] * dq, hat, inv, 0)
    lane = lax.broadcasted_iota(jnp.int32, (side, 256), 1)
    row = lax.broadcasted_iota(jnp.int32, (side, 256), 0)

    def laid(ref):
        column = jnp.sum(ref[...], axis=1, keepdims=True)
        return jnp.sum(jnp.where(row == lane, column, 0.0), axis=0, keepdims=True)

    ge_ref[...] = jnp.concatenate([laid(ga_ref), laid(gb_ref), jnp.zeros((6, 256), F32)], axis=0)


def late_grads(edge_ref, s_ref, dt_ref, keep_ref, send_ref):
    rows, width = dt_ref.shape
    gout = dot_tn(s_ref[...], dt_ref[...])
    pieces = [edge_ref[...].astype(F32)] + [gout[:, i * 128 : i * 128 + 128] for i in range(width // 128)]
    every = jnp.concatenate(pieces, axis=0).astype(BF16)
    half = keep_ref.shape[0]

    def put(one, two):
        one[...] = every[:half]
        two[...] = every[half:]

    by_core(lambda: put(keep_ref, send_ref), lambda: put(send_ref, keep_ref))


def node_finish(t0, t1, t2, t3, nodes_ref, dh1_ref, gain_ref, keep_ref, got_ref, out_ref, late_ref):
    rows, width = dh1_ref.shape
    half = keep_ref.shape[0]
    every = sum_of((t0, t1, t2, t3))
    hat, inv = normalize(nodes_ref[...].astype(F32))
    out_ref[...] = dh1_ref[...] + norm_back(every[:rows] * gain_ref[0:1, :], hat, inv)
    late_ref[:half, :] = (keep_ref[...].astype(F32) + got_ref[...].astype(F32)).astype(BF16)
    late_ref[half:, :] = jnp.concatenate(
        [every[rows : rows + 8, i * 128 : i * 128 + 128] for i in range(width // 128)], axis=0
    ).astype(BF16)


def message_grads(parts, a_ref, *rest):
    shares, lates, out_ref = rest[:parts], rest[parts : 2 * parts], rest[-1]
    rows = a_ref.shape[0] // parts
    width = a_ref.shape[1]
    both = jnp.concatenate(
        [jnp.concatenate([r[:rows, :], r[rows:, :]], axis=1) for r in shares], axis=0
    )
    grad = dot_tn(a_ref[...], both).astype(BF16)
    out_ref[:width, :] = grad[:, :128]
    out_ref[width : 2 * width, :] = grad[:, 128:]
    out_ref[2 * width :, :] = sum(r[...].astype(F32) for r in lates).astype(BF16)


def finish_late(
    mine_ref, theirs_ref, other_ref, self_ref, edge_ref, out_ref, ga_ref, gb_ref, gc_ref, gea_ref, geb_ref
):
    width, side = other_ref.shape[0], edge_ref.shape[0]
    rows = out_ref.shape[0]
    other_ref[...] = mine_ref[:width, :].astype(F32) + theirs_ref[:width, :].astype(F32)
    self_ref[...] = mine_ref[width : 2 * width, :].astype(F32) + theirs_ref[width : 2 * width, :].astype(F32)
    low = mine_ref.shape[0] - 8 * (width // 128)
    gains = mine_ref[low:, :].astype(F32) + theirs_ref[low:, :].astype(F32)
    for i, ref in enumerate((ga_ref, gb_ref, gc_ref)):
        ref[...] = jnp.concatenate([gains[8 * j + i : 8 * j + i + 1] for j in range(width // 128)], axis=1)
    for i, ref in ((3, gea_ref), (4, geb_ref)):
        ref[...] = jnp.concatenate([gains[i : i + 1], gains[8 + i : 9 + i]], axis=1)[:, :side]

    def run(first, second):
        every = jnp.concatenate([first[2 * width : low, :], second[2 * width : low, :]], axis=0).astype(F32)
        edge_ref[...] = every[:side]
        out_ref[...] = jnp.concatenate(
            [every[side + i * rows : side + (i + 1) * rows] for i in range(width // 128)], axis=1
        )

    by_core(lambda: run(mine_ref, theirs_ref), lambda: run(theirs_ref, mine_ref))


def whole(shape):
    zeros = (0,) * len(shape)
    return pl.BlockSpec(tuple(shape), lambda i: zeros)


def in_bytes(shape, dtype):
    n = jnp.dtype(dtype).itemsize
    for d in shape:
        n *= d
    return n


AFTER = pl.BlockSpec(memory_space=pl.ANY)


def call(name, body, grid, ins, outs, scratch=(), vmem=24, heavy=False):
    ins = [a if isinstance(a, tuple) else (a, whole(a.shape)) for a in ins]
    outs = [o if len(o) == 3 else o + (whole(o[0]),) for o in outs]
    moved = sum(in_bytes(a.shape, a.dtype) for a, _ in ins) + sum(in_bytes(sh, t) for sh, t, _ in outs)
    return pl.pallas_call(
        body,
        grid=(grid,),
        in_specs=[s for _, s in ins],
        out_specs=[s for _, _, s in outs],
        out_shape=[jax.ShapeDtypeStruct(sh, t) for sh, t, _ in outs],
        scratch_shapes=list(scratch),
        compiler_params=pltpu.CompilerParams(vmem_limit_bytes=vmem << 20, dimension_semantics=("arbitrary",)),
        cost_estimate=pl.CostEstimate(flops=2 * 10**10 if heavy else 0, bytes_accessed=moved, transcendentals=0),
        name=name,
    )(*[a for a, _ in ins])


def far_in(values):
    return pltpu.with_memory_space_constraint(values, pltpu.HBM)


def swap(values, axis, bits, size):
    return lax.ppermute(values, axis, [(i, i ^ bits) for i in range(size)])


def partners(values, axis, size):
    return [values] + [swap(values, axis, k, size) for k in range(1, size)]


def deal(pieces, axis, size):
    return [pieces[0]] + [swap(pieces[k], axis, k, size) for k in range(1, size)]


def turn(values, start, axis):
    return lax.dynamic_slice_in_dim(
        jnp.concatenate([values, values], axis=axis), start, values.shape[axis], axis=axis
    )


def after(values, *others):
    return lax.optimization_barrier((values,) + others)[0]


def local(sizes, *args):
    (
        nodes, edges, neighbours, resmask, node_gain_a, edge_gain_a, message_self, message_other, message_edge,
        message_out, node_gain_b, ffn_in, ffn_out, node_gain_c, edge_gain_b, update_self, update_other, update_edge,
        update_out, node_cot, edge_cot,
    ) = args
    cores, graph, mp = sizes
    near = graph <= 4
    at_graph = None if near else lax.axis_index("graph")
    _, rows, width = nodes.shape
    slots, side = edges.shape[2:]
    nbrs = neighbours.shape[2]
    total = resmask.shape[1]
    shard = message_self.shape[1]
    hidden = shard * mp
    ff = ffn_in.shape[1]
    vmem = 20 if total <= 1024 else 60
    run = functools.partial(call, vmem=vmem)

    def gather_rows(values):
        if near:
            return partners(values, "graph", graph)
        return [turn(lax.all_gather(values, "graph", axis=0, tiled=True), at_graph * rows, 0)]

    def return_rows(blocks):
        if near:
            return deal(blocks, "graph", graph)
        placed = turn(blocks[0], total - at_graph * rows, 0)
        return [lax.psum_scatter(placed, "graph", scatter_dimension=0, tiled=True)]

    blocks = [((rows, hidden), BF16)] * graph if near else [((total, hidden), BF16)]
    outs = len(blocks)
    node, cot_n = nodes[0], node_cot[0]

    nodes_all = gather_rows(node)
    et = jnp.transpose(edges[0], (1, 2, 0))
    cot = jnp.transpose(edge_cot[0], (1, 2, 0))
    edge_sh, hid_sh = (slots, side, rows), (hidden, slots * rows)

    mix, mask_row, gains_e, gains_n = run(
        "edge_prep", functools.partial(edge_prep, graph, near), 1,
        [
            far_in(v) for v in (
                et, jnp.transpose(neighbours, (2, 0, 1)), resmask, edge_gain_a[None, :], edge_gain_b[None, :],
                node_gain_a[None, :], node_gain_b[None, :], node_gain_c[None, :],
            )
        ],
        [((2 * side + total, slots * rows), BF16), ((1, total), jnp.int32), ((2, side, rows), F32), ((8, width), F32)],
    )
    full, half, later = run(
        "pack_weights", pack_weights, 1,
        [far_in(w) for w in (
            message_self, message_other, message_edge, message_out, update_self, update_other, update_edge, update_out.T
        )],
        [((shard, 2 * width + 2 * 640), BF16), ((shard, width + 640), BF16), ((shard, 2 * width), BF16)],
    )
    cross = lax.ppermute(full, ("dp", "mp"), [(c * mp + m, c * mp + (m ^ (1 + c))) for c in range(2) for m in range(mp)])
    diag = swap(half, "mp", 3, mp)
    (a_all,) = run(
        "row_prep", functools.partial(row_prep, len(nodes_all)), 1, nodes_all + [gains_n], [((total, width), BF16)],
    )
    cross, diag = after(cross, a_all), after(diag, a_all)
    slope_m, pooled_part, fronts, backs = run(
        "message_forward", functools.partial(message_forward, 1.0 / nbrs, slots), 1,
        [mix, mask_row, a_all, full, cross, diag, swap(cross, "dp", 1, cores), swap(diag, "dp", 1, cores)],
        [(hid_sh, BF16), ((rows, hidden), BF16), ((hidden, width + 640), BF16), ((hidden, width + 640), BF16)],
        [pltpu.VMEM((hidden + 16, total + side), BF16), pltpu.VMEM((hidden + 16, slots * rows), F32),
         pltpu.VMEM((hidden, rows), F32), pltpu.VMEM((hidden, rows), F32)], heavy=True,
    )

    pooled, h1, b, y, slope_f, h2_part = run(
        "node_forward", node_forward, 1,
        partners(pooled_part, "mp", mp) + [node, backs, gains_n, ffn_in, ffn_out],
        [((rows, hidden), BF16), ((rows, width), F32), ((rows, width), BF16), ((rows, ff), BF16), ((rows, ff), BF16),
         ((rows, width), BF16)],
    )
    h2, c_own, nodes_out = run(
        "node_close", node_close, 1, [h1] + partners(h2_part, "mp", mp) + [gains_n],
        [((rows, width), F32), ((rows, width), BF16), ((rows, width), BF16)],
    )
    c_all = gather_rows(c_own)

    wl = partners(after(later, c_own), "mp", mp)
    w_act, dv, r_upd, *s_upd = run(
        "update_nodes", functools.partial(update_nodes, slots, len(c_all), outs), 1,
        [mix, cot, fronts] + c_all + wl,
        [(hid_sh, BF16), (hid_sh, BF16), ((rows, hidden), BF16)] + blocks,
        [pltpu.VMEM((hidden, total + side), BF16), pltpu.VMEM(hid_sh, F32), pltpu.VMEM(hid_sh, F32),
         pltpu.VMEM((hidden, rows), F32), pltpu.VMEM((hidden, rows), F32)], heavy=True,
    )
    s_upd_parts = return_rows(s_upd)
    eo, dq, *extra = run(
        "update_edges", update_edges, 1, [et, w_act, dv, mix, cot, r_upd, fronts],
        [(edge_sh, BF16), ((side, slots * rows), BF16)] + [((rows + 2 * side, shard), BF16)] * mp,
    )
    edges_out = jnp.transpose(eo, (2, 0, 1))[None]
    order = extra[0]
    extra = deal(extra, "mp", mp)

    terms = run(
        "update_terms", functools.partial(update_terms, outs), 1, [r_upd] + wl + s_upd_parts + [(order, AFTER)],
        [((rows, width + shard), BF16)] * mp,
    )
    dh2, dr, dp_ffn, gain_c, share, db_part = run(
        "node_backward", node_backward, 1, deal(terms, "mp", mp) + [h2, cot_n, gains_n, slope_f, ffn_in, ffn_out],
        [((rows, width), F32), ((rows, width), BF16), ((rows, ff), BF16), ((1, width), F32), ((rows, shard), BF16),
         ((rows, width), BF16)],
    )
    db_parts = partners(db_part, "mp", mp)

    size = (width + (width + side) // 4 + 63) // 64 * 64
    keep, send = run(
        "early_grads", early_grads, 1, [b, dp_ffn, y, dr, c_own, share] + extra + [(v, AFTER) for v in db_parts[1:]], [((size, ff), BF16)] * 2,
    )
    got = swap(send, "dp", 1, cores)
    halves, quarters = [((size // 2, ff), BF16)], [((size // 4, ff), BF16)]

    dh1, dt, gain_b, du, *shares = run(
        "message_backward", functools.partial(message_backward, 1.0 / nbrs, slots), 1,
        db_parts + [h1, dh2, gains_n, backs, slope_m, mix],
        [((rows, width), F32), ((rows, width), BF16), ((1, width), F32), (hid_sh, BF16)]
        + [((total + rows + side, shard), BF16)] * mp,
        [pltpu.VMEM((hidden, rows), F32), pltpu.VMEM((hidden, rows), F32)], heavy=True,
    )
    if near:
        stay, go = run("early_one", functools.partial(sum_split, 2), 1, [keep, got, (gain_b, AFTER)], halves * 2)
        go = swap(go, "graph", 2, graph)
    shares = deal(shares, "mp", mp)
    ge, gains_edge = run(
        "message_edges", message_edges, 1, [et, du, dq, cot, gains_e, fronts], [(edge_sh, F32), ((8, 256), F32)],
        [pltpu.VMEM((side, rows), F32), pltpu.VMEM((side, rows), F32)],
    )
    grad_edges = jnp.transpose(ge, (2, 0, 1))[None]

    share_r, grad_edge, *share_s = run(
        "message_shares", message_shares, 1, shares + [(gains_edge, AFTER)],
        [((rows, shard), BF16), ((side, shard), BF16)] + [(sh[:1] + (shard,), t) for sh, t in blocks],
    )
    if near:
        stay, go = run("early_two", functools.partial(sum_split, 1), 1, [stay, go, (share_r, AFTER)], quarters * 2)
        go = swap(go, "graph", 1, graph)
    term, share = run(
        "message_terms", functools.partial(message_terms, outs), 1,
        [share_r, fronts, backs, node, gain_b, gain_c, gains_edge] + return_rows(share_s),
        [((rows + 16, width), BF16), ((2 * rows, shard), BF16)],
    )
    if near:
        (own,) = run("early_three", sum_two, 1, [stay, go, (term, AFTER)], quarters)
        go = swap(own, "graph", 2, graph)
    half = (side + width) // 2
    keep_late, send_late = run(
        "late_grads", late_grads, 1,
        [grad_edge, (pooled, pl.BlockSpec((rows, shard), lambda i: (0, 0))), dt], [((half, shard), BF16)] * 2,
    )
    grad_nodes, late = run(
        "node_finish", node_finish, 1,
        partners(term, "mp", mp) + [node, dh1, gains_n, keep_late, swap(send_late, "dp", 1, cores)],
        [((rows, width), F32), ((half + width // 16, shard), BF16)],
    )
    if near:
        (own,) = run("early_four", functools.partial(join_two, 2), 1, [own, go, (late, AFTER)], halves)
        early_sum = [own, swap(own, "graph", 1, graph)]
        share, late = partners(share, "graph", graph), partners(late, "graph", graph)
    else:
        early = lax.psum(keep.astype(F32) + got.astype(F32), "graph").astype(BF16)
        early_sum = [early[: size // 2], early[size // 2 :]]
        share, late = [share], [late]
    parts = len(share)
    (part,) = run(
        "message_grads", functools.partial(message_grads, parts), 1,
        [(a_all, pl.BlockSpec((parts * rows, width), lambda i: (0, 0)))] + share + late,
        [((2 * width + half + width // 16, shard), BF16)],
    )
    if not near:
        part = lax.psum(part, "graph")
    grad_mo, grad_ms, grad_me, grad_mout, gain_a, gain_b, gain_c, gain_ea, gain_eb = run(
        "finish_late", finish_late, 1, [part, swap(part, "dp", 1, cores)],
        [((width, shard), F32), ((width, shard), F32), ((side, shard), F32), ((shard, width), F32), ((1, width), F32),
         ((1, width), F32), ((1, width), F32), ((1, side), F32), ((1, side), F32)],
    )
    grad_in, grad_out, grad_us, grad_ue, grad_uo, grad_uout = run(
        "finish_early", functools.partial(finish_early, 1 if near else 0), 1, early_sum + [swap(v, "dp", 1, cores) for v in early_sum],
        [((width, ff), F32), ((ff, width), F32), ((width, shard), F32), ((side, shard), F32), ((width, shard), F32),
         ((side, shard), F32)],
    )
    return (
        nodes_out[None],
        edges_out,
        grad_nodes[None],
        grad_edges,
        gain_a[0],
        gain_ea[0],
        grad_ms,
        grad_mo,
        grad_me,
        grad_mout,
        gain_b[0],
        grad_in,
        grad_out,
        gain_c[0],
        gain_eb[0],
        grad_us,
        grad_uo,
        grad_ue,
        grad_uout.T,
    )


def solution(mesh):
    sizes = (mesh.shape["dp"], mesh.shape["graph"], mesh.shape["mp"])
    rows = P("dp", "graph", None)
    slots = P("dp", "graph", "mp", None)
    cols, tops = P(None, "mp"), P("mp", None)
    return jax.shard_map(
        functools.partial(local, sizes),
        mesh=mesh,
        in_specs=(
            rows, slots, rows, P("dp", None), P(), P(), cols, cols, cols, tops, P(), cols, tops, P(), P(), cols, cols,
            cols, tops, rows, slots,
        ),
        out_specs=(
            rows, slots, rows, slots, P(), P(), cols, cols, cols, tops, P(), cols, tops, P(), P(), cols, cols, cols,
            tops,
        ),
        check_vma=False,
    )
```

time: 199 us -> 172 us (0.86)
  starting transfers between devices: 92.2 us -> 67.1 us
  waiting for transfers between devices: 62.4 us -> 72.1 us
  Pallas kernels: 37 us -> 30.4 us
  local copies, waits for them, and re-layouts: 5.53 us -> 0.93 us
    ppermute x64 -> x54, starting transfers between devices: 92.2 us -> 64.1 us  [swap(): return lax.ppermute(values, axis, [(i, i ^ bits) for i in range(size)])]
    ppermute x64 -> x54, waiting for transfers between devices: 62.4 us -> 72.1 us  [swap(): return lax.ppermute(values, axis, [(i, i ^ bits) for i in range(size)])]
    pallas_call x20 -> x24, Pallas kernels: 37 us -> 30.4 us  [call(): pl.pallas_call(body, grid=(grid,), in_specs=[s for _, s in ins], out_spec...]
    unnamed x32 -> x14, local copies, waits for them, and re-layouts: 5.53 us -> 0.93 us
    ppermute x0 -> x1, starting transfers between devices: none -> 3 us  [local(): lax.ppermute(full, ('dp', 'mp'), [(c * mp + m, c * mp + (m ^ 1 + c)) for...]
  transfers between devices with their start and end apart: 64 -> 55, of which waited for: 27 -> 31; matrix products, arithmetic and copies ran while one was open for 0% -> 0% of each run, Pallas kernels for 7% -> 9%
where the time goes in v3:
time: 172 us; the launch traced here: 171 us
  waiting for transfers between devices  72.1 us (42%)
  starting transfers between devices  67.1 us (39%)
  Pallas kernels  30.4 us (18%)
    ppermute x54, waiting for transfers between devices, swap(): return lax.ppermute(values, axis, [(i, i ^ bits) for i in range(size)])  72.1 us
    ppermute x54, starting transfers between devices, swap(): return lax.ppermute(values, axis, [(i, i ^ bits) for i in range(size)])  64.1 us
    pallas_call x24, Pallas kernels, call(): pl.pallas_call(body, grid=(grid,), in_specs=[s for _, s in ins], out_spec...  30.4 us
  transfers between devices with their start and end apart: 55, of which 31 were waited for; matrix products, arithmetic and copies ran while one was open for 0% of the time, Pallas kernels for 9%

profile of v3, /device:TPU:0, one launch (start us, length us, event | category | flops | bytes accessed | tf_op | source)
XLA Modules:
  0.0 171.5 jit_solution(13761524629370383640)
XLA Ops:
  2.2 3.0 %collective-permute-start.3 = (bf16[128,2304]{1,0:T(8,128)(2,1)S(1)}, bf16[128,2304]{1,0:T(8,128)(2,1)S(1)}, u32[]{:S(2)}, u32[]{:S(2)}) collective-permute-start(bf16[128,2304]{1,0:T(8,128)(2,1)S(1)} %get-tuple-element.111.full_ref), channel_id=1, source_target_pairs={{0,1},{1,0},{2,3},{3,2},{16,18},{17,19},{18,16},{19,17},{4,5},{5,4... | collective-permute-start | bytes 1769480 | tf_op jit(solution)/shard_map/ppermute | solution.py:678
  5.2 3.6 %collective-permute-start.2 = (bf16[128,512]{1,0:T(8,128)(2,1)}, bf16[128,512]{1,0:T(8,128)(2,1)S(1)}, u32[]{:S(2)}, u32[]{:S(2)}) collective-permute-start(bf16[128,512]{1,0:T(8,128)(2,1)} %bitcast.35), channel_id=1, source_target_pairs={{0,12},{4,8},{8,4},{12,0},{1,13},{5,9},{9,5},{13,1},{2,14},{6,10},... | collective-permute-start | bytes 393224 | tf_op jit(solution)/shard_map/ppermute | solution.py:601
  11.1 2.6 %edge_prep.1 = (bf16[896,1920]{1,0:T(8,128)(2,1)S(1)}, s32[1,512]{1,0:T(1,128)S(1)}, f32[2,192,128]{2,1,0:T(8,128)S(1)}, f32[8,512]{1,0:T(8,128)S(1)}) custom-call(bf16[15,192,128]{2,1,0:T(8,128)(2,1)} %bitcast.29, s32[60,1,128]{2,1,0:T(1,128)} %bitcast.44, s32[1,512]{1,0:T(1,128)} %res_ref.1, f32[1,192]{1,0:T(1,128)} %bitcast.48, f32[1,192]{1,0:T(1,128)} %bitcast.49, ...), custom_call_target="tpu_custom_call" | custom-call | bytes 4433408 | tf_op jit(solution)/shard_map/edge_prep/pallas_call | solution.py:583
  13.8 6.1 %collective-permute-done.1.refs_2_ = bf16[128,512]{1,0:T(8,128)(2,1)S(1)} collective-permute-done((bf16[128,512]{1,0:T(8,128)(2,1)}, bf16[128,512]{1,0:T(8,128)(2,1)S(1)}, u32[]{:S(2)}, u32[]{:S(2)}) %collective-permute-start.1) | collective-permute-done | bytes 131104 | tf_op jit(solution)/shard_map/ppermute | solution.py:601
  23.7 3.9 %message_forward.1 = (bf16[512,1920]{1,0:T(8,128)(2,1)S(1)}, bf16[128,512]{1,0:T(8,128)(2,1)S(1)}, bf16[512,1152]{1,0:T(8,128)(2,1)S(1)}, bf16[512,1152]{1,0:T(8,128)(2,1)S(1)}) custom-call(bf16[896,1920]{1,0:T(8,128)(2,1)S(1)} %get-tuple-element.108.mix_ref, s32[1,512]{1,0:T(1,128)S(1)} %get-tuple-element.109.mask_ref, bf16[512,512]{1,0:T(8,128)(2,1)S(1)} %row_prep.1.a_ref, ...), custom_call_target="tpu_custom_call" | custom-call | flops 20000000000 | bytes 10782720 | tf_op jit(solution)/shard_map/message_forward/pallas_call | solution.py:583
  31.1 3.8 %collective-permute-done.9.s3 = bf16[128,512]{1,0:T(8,128)(2,1)S(1)} collective-permute-done((bf16[128,512]{1,0:T(8,128)(2,1)S(1)}, bf16[128,512]{1,0:T(8,128)(2,1)S(1)}, u32[]{:S(2)}, u32[]{:S(2)}) %collective-permute-start.9) | collective-permute-done | bytes 131104 | tf_op jit(solution)/shard_map/ppermute | solution.py:601
  41.3 3.8 %collective-permute-done.12.p3 = bf16[128,512]{1,0:T(8,128)(2,1)S(1)} collective-permute-done((bf16[128,512]{1,0:T(8,128)(2,1)S(1)}, bf16[128,512]{1,0:T(8,128)(2,1)S(1)}, u32[]{:S(2)}, u32[]{:S(2)}) %collective-permute-start.12) | collective-permute-done | bytes 131104 | tf_op jit(solution)/shard_map/ppermute | solution.py:601
  47.6 2.5 %collective-permute-start.15 = (bf16[128,512]{1,0:T(8,128)(2,1)S(1)}, bf16[128,512]{1,0:T(8,128)(2,1)S(1)}, u32[]{:S(2)}, u32[]{:S(2)}) collective-permute-start(bf16[128,512]{1,0:T(8,128)(2,1)S(1)} %get-tuple-element.121.rest_0_.c_ref), channel_id=1, source_target_pairs={{0,12},{4,8},{8,4},{12,0},{1,13},{5,9},{9,5},{13,1},{2,14},{6,10},... | collective-permute-start | bytes 393224 | tf_op jit(solution)/shard_map/ppermute | solution.py:601
  55.0 4.4 %collective-permute-start.13 = (bf16[128,512]{1,0:T(8,128)(2,1)S(1)}, bf16[128,512]{1,0:T(8,128)(2,1)S(1)}, u32[]{:S(2)}, u32[]{:S(2)}) collective-permute-start(bf16[128,512]{1,0:T(8,128)(2,1)S(1)} %get-tuple-element.121.rest_0_.c_ref), channel_id=1, source_target_pairs={{0,4},{4,0},{8,12},{12,8},{1,5},{5,1},{9,13},{13,9},{2,6},{6,2},{1... | collective-permute-start | bytes 393224 | tf_op jit(solution)/shard_map/ppermute | solution.py:601
  64.6 4.9 %update_nodes.1 = (bf16[512,1920]{1,0:T(8,128)(2,1)S(1)}, bf16[512,1920]{1,0:T(8,128)(2,1)S(1)}, bf16[128,512]{1,0:T(8,128)(2,1)S(1)}, bf16[128,512]{1,0:T(8,128...) custom-call(bf16[896,1920]{1,0:T(8,128)(2,1)S(1)} %get-tuple-element.108.mix_re, ...), custom_call_target="tpu_custom_call" | custom-call | flops 20000000000 | bytes 11517952 | tf_op jit(solution)/shard_map/update_nodes/pallas_call | solution.py:583
  71.5 2.5 %collective-permute-start.21 = (bf16[128,512]{1,0:T(8,128)(2,1)S(1)}, bf16[128,512]{1,0:T(8,128)(2,1)S(1)}, u32[]{:S(2)}, u32[]{:S(2)}) collective-permute-start(bf16[128,512]{1,0:T(8,128)(2,1)S(1)} %get-tuple-element.131), channel_id=1, source_target_pairs={{0,12},{4,8},{8,4},{12,0},{1,13},{5,9},{9,5},{13,1},{2,14},{6,10},... | collective-permute-start | bytes 393224 | tf_op jit(solution)/shard_map/ppermute | solution.py:601
  74.0 2.5 %update_edges.1 = (bf16[15,192,128]{2,1,0:T(8,128)(2,1)}, bf16[192,1920]{1,0:T(8,128)(2,1)S(1)}, bf16[512,128]{1,0:T(8,128)(2,1)S(1)}, bf16[512,128]{1,0:T(8,128...) custom-call(bf16[15,192,128]{2,1,0:T(8,128)(2,1)S(1)} %bitcast.30, ...), custom_call_target="tpu_custom_call" | custom-call | bytes 12156928 | tf_op jit(solution)/shard_map/update_edges/pallas_call | solution.py:583
  77.0 5.6 %collective-permute-done.20.rest_2_ = bf16[128,512]{1,0:T(8,128)(2,1)S(1)} collective-permute-done((bf16[128,512]{1,0:T(8,128)(2,1)S(1)}, bf16[128,512]{1,0:T(8,128)(2,1)S(1)}, u32[]{:S(2)}, u32[]{:S(2)}) %collective-permute-start.20) | collective-permute-done | bytes 131104 | tf_op jit(solution)/shard_map/ppermute | solution.py:601
  91.6 2.2 %collective-permute-done.24.t3 = bf16[128,640]{1,0:T(8,128)(2,1)S(1)} collective-permute-done((bf16[128,640]{1,0:T(8,128)(2,1)S(1)}, bf16[128,640]{1,0:T(8,128)(2,1)S(1)}, u32[]{:S(2)}, u32[]{:S(2)}) %collective-permute-start.24) | collective-permute-done | bytes 163872 | tf_op jit(solution)/shard_map/ppermute | solution.py:601
  95.9 2.4 %collective-permute-start.26 = (bf16[128,512]{1,0:T(8,128)(2,1)S(1)}, bf16[128,512]{1,0:T(8,128)(2,1)S(1)}, u32[]{:S(2)}, u32[]{:S(2)}) collective-permute-start(bf16[128,512]{1,0:T(8,128)(2,1)S(1)} %get-tuple-element.139.t0), channel_id=1, source_target_pairs={{0,2},{1,3},{2,0},{3,1},{4,6},{5,7},{6,4},{7,5},{8,10},{9,11},{10,... | collective-permute-start | bytes 393224 | tf_op jit(solution)/shard_map/ppermute | solution.py:601
  104.1 2.9 %message_backward.1 = (f32[128,512]{1,0:T(8,128)S(1)}, bf16[128,512]{1,0:T(8,128)(2,1)S(1)}, f32[1,512]{1,0:T(1,128)S(1)}, bf16[512,1920]{1,0:T(8,128)(2,1)S(1)}...) custom-call(bf16[128,512]{1,0:T(8,128)(2,1)S(1)} %get-tuple-element., ...), custom_call_target="tpu_custom_call" | custom-call | flops 20000000000 | bytes 10864640 | tf_op jit(solution)/shard_map/message_backward/pallas_call | solution.py:583
  107.3 2.5 %collective-permute-start.49 = (bf16[352,512]{1,0:T(8,128)(2,1)S(1)}, bf16[352,512]{1,0:T(8,128)(2,1)S(1)}, u32[]{:S(2)}, u32[]{:S(2)}) collective-permute-start(bf16[352,512]{1,0:T(8,128)(2,1)S(1)} %get-tuple-element.186), channel_id=1, source_target_pairs={{0,8},{4,12},{8,0},{12,4},{1,9},{5,13},{9,1},{13,5},{2,10},{6,14},... | collective-permute-start | bytes 1081352 | tf_op jit(solution)/shard_map/ppermute | solution.py:601
  113.3 2.8 %message_edges.1 = (f32[15,192,128]{2,1,0:T(8,128)}, f32[8,256]{1,0:T(8,128)S(1)}) custom-call(bf16[15,192,128]{2,1,0:T(8,128)(2,1)S(1)} %bitcast.31, bf16[512,1920]{1,0:T(8,128)(2,1)S(1)} %get-tuple-element.146.du_ref, bf16[192,1920]{1,0:T(8,128)(2,1)S(1)} %get-tuple-element.147.dq_ref, bf16[15,192,128]{2,1,0:T(8,128)(2,1)S(1)} %bitcast.34, ...), custom_call_target="tpu_custom_call" | custom-call | bytes 7036928 | tf_op jit(solution)/shard_map/message_edges/pallas_call | solution.py:583
  117.9 4.4 %collective-permute-done.29.x2 = bf16[832,128]{1,0:T(8,128)(2,1)S(1)} collective-permute-done((bf16[832,128]{1,0:T(8,128)(2,1)S(1)}, bf16[832,128]{1,0:T(8,128)(2,1)S(1)}, u32[]{:S(2)}, u32[]{:S(2)}) %collective-permute-start.29) | collective-permute-done | bytes 213024 | tf_op jit(solution)/shard_map/ppermute | solution.py:601
  122.4 4.4 %collective-permute-done.49.two_ref = bf16[352,512]{1,0:T(8,128)(2,1)S(1)} collective-permute-done((bf16[352,512]{1,0:T(8,128)(2,1)S(1)}, bf16[352,512]{1,0:T(8,128)(2,1)S(1)}, u32[]{:S(2)}, u32[]{:S(2)}) %collective-permute-start.49) | collective-permute-done | bytes 360480 | tf_op jit(solution)/shard_map/ppermute | solution.py:601
  131.5 3.5 %collective-permute-done.31.rest_1_ = bf16[128,128]{1,0:T(8,128)(2,1)S(1)} collective-permute-done((bf16[128,128]{1,0:T(8,128)(2,1)S(1)}, bf16[128,128]{1,0:T(8,128)(2,1)S(1)}, u32[]{:S(2)}, u32[]{:S(2)}) %collective-permute-start.31) | collective-permute-done | bytes 32800 | tf_op jit(solution)/shard_map/ppermute | solution.py:601
  148.0 2.4 %collective-permute-start.40 = (bf16[256,128]{1,0:T(8,128)(2,1)S(1)}, bf16[256,128]{1,0:T(8,128)(2,1)S(1)}, u32[]{:S(2)}, u32[]{:S(2)}) collective-permute-start(bf16[256,128]{1,0:T(8,128)(2,1)S(1)} %get-tuple-element.166.rest_0_), channel_id=1, source_target_pairs={{0,12},{4,8},{8,4},{12,0},{1,13},{5,9},{9,5},{13,1},{2,14},{6,10},... | collective-permute-start | bytes 196616 | tf_op jit(solution)/shard_map/ppermute | solution.py:601
  153.8 7.4 %collective-permute-done.40.rest_3_ = bf16[256,128]{1,0:T(8,128)(2,1)S(1)} collective-permute-done((bf16[256,128]{1,0:T(8,128)(2,1)S(1)}, bf16[256,128]{1,0:T(8,128)(2,1)S(1)}, u32[]{:S(2)}, u32[]{:S(2)}) %collective-permute-start.40) | collective-permute-done | bytes 65568 | tf_op jit(solution)/shard_map/ppermute | solution.py:601
  163.3 3.3 %collective-permute-done.38.rest_1_ = bf16[256,128]{1,0:T(8,128)(2,1)S(1)} collective-permute-done((bf16[256,128]{1,0:T(8,128)(2,1)S(1)}, bf16[256,128]{1,0:T(8,128)(2,1)S(1)}, u32[]{:S(2)}, u32[]{:S(2)}) %collective-permute-start.38) | collective-permute-done | bytes 65568 | tf_op jit(solution)/shard_map/ppermute | solution.py:601
  (124 shorter events, 83.2 us)
Async XLA Ops:
  2.2 18.9 %collective-permute-start.3 = (bf16[128,2304]{1,0:T(8,128)(2,1)S(1)}, bf16[128,2304]{1,0:T(8,128)(2,1)S(1)}, u32[]{:S(2)}, u32[]{:S(2)}) collective-permute-start(bf16[128,2304]{1,0:T(8,128)(2,1)S(1)} %get-tuple-element.111.full_ref), channel_id=1, source_target_pairs={{0,1},{1,0},{2,3},{3,2},{16,18},{17,19},{18,16},{19,17},{4,5},{5,4... | collective-permute-start | bytes 1769480 | tf_op jit(solution)/shard_map/ppermute | solution.py:678
  5.2 8.5 %collective-permute-start.2 = (bf16[128,512]{1,0:T(8,128)(2,1)}, bf16[128,512]{1,0:T(8,128)(2,1)S(1)}, u32[]{:S(2)}, u32[]{:S(2)}) collective-permute-start(bf16[128,512]{1,0:T(8,128)(2,1)} %bitcast.35), channel_id=1, source_target_pairs={{0,12},{4,8},{8,4},{12,0},{1,13},{5,9},{9,5},{13,1},{2,14},{6,10},... | collective-permute-start | bytes 393224 | tf_op jit(solution)/shard_map/ppermute | solution.py:601
  8.8 11.0 %collective-permute-start.1 = (bf16[128,512]{1,0:T(8,128)(2,1)}, bf16[128,512]{1,0:T(8,128)(2,1)S(1)}, u32[]{:S(2)}, u32[]{:S(2)}) collective-permute-start(bf16[128,512]{1,0:T(8,128)(2,1)} %bitcast.36), channel_id=1, source_target_pairs={{0,8},{4,12},{8,0},{12,4},{1,9},{5,13},{9,1},{13,5},{2,10},{6,14},... | collective-permute-start | bytes 393224 | tf_op jit(solution)/shard_map/ppermute | solution.py:601
  8.8 11.0 %collective-permute-start = (bf16[128,512]{1,0:T(8,128)(2,1)}, bf16[128,512]{1,0:T(8,128)(2,1)S(1)}, u32[]{:S(2)}, u32[]{:S(2)}) collective-permute-start(bf16[128,512]{1,0:T(8,128)(2,1)} %bitcast.37), channel_id=1, source_target_pairs={{0,4},{4,0},{8,12},{12,8},{1,5},{5,1},{9,13},{13,9},{2,6},{6,2},{1... | collective-permute-start | bytes 393224 | tf_op jit(solution)/shard_map/ppermute | solution.py:601
  9.6 11.6 %collective-permute-start.4 = (bf16[128,1152]{1,0:T(8,128)(2,1)S(1)}, bf16[128,1152]{1,0:T(8,128)(2,1)S(1)}, u32[]{:S(2)}, u32[]{:S(2)}) collective-permute-start(bf16[128,1152]{1,0:T(8,128)(2,1)S(1)} %get-tuple-element.113), channel_id=1, source_target_pairs={{0,3},{1,2},{2,1},{3,0},{4,7},{5,6},{6,5},{7,4},{8,11},{9,10},{10,... | collective-permute-start | bytes 884744 | tf_op jit(solution)/shard_map/ppermute | solution.py:601
  50.1 12.6 %collective-permute-start.18 = (bf16[128,1024]{1,0:T(8,128)(2,1)S(1)}, bf16[128,1024]{1,0:T(8,128)(2,1)S(1)}, u32[]{:S(2)}, u32[]{:S(2)}) collective-permute-start(bf16[128,1024]{1,0:T(8,128)(2,1)S(1)} %get-tuple-element.123.rest_4_.w0), channel_id=1, source_target_pairs={{0,3},{1,2},{2,1},{3,0},{4,7},{5,6},{6,5},{7,4},{8,11},{9,10},{10,... | collective-permute-start | bytes 786440 | tf_op jit(solution)/shard_map/ppermute | solution.py:601
  51.5 13.0 %collective-permute-start.17 = (bf16[128,1024]{1,0:T(8,128)(2,1)S(1)}, bf16[128,1024]{1,0:T(8,128)(2,1)S(1)}, u32[]{:S(2)}, u32[]{:S(2)}) collective-permute-start(bf16[128,1024]{1,0:T(8,128)(2,1)S(1)} %get-tuple-element.123.rest_4_.w0), channel_id=1, source_target_pairs={{0,2},{1,3},{2,0},{3,1},{4,6},{5,7},{6,4},{7,5},{8,10},{9,11},{10,... | collective-permute-start | bytes 786440 | tf_op jit(solution)/shard_map/ppermute | solution.py:601
  52.1 12.5 %collective-permute-start.16 = (bf16[128,1024]{1,0:T(8,128)(2,1)S(1)}, bf16[128,1024]{1,0:T(8,128)(2,1)S(1)}, u32[]{:S(2)}, u32[]{:S(2)}) collective-permute-start(bf16[128,1024]{1,0:T(8,128)(2,1)S(1)} %get-tuple-element.123.rest_4_.w0), channel_id=1, source_target_pairs={{0,1},{1,0},{2,3},{3,2},{4,5},{5,4},{6,7},{7,6},{8,9},{9,8},{10,11... | collective-permute-start | bytes 786440 | tf_op jit(solution)/shard_map/ppermute | solution.py:601
  69.6 13.0 %collective-permute-start.20 = (bf16[128,512]{1,0:T(8,128)(2,1)S(1)}, bf16[128,512]{1,0:T(8,128)(2,1)S(1)}, u32[]{:S(2)}, u32[]{:S(2)}) collective-permute-start(bf16[128,512]{1,0:T(8,128)(2,1)S(1)} %get-tuple-element.130), channel_id=1, source_target_pairs={{0,8},{4,12},{8,0},{12,4},{1,9},{5,13},{9,1},{13,5},{2,10},{6,14},... | collective-permute-start | bytes 393224 | tf_op jit(solution)/shard_map/ppermute | solution.py:601
  71.5 11.1 %collective-permute-start.21 = (bf16[128,512]{1,0:T(8,128)(2,1)S(1)}, bf16[128,512]{1,0:T(8,128)(2,1)S(1)}, u32[]{:S(2)}, u32[]{:S(2)}) collective-permute-start(bf16[128,512]{1,0:T(8,128)(2,1)S(1)} %get-tuple-element.131), channel_id=1, source_target_pairs={{0,12},{4,8},{8,4},{12,0},{1,13},{5,9},{9,5},{13,1},{2,14},{6,10},... | collective-permute-start | bytes 393224 | tf_op jit(solution)/shard_map/ppermute | solution.py:601
  85.0 8.7 %collective-permute-start.24 = (bf16[128,640]{1,0:T(8,128)(2,1)S(1)}, bf16[128,640]{1,0:T(8,128)(2,1)S(1)}, u32[]{:S(2)}, u32[]{:S(2)}) collective-permute-start(bf16[128,640]{1,0:T(8,128)(2,1)S(1)} %get-tuple-element.136), channel_id=1, source_target_pairs={{0,3},{1,2},{2,1},{3,0},{4,7},{5,6},{6,5},{7,4},{8,11},{9,10},{10,... | collective-permute-start | bytes 491528 | tf_op jit(solution)/shard_map/ppermute | solution.py:601
  86.5 11.9 %collective-permute-start.45 = (bf16[512,128]{1,0:T(8,128)(2,1)S(1)}, bf16[512,128]{1,0:T(8,128)(2,1)S(1)}, u32[]{:S(2)}, u32[]{:S(2)}) collective-permute-start(bf16[512,128]{1,0:T(8,128)(2,1)S(1)} %get-tuple-element.180), channel_id=1, source_target_pairs={{0,1},{1,0},{2,3},{3,2},{4,5},{5,4},{6,7},{7,6},{8,9},{9,8},{10,11... | collective-permute-start | bytes 393224 | tf_op jit(solution)/shard_map/ppermute | solution.py:601
  86.8 11.7 %collective-permute-start.46 = (bf16[512,128]{1,0:T(8,128)(2,1)S(1)}, bf16[512,128]{1,0:T(8,128)(2,1)S(1)}, u32[]{:S(2)}, u32[]{:S(2)}) collective-permute-start(bf16[512,128]{1,0:T(8,128)(2,1)S(1)} %get-tuple-element.181), channel_id=1, source_target_pairs={{0,2},{1,3},{2,0},{3,1},{4,6},{5,7},{6,4},{7,5},{8,10},{9,11},{10,... | collective-permute-start | bytes 393224 | tf_op jit(solution)/shard_map/ppermute | solution.py:601
  90.2 8.9 %collective-permute-start.47 = (bf16[512,128]{1,0:T(8,128)(2,1)S(1)}, bf16[512,128]{1,0:T(8,128)(2,1)S(1)}, u32[]{:S(2)}, u32[]{:S(2)}) collective-permute-start(bf16[512,128]{1,0:T(8,128)(2,1)S(1)} %get-tuple-element.182), channel_id=1, source_target_pairs={{0,3},{1,2},{2,1},{3,0},{4,7},{5,6},{6,5},{7,4},{8,11},{9,10},{10,... | collective-permute-start | bytes 393224 | tf_op jit(solution)/shard_map/ppermute | solution.py:601
  107.3 19.5 %collective-permute-start.49 = (bf16[352,512]{1,0:T(8,128)(2,1)S(1)}, bf16[352,512]{1,0:T(8,128)(2,1)S(1)}, u32[]{:S(2)}, u32[]{:S(2)}) collective-permute-start(bf16[352,512]{1,0:T(8,128)(2,1)S(1)} %get-tuple-element.186), channel_id=1, source_target_pairs={{0,8},{4,12},{8,0},{12,4},{1,9},{5,13},{9,1},{13,5},{2,10},{6,14},... | collective-permute-start | bytes 1081352 | tf_op jit(solution)/shard_map/ppermute | solution.py:601
  110.6 11.7 %collective-permute-start.29 = (bf16[832,128]{1,0:T(8,128)(2,1)S(1)}, bf16[832,128]{1,0:T(8,128)(2,1)S(1)}, u32[]{:S(2)}, u32[]{:S(2)}) collective-permute-start(bf16[832,128]{1,0:T(8,128)(2,1)S(1)} %get-tuple-element.144), channel_id=1, source_target_pairs={{0,2},{1,3},{2,0},{3,1},{4,6},{5,7},{6,4},{7,5},{8,10},{9,11},{10,... | collective-permute-start | bytes 638984 | tf_op jit(solution)/shard_map/ppermute | solution.py:601
  111.5 10.8 %collective-permute-start.30 = (bf16[832,128]{1,0:T(8,128)(2,1)S(1)}, bf16[832,128]{1,0:T(8,128)(2,1)S(1)}, u32[]{:S(2)}, u32[]{:S(2)}) collective-permute-start(bf16[832,128]{1,0:T(8,128)(2,1)S(1)} %get-tuple-element.145), channel_id=1, source_target_pairs={{0,3},{1,2},{2,1},{3,0},{4,7},{5,6},{6,5},{7,4},{8,11},{9,10},{10,... | collective-permute-start | bytes 638984 | tf_op jit(solution)/shard_map/ppermute | solution.py:601
  127.0 9.1 %collective-permute-start.50 = (bf16[176,512]{1,0:T(8,128)(2,1)S(1)}, bf16[176,512]{1,0:T(8,128)(2,1)S(1)}, u32[]{:S(2)}, u32[]{:S(2)}) collective-permute-start(bf16[176,512]{1,0:T(8,128)(2,1)S(1)} %get-tuple-element.188), channel_id=1, source_target_pairs={{0,4},{4,0},{8,12},{12,8},{1,5},{5,1},{9,13},{13,9},{2,6},{6,2},{1... | collective-permute-start | bytes 540680 | tf_op jit(solution)/shard_map/ppermute | solution.py:601
  136.2 10.1 %collective-permute-start.51 = (bf16[176,512]{1,0:T(8,128)(2,1)S(1)}, bf16[176,512]{1,0:T(8,128)(2,1)S(1)}, u32[]{:S(2)}, u32[]{:S(2)}) collective-permute-start(bf16[176,512]{1,0:T(8,128)(2,1)S(1)} %early_three.1.one_ref), channel_id=1, source_target_pairs={{0,8},{4,12},{8,0},{12,4},{1,9},{5,13},{9,1},{13,5},{2,10},{6,14},... | collective-permute-start | bytes 540680 | tf_op jit(solution)/shard_map/ppermute | solution.py:601
  146.3 21.2 %collective-permute-start.52 = (bf16[352,512]{1,0:T(8,128)(2,1)S(1)}, bf16[352,512]{1,0:T(8,128)(2,1)S(1)}, u32[]{:S(2)}, u32[]{:S(2)}) collective-permute-start(bf16[352,512]{1,0:T(8,128)(2,1)S(1)} %early_four.1.m0), channel_id=1, source_target_pairs={{0,4},{4,0},{8,12},{12,8},{1,5},{5,1},{9,13},{13,9},{2,6},{6,2},{1... | collective-permute-start | bytes 1081352 | tf_op jit(solution)/shard_map/ppermute | solution.py:601
  148.0 13.2 %collective-permute-start.40 = (bf16[256,128]{1,0:T(8,128)(2,1)S(1)}, bf16[256,128]{1,0:T(8,128)(2,1)S(1)}, u32[]{:S(2)}, u32[]{:S(2)}) collective-permute-start(bf16[256,128]{1,0:T(8,128)(2,1)S(1)} %get-tuple-element.166.rest_0_), channel_id=1, source_target_pairs={{0,12},{4,8},{8,4},{12,0},{1,13},{5,9},{9,5},{13,1},{2,14},{6,10},... | collective-permute-start | bytes 196616 | tf_op jit(solution)/shard_map/ppermute | solution.py:601
  150.4 10.8 %collective-permute-start.39 = (bf16[256,128]{1,0:T(8,128)(2,1)S(1)}, bf16[256,128]{1,0:T(8,128)(2,1)S(1)}, u32[]{:S(2)}, u32[]{:S(2)}) collective-permute-start(bf16[256,128]{1,0:T(8,128)(2,1)S(1)} %get-tuple-element.166.rest_0_), channel_id=1, source_target_pairs={{0,8},{4,12},{8,0},{12,4},{1,9},{5,13},{9,1},{13,5},{2,10},{6,14},... | collective-permute-start | bytes 196616 | tf_op jit(solution)/shard_map/ppermute | solution.py:601
  150.4 16.1 %collective-permute-start.43 = (bf16[384,128]{1,0:T(8,128)(2,1)S(1)}, bf16[384,128]{1,0:T(8,128)(2,1)S(1)}, u32[]{:S(2)}, u32[]{:S(2)}) collective-permute-start(bf16[384,128]{1,0:T(8,128)(2,1)S(1)} %get-tuple-element.167.rest_4_._), channel_id=1, source_target_pairs={{0,12},{4,8},{8,4},{12,0},{1,13},{5,9},{9,5},{13,1},{2,14},{6,10},... | collective-permute-start | bytes 294920 | tf_op jit(solution)/shard_map/ppermute | solution.py:601
  152.1 14.5 %collective-permute-start.42 = (bf16[384,128]{1,0:T(8,128)(2,1)S(1)}, bf16[384,128]{1,0:T(8,128)(2,1)S(1)}, u32[]{:S(2)}, u32[]{:S(2)}) collective-permute-start(bf16[384,128]{1,0:T(8,128)(2,1)S(1)} %get-tuple-element.167.rest_4_._), channel_id=1, source_target_pairs={{0,8},{4,12},{8,0},{12,4},{1,9},{5,13},{9,1},{13,5},{2,10},{6,14},... | collective-permute-start | bytes 294920 | tf_op jit(solution)/shard_map/ppermute | solution.py:601
  (38 other events, 295.9 us)

commit v4 on v3

--- a/solution.py
+++ b/solution.py
@@ -91,7 +91,8 @@
 
 
 def edge_prep(
-    graph, near, et_ref, nbr_ref, res_ref, ga_ref, gb_ref, na_ref, nb_ref, nc_ref, mix_ref, mask_ref, gains_ref, nodes_ref
+    graph, near, et_ref, nbr_ref, res_ref, ga_ref, gb_ref, na_ref, nb_ref, nc_ref, node_ref,
+    mix_ref, mask_ref, gains_ref, nodes_ref, own_ref,
 ):
     slots, side, rows = et_ref.shape
     total = mask_ref.shape[1]
@@ -101,6 +102,8 @@
         mask_ref[:, k * rows : (k + 1) * rows] = res_ref[:, pl.ds(pl.multiple_of(block * rows, rows), rows)]
     for i, ref in enumerate((na_ref, nb_ref, nc_ref)):
         nodes_ref[i : i + 1, :] = ref[...]
+    hat, _ = normalize(node_ref[...].astype(F32))
+    own_ref[...] = (hat * na_ref[...]).astype(BF16)
     for i, ref in enumerate((ga_ref, gb_ref)):
         gains_ref[i] = jnp.broadcast_to(ref[...], (rows, ref.shape[1])).T
     for s in range(slots):
@@ -143,7 +146,7 @@
     part_ref[...] = dot_nt(dp, win_ref[...]).astype(BF16)
 
 
-def pack_weights(ms, mo, me, mout, us, uo, ue, uout_t, full_ref, half_ref, later_ref):
+def pack_weights(ms, mo, me, mout, us, uo, ue, uout_t, full_ref, half_ref, later_ref, later_half_ref):
     wide = ms.shape[0]
     size = half_ref.shape[1]
 
@@ -163,9 +166,11 @@
 
     def keep_front():
         half_ref[...] = front
+        later_half_ref[...] = later_ref[:, :wide]
 
     def keep_back():
         half_ref[...] = back
+        later_half_ref[...] = later_ref[:, wide:]
 
     by_core(keep_front, keep_back)
 
@@ -176,8 +181,11 @@
     block = node_refs[0].shape[0] if parts > 1 else 512
     for at in range(0, total, block):
         ref = node_refs[at // block] if parts > 1 else node_refs[0].at[at : at + block]
-        hat, _ = normalize(ref[...].astype(F32))
-        a_ref[at : at + block, :] = (hat * gain_ref[0:1, :]).astype(BF16)
+        if parts > 1 and at == 0:
+            a_ref[:block, :] = ref[...]
+        else:
+            hat, _ = normalize(ref[...].astype(F32))
+            a_ref[at : at + block, :] = (hat * gain_ref[0:1, :]).astype(BF16)
 
 
 def message_forward(
@@ -236,7 +244,8 @@
 
 
 def node_forward(
-    s0, s1, s2, s3, nodes_ref, backs_ref, gain_ref, win_ref, wout_ref, s_ref, h1_ref, b_ref, y_ref, slope_ref, part_ref
+    s0, s1, s2, s3, nodes_ref, backs_ref, gain_ref, win_ref, wout_ref, _, __,
+    s_ref, h1_ref, b_ref, y_ref, slope_ref, part_ref
 ):
     width = nodes_ref.shape[1]
     sums = []
@@ -259,22 +268,35 @@
 
 
 def update_nodes(slots, parts, outs, mix_ref, cot_ref, fronts_ref, *rest):
-    node_refs, w_refs = rest[:parts], rest[parts : parts + 4]
-    w_ref, dv_ref, r_ref = rest[parts + 4 : parts + 7]
-    s_refs = rest[parts + 7 : parts + 7 + outs]
-    lhs_ref, v_ref, g_ref, ps_ref, racc_ref = rest[parts + 7 + outs :]
+    node_refs = rest[:parts]
+    own_ref, cross_ref, diag_ref, cross_two_ref, diag_two_ref, w_ref, dv_ref, r_ref, laters_ref = rest[parts : parts + 9]
+    s_refs = rest[parts + 9 : parts + 9 + outs]
+    lhs_ref, v_ref, g_ref, ps_ref, racc_ref = rest[parts + 9 + outs :]
     side, rows = cot_ref.shape[1:]
     total = mix_ref.shape[0] - 2 * side
     width = node_refs[0].shape[1]
     hidden = ps_ref.shape[0]
-    other = stack(w_refs, width, 2 * width)
-    block = node_refs[0].shape[0] if parts > 1 else 512
-    for at in range(0, total, block):
-        ref = node_refs[at // block] if parts > 1 else node_refs[0].at[at : at + block]
-        lhs_ref[:, at : at + block] = dot_nt(other, ref[...]).astype(BF16)
+    shard = own_ref.shape[0]
+
+    def place(blocks, own, other):
+        for k, ref in enumerate(blocks):
+            laters_ref[k * shard : (k + 1) * shard, :] = ref[...]
+        laters_ref[3 * shard :, :width] = own[...]
+        laters_ref[3 * shard :, width:] = other[...]
+
+    by_core(
+        lambda: place((own_ref, cross_ref, cross_two_ref), diag_ref, diag_two_ref),
+        lambda: place((own_ref, cross_two_ref, cross_ref), diag_two_ref, diag_ref),
+    )
+    other = laters_ref[:, width:]
+    if parts > 1:
+        lhs_ref[:, :total] = dot_nt(other, rows_of(node_refs)).astype(BF16)
+    else:
+        for at in range(0, total, 512):
+            lhs_ref[:, at : at + 512] = dot_nt(other, node_refs[0][at : at + 512, :]).astype(BF16)
     lhs_ref[:, total:] = fronts_ref[:, width + side : width + 2 * side]
     wo = fronts_ref[:, width + 2 * side : width + 3 * side]
-    ps_ref[...] = dot_nt(stack(w_refs, 0, width), node_refs[0][:rows, :])
+    ps_ref[...] = dot_nt(laters_ref[:, :width], node_refs[0][:rows, :])
 
     v_all = dot(lhs_ref[...], mix_ref[side:, :])
     g_all = dot(wo, lanes(cot_ref))
@@ -322,12 +344,11 @@
         ref[rows + side :, :] = gout[:, at]
 
 
-def update_terms(parts, r_ref, w0, w1, w2, w3, *rest):
+def update_terms(parts, r_ref, laters_ref, *rest):
     s_refs, outs = rest[:parts], rest[-4:]
     width = r_ref.shape[1]
     total = sum_of(s_refs).astype(BF16)
-    ws = (w0, w1, w2, w3)
-    term = (dot(r_ref[...], stack(ws, 0, width)) + dot(total, stack(ws, width, 2 * width))).astype(BF16)
+    term = (dot(r_ref[...], laters_ref[:, :width]) + dot(total, laters_ref[:, width:])).astype(BF16)
     for k, ref in enumerate(outs):
         ref[:, :width] = term
         ref[:, width:] = total[:, k * 128 : k * 128 + 128]
@@ -344,8 +365,9 @@
     edge_ref[...] = every[low:]
 
 
-def message_terms(parts, r_ref, fronts_ref, backs_ref, nodes_ref, gb_ref, gc_ref, ge_ref, *rest):
-    s_refs, (term_ref, share_ref) = rest[:parts], rest[parts:]
+def message_terms(parts, r_ref, fronts_ref, backs_ref, nodes_ref, gb_ref, gc_ref, ge_ref, keep_ref, got_ref, *rest):
+    s_refs, (term_ref, share_ref, late_ref) = rest[:parts], rest[parts:]
+    late_ref[...] = (keep_ref[...].astype(F32) + got_ref[...].astype(F32)).astype(BF16)
     rows, shard = r_ref.shape
     width = nodes_ref.shape[1]
     total = sum_of(s_refs).astype(BF16)
@@ -359,7 +381,7 @@
     term_ref[...] = jnp.concatenate([term] + gains, axis=0).astype(BF16)
 
 
-def early_grads(b_ref, dp_ref, y_ref, dr_ref, c_ref, share_ref, x0, x1, x2, x3, _, __, ___, keep_ref, send_ref):
+def early_grads(b_ref, dp_ref, y_ref, dr_ref, c_ref, share_ref, x0, x1, x2, x3, _, keep_ref, send_ref):
     rows, width = c_ref.shape
     extra = sum_of((x0, x1, x2, x3)).astype(BF16)
     side = (extra.shape[0] - rows) // 2
@@ -424,9 +446,7 @@
         for pair, large, top, low in ((one, gin_ref, self_ref, edge_ref), (two, gout_ref, other_ref, out_ref)):
             pair = [r[...] for r in pair]
             if bit:
-                clear, full = join(bit, *pair)
-                quarter = clear.shape[0] // 2
-                pair = [clear[:quarter], full[:quarter], clear[quarter:], full[quarter:]]
+                pair = join(bit, *pair)
             every = jnp.concatenate(pair, axis=0).astype(F32)
             large[...] = every[:width]
             small = jnp.concatenate([every[width : width + part, i * 128 : i * 128 + 128] for i in range(4)], axis=0)
@@ -512,29 +532,36 @@
     by_core(lambda: put(keep_ref, send_ref), lambda: put(send_ref, keep_ref))
 
 
-def node_finish(t0, t1, t2, t3, nodes_ref, dh1_ref, gain_ref, keep_ref, got_ref, out_ref, late_ref):
+def node_finish(t0, t1, t2, t3, nodes_ref, dh1_ref, gain_ref, share_ref, late_ref, got_ref, out_ref, pack_ref, long_ref):
     rows, width = dh1_ref.shape
-    half = keep_ref.shape[0]
+    low = share_ref.shape[0]
     every = sum_of((t0, t1, t2, t3))
     hat, inv = normalize(nodes_ref[...].astype(F32))
     out_ref[...] = dh1_ref[...] + norm_back(every[:rows] * gain_ref[0:1, :], hat, inv)
-    late_ref[:half, :] = (keep_ref[...].astype(F32) + got_ref[...].astype(F32)).astype(BF16)
-    late_ref[half:, :] = jnp.concatenate(
+    gains = jnp.concatenate(
         [every[rows : rows + 8, i * 128 : i * 128 + 128] for i in range(width // 128)], axis=0
     ).astype(BF16)
+    pack_ref[:low, :] = share_ref[...]
+    pack_ref[low:, :] = gains
+    long_ref[:low, :] = share_ref[...]
+    long_ref[low : pack_ref.shape[0], :] = gains
+    long_ref[pack_ref.shape[0] :, :] = (late_ref[...].astype(F32) + got_ref[...].astype(F32)).astype(BF16)
 
 
 def message_grads(parts, a_ref, *rest):
-    shares, lates, out_ref = rest[:parts], rest[parts : 2 * parts], rest[-1]
+    packs, (one_ref, two_ref, out_ref) = rest[:parts], rest[parts:]
     rows = a_ref.shape[0] // parts
     width = a_ref.shape[1]
+    size = packs[0].shape[0]
     both = jnp.concatenate(
-        [jnp.concatenate([r[:rows, :], r[rows:, :]], axis=1) for r in shares], axis=0
+        [jnp.concatenate([r[:rows, :], r[rows : 2 * rows, :]], axis=1) for r in packs], axis=0
     )
     grad = dot_tn(a_ref[...], both).astype(BF16)
     out_ref[:width, :] = grad[:, :128]
     out_ref[width : 2 * width, :] = grad[:, 128:]
-    out_ref[2 * width :, :] = sum(r[...].astype(F32) for r in lates).astype(BF16)
+    low = 2 * width + one_ref.shape[0] - size
+    out_ref[2 * width : low, :] = (one_ref[size:, :].astype(F32) + two_ref[size:, :].astype(F32)).astype(BF16)
+    out_ref[low:, :] = sum(r[2 * rows : size, :].astype(F32) for r in packs).astype(BF16)
 
 
 def finish_late(
@@ -658,32 +685,39 @@
     cot = jnp.transpose(edge_cot[0], (1, 2, 0))
     edge_sh, hid_sh = (slots, side, rows), (hidden, slots * rows)
 
-    mix, mask_row, gains_e, gains_n = run(
+    mix, mask_row, gains_e, gains_n, a_own = run(
         "edge_prep", functools.partial(edge_prep, graph, near), 1,
         [
             far_in(v) for v in (
                 et, jnp.transpose(neighbours, (2, 0, 1)), resmask, edge_gain_a[None, :], edge_gain_b[None, :],
-                node_gain_a[None, :], node_gain_b[None, :], node_gain_c[None, :],
+                node_gain_a[None, :], node_gain_b[None, :], node_gain_c[None, :], node,
             )
         ],
-        [((2 * side + total, slots * rows), BF16), ((1, total), jnp.int32), ((2, side, rows), F32), ((8, width), F32)],
-    )
-    full, half, later = run(
+        [((2 * side + total, slots * rows), BF16), ((1, total), jnp.int32), ((2, side, rows), F32), ((8, width), F32),
+         ((rows, width), BF16)],
+    )
+    full, half, later, later_half = run(
         "pack_weights", pack_weights, 1,
         [far_in(w) for w in (
             message_self, message_other, message_edge, message_out, update_self, update_other, update_edge, update_out.T
         )],
-        [((shard, 2 * width + 2 * 640), BF16), ((shard, width + 640), BF16), ((shard, 2 * width), BF16)],
-    )
-    cross = lax.ppermute(full, ("dp", "mp"), [(c * mp + m, c * mp + (m ^ (1 + c))) for c in range(2) for m in range(mp)])
-    diag = swap(half, "mp", 3, mp)
+        [((shard, 2 * width + 2 * 640), BF16), ((shard, width + 640), BF16), ((shard, 2 * width), BF16),
+         ((shard, width), BF16)],
+    )
+    def across(values):
+        pairs = [(c * mp + m, c * mp + (m ^ (1 + c))) for c in range(2) for m in range(mp)]
+        return lax.ppermute(values, ("dp", "mp"), pairs)
+
+    cross, diag = across(full), swap(half, "mp", 3, mp)
+    cross_later, diag_later = across(later), swap(later_half, "mp", 3, mp)
     (a_all,) = run(
-        "row_prep", functools.partial(row_prep, len(nodes_all)), 1, nodes_all + [gains_n], [((total, width), BF16)],
+        "row_prep", functools.partial(row_prep, len(nodes_all)), 1,
+        ([a_own] + nodes_all[1:] if near else nodes_all) + [gains_n], [((total, width), BF16)],
     )
     cross, diag = after(cross, a_all), after(diag, a_all)
     slope_m, pooled_part, fronts, backs = run(
         "message_forward", functools.partial(message_forward, 1.0 / nbrs, slots), 1,
-        [mix, mask_row, a_all, full, cross, diag, swap(cross, "dp", 1, cores), swap(diag, "dp", 1, cores)],
+        [mix, mask_row, a_all, full, cross, diag, swap(cross, "dp", 1, cores), swap(diag, "dp", 1, cores),],
         [(hid_sh, BF16), ((rows, hidden), BF16), ((hidden, width + 640), BF16), ((hidden, width + 640), BF16)],
         [pltpu.VMEM((hidden + 16, total + side), BF16), pltpu.VMEM((hidden + 16, slots * rows), F32),
          pltpu.VMEM((hidden, rows), F32), pltpu.VMEM((hidden, rows), F32)], heavy=True,
@@ -691,7 +725,7 @@
 
     pooled, h1, b, y, slope_f, h2_part = run(
         "node_forward", node_forward, 1,
-        partners(pooled_part, "mp", mp) + [node, backs, gains_n, ffn_in, ffn_out],
+        partners(pooled_part, "mp", mp) + [node, backs, gains_n, ffn_in, ffn_out, (cross_later, AFTER), (diag_later, AFTER)],
         [((rows, hidden), BF16), ((rows, width), F32), ((rows, width), BF16), ((rows, ff), BF16), ((rows, ff), BF16),
          ((rows, width), BF16)],
     )
@@ -701,11 +735,11 @@
     )
     c_all = gather_rows(c_own)
 
-    wl = partners(after(later, c_own), "mp", mp)
-    w_act, dv, r_upd, *s_upd = run(
+    w_act, dv, r_upd, laters, *s_upd = run(
         "update_nodes", functools.partial(update_nodes, slots, len(c_all), outs), 1,
-        [mix, cot, fronts] + c_all + wl,
-        [(hid_sh, BF16), (hid_sh, BF16), ((rows, hidden), BF16)] + blocks,
+        [mix, cot, fronts] + c_all
+        + [later, cross_later, diag_later, swap(cross_later, "dp", 1, cores), swap(diag_later, "dp", 1, cores)],
+        [(hid_sh, BF16), (hid_sh, BF16), ((rows, hidden), BF16), ((hidden, 2 * width), BF16)] + blocks,
         [pltpu.VMEM((hidden, total + side), BF16), pltpu.VMEM(hid_sh, F32), pltpu.VMEM(hid_sh, F32),
          pltpu.VMEM((hidden, rows), F32), pltpu.VMEM((hidden, rows), F32)], heavy=True,
     )
@@ -719,7 +753,7 @@
     extra = deal(extra, "mp", mp)
 
     terms = run(
-        "update_terms", functools.partial(update_terms, outs), 1, [r_upd] + wl + s_upd_parts + [(order, AFTER)],
+        "update_terms", functools.partial(update_terms, outs), 1, [r_upd, laters] + s_upd_parts + [(order, AFTER)],
         [((rows, width + shard), BF16)] * mp,
     )
     dh2, dr, dp_ffn, gain_c, share, db_part = run(
@@ -731,7 +765,7 @@
 
     size = (width + (width + side) // 4 + 63) // 64 * 64
     keep, send = run(
-        "early_grads", early_grads, 1, [b, dp_ffn, y, dr, c_own, share] + extra + [(v, AFTER) for v in db_parts[1:]], [((size, ff), BF16)] * 2,
+        "early_grads", early_grads, 1, [b, dp_ffn, y, dr, c_own, share] + extra + [(db_parts[3], AFTER)], [((size, ff), BF16)] * 2,
     )
     got = swap(send, "dp", 1, cores)
     halves, quarters = [((size // 2, ff), BF16)], [((size // 4, ff), BF16)]
@@ -744,8 +778,8 @@
         [pltpu.VMEM((hidden, rows), F32), pltpu.VMEM((hidden, rows), F32)], heavy=True,
     )
     if near:
-        stay, go = run("early_one", functools.partial(sum_split, 2), 1, [keep, got, (gain_b, AFTER)], halves * 2)
-        go = swap(go, "graph", 2, graph)
+        stay, go = run("early_one", functools.partial(sum_split, 1), 1, [keep, got, (gain_b, AFTER)], halves * 2)
+        go = swap(go, "graph", 1, graph)
     shares = deal(shares, "mp", mp)
     ge, gains_edge = run(
         "message_edges", message_edges, 1, [et, du, dq, cot, gains_e, fronts], [(edge_sh, F32), ((8, 256), F32)],
@@ -758,38 +792,48 @@
         [((rows, shard), BF16), ((side, shard), BF16)] + [(sh[:1] + (shard,), t) for sh, t in blocks],
     )
     if near:
-        stay, go = run("early_two", functools.partial(sum_split, 1), 1, [stay, go, (share_r, AFTER)], quarters * 2)
-        go = swap(go, "graph", 1, graph)
-    term, share = run(
-        "message_terms", functools.partial(message_terms, outs), 1,
-        [share_r, fronts, backs, node, gain_b, gain_c, gains_edge] + return_rows(share_s),
-        [((rows + 16, width), BF16), ((2 * rows, shard), BF16)],
-    )
-    if near:
-        (own,) = run("early_three", sum_two, 1, [stay, go, (term, AFTER)], quarters)
-        go = swap(own, "graph", 2, graph)
+        stay, go = run("early_two", functools.partial(sum_split, 2), 1, [stay, go, (gains_edge, AFTER)], quarters * 2)
+        go = swap(go, "graph", 2, graph)
     half = (side + width) // 2
     keep_late, send_late = run(
         "late_grads", late_grads, 1,
         [grad_edge, (pooled, pl.BlockSpec((rows, shard), lambda i: (0, 0))), dt], [((half, shard), BF16)] * 2,
     )
-    grad_nodes, late = run(
+    term, share, late = run(
+        "message_terms", functools.partial(message_terms, outs), 1,
+        [share_r, fronts, backs, node, gain_b, gain_c, gains_edge, keep_late, swap(send_late, "dp", 1, cores)]
+        + return_rows(share_s),
+        [((rows + 16, width), BF16), ((2 * rows, shard), BF16), ((half, shard), BF16)],
+    )
+    if near:
+        (own,) = run("early_three", sum_two, 1, [stay, go, (term, AFTER)], quarters)
+        go = swap(own, "graph", 2, graph)
+    none = jnp.zeros((half, shard), BF16)
+    grad_nodes, pack, long = run(
         "node_finish", node_finish, 1,
-        partners(term, "mp", mp) + [node, dh1, gains_n, keep_late, swap(send_late, "dp", 1, cores)],
-        [((rows, width), F32), ((half + width // 16, shard), BF16)],
+        partners(term, "mp", mp) + [node, dh1, gains_n, share, late, swap(late, "graph", 1, graph) if near else none],
+        [((rows, width), F32), ((2 * rows + width // 16, shard), BF16),
+         ((2 * rows + width // 16 + half, shard), BF16)],
     )
     if near:
-        (own,) = run("early_four", functools.partial(join_two, 2), 1, [own, go, (late, AFTER)], halves)
-        early_sum = [own, swap(own, "graph", 1, graph)]
-        share, late = partners(share, "graph", graph), partners(late, "graph", graph)
+        (own,) = run("early_four", functools.partial(join_two, 2), 1, [own, go, (pack, AFTER)], halves)
+        got = swap(own, "graph", 1, graph)
+        long_two = swap(long, "graph", 2, graph)
+        packs = [pack, swap(pack, "graph", 1, graph), long_two, swap(pack, "graph", 3, graph)]
+        early_sum = [own, after(got, *packs[1:])]
     else:
         early = lax.psum(keep.astype(F32) + got.astype(F32), "graph").astype(BF16)
         early_sum = [early[: size // 2], early[size // 2 :]]
-        share, late = [share], [late]
-    parts = len(share)
+        packs, long_two = [pack], jnp.zeros_like(long)
+    grad_in, grad_out, grad_us, grad_ue, grad_uo, grad_uout = run(
+        "finish_early", functools.partial(finish_early, 1 if near else 0), 1, early_sum + [swap(v, "dp", 1, cores) for v in early_sum],
+        [((width, ff), F32), ((ff, width), F32), ((width, shard), F32), ((side, shard), F32), ((width, shard), F32),
+         ((side, shard), F32)],
+    )
+    parts = len(packs)
     (part,) = run(
         "message_grads", functools.partial(message_grads, parts), 1,
-        [(a_all, pl.BlockSpec((parts * rows, width), lambda i: (0, 0)))] + share + late,
+        [(a_all, pl.BlockSpec((parts * rows, width), lambda i: (0, 0)))] + packs + [long, long_two],
         [((2 * width + half + width // 16, shard), BF16)],
     )
     if not near:
@@ -798,11 +842,6 @@
         "finish_late", finish_late, 1, [part, swap(part, "dp", 1, cores)],
         [((width, shard), F32), ((width, shard), F32), ((side, shard), F32), ((shard, width), F32), ((1, width), F32),
          ((1, width), F32), ((1, width), F32), ((1, side), F32), ((1, side), F32)],
-    )
-    grad_in, grad_out, grad_us, grad_ue, grad_uo, grad_uout = run(
-        "finish_early", functools.partial(finish_early, 1 if near else 0), 1, early_sum + [swap(v, "dp", 1, cores) for v in early_sum],
-        [((width, ff), F32), ((ff, width), F32), ((width, shard), F32), ((side, shard), F32), ((width, shard), F32),
-         ((side, shard), F32)],
     )
     return (
         nodes_out[None],

time: 172 us -> 159 us (0.924)
  waiting for transfers between devices: 72.1 us -> 64.4 us
  starting transfers between devices: 67.1 us -> 62.8 us
    ppermute x54 -> x52, waiting for transfers between devices: 72.1 us -> 64.4 us  [swap(): return lax.ppermute(values, axis, [(i, i ^ bits) for i in range(size)])]
    ppermute x54 -> x52, starting transfers between devices: 64.1 us -> 59.5 us  [swap(): return lax.ppermute(values, axis, [(i, i ^ bits) for i in range(size)])]
  transfers between devices with their start and end apart: 55 -> 54, of which waited for: 31 -> 22; matrix products, arithmetic and copies ran while one was open for 0% -> 0% of each run, Pallas kernels for 9% -> 13%
where the time goes in v4:
time: 159 us
  waiting for transfers between devices  64.4 us (41%)
  starting transfers between devices  62.8 us (39%)
  Pallas kernels  30.5 us (19%)
    ppermute x52, waiting for transfers between devices, swap(): return lax.ppermute(values, axis, [(i, i ^ bits) for i in range(size)])  64.4 us
    ppermute x52, starting transfers between devices, swap(): return lax.ppermute(values, axis, [(i, i ^ bits) for i in range(size)])  59.5 us
    pallas_call x24, Pallas kernels, call(): pl.pallas_call(body, grid=(grid,), in_specs=[s for _, s in ins], out_spec...  30.5 us
    ppermute x2, starting transfers between devices, across(): return lax.ppermute(values, ('dp', 'mp'), pairs)  3.4 us
  transfers between devices with their start and end apart: 54, of which 22 were waited for; matrix products, arithmetic and copies ran while one was open for 0% of the time, Pallas kernels for 13%

profile of v4, /device:TPU:0, one launch (start us, length us, event | category | flops | bytes accessed | tf_op | source)
XLA Modules:
  0.0 158.7 jit_solution(13347474936533048804)
XLA Ops:
  2.3 3.0 %collective-permute-start.3 = (bf16[128,2304]{1,0:T(8,128)(2,1)S(1)}, bf16[128,2304]{1,0:T(8,128)(2,1)S(1)}, u32[]{:S(2)}, u32[]{:S(2)}) collective-permute-start(bf16[128,2304]{1,0:T(8,128)(2,1)S(1)} %get-tuple-element.117.full_ref), channel_id=1, source_target_pairs={{0,1},{1,0},{2,3},{3,2},{16,18},{17,19},{18,16},{19,17},{4,5},{5,4... | collective-permute-start | bytes 1769480 | tf_op jit(solution)/shard_map/ppermute | solution.py:709
  5.3 3.6 %collective-permute-start.2 = (bf16[128,512]{1,0:T(8,128)(2,1)}, bf16[128,512]{1,0:T(8,128)(2,1)S(1)}, u32[]{:S(2)}, u32[]{:S(2)}) collective-permute-start(bf16[128,512]{1,0:T(8,128)(2,1)} %bitcast.35), channel_id=1, source_target_pairs={{0,12},{4,8},{8,4},{12,0},{1,13},{5,9},{9,5},{13,1},{2,14},{6,10},... | collective-permute-start | bytes 393224 | tf_op jit(solution)/shard_map/ppermute | solution.py:628
  11.1 2.9 %edge_prep.1 = (bf16[896,1920]{1,0:T(8,128)(2,1)S(1)}, s32[1,512]{1,0:T(1,128)S(1)}, f32[2,192,128]{2,1,0:T(8,128)S(1)}, f32[8,512]{1,0:T(8,128)S(1)}, bf16[128,512]{1,0:T(8,128)(2,1)S(1)}) custom-call(bf16[15,192,128]{2,1,0:T(8,128)(2,1)} %bitcast.29, s32[60,1,128]{2,1,0:T(1,128)} %bitcast.44, s32[1,512]{1,0:T(1,128)} %res_ref.1, f32[1,192]{1,0:T(1,128)} %bitcast.48, ...), custom_call_target="tpu_custom_call" | custom-call | bytes 4695552 | tf_op jit(solution)/shard_map/edge_prep/pallas_call | solution.py:610
  14.0 5.8 %collective-permute-done.1.refs_2_ = bf16[128,512]{1,0:T(8,128)(2,1)S(1)} collective-permute-done((bf16[128,512]{1,0:T(8,128)(2,1)}, bf16[128,512]{1,0:T(8,128)(2,1)S(1)}, u32[]{:S(2)}, u32[]{:S(2)}) %collective-permute-start.1) | collective-permute-done | bytes 131104 | tf_op jit(solution)/shard_map/ppermute | solution.py:628
  22.8 3.7 %message_forward.1 = (bf16[512,1920]{1,0:T(8,128)(2,1)S(1)}, bf16[128,512]{1,0:T(8,128)(2,1)S(1)}, bf16[512,1152]{1,0:T(8,128)(2,1)S(1)}, bf16[512,1152]{1,0:T(8,128)(2,1)S(1)}) custom-call(bf16[896,1920]{1,0:T(8,128)(2,1)S(1)} %get-tuple-element.113.mix_ref, s32[1,512]{1,0:T(1,128)S(1)} %get-tuple-element.114.mask_ref, bf16[512,512]{1,0:T(8,128)(2,1)S(1)} %row_prep.1.a_ref, ...), custom_call_target="tpu_custom_call" | custom-call | flops 20000000000 | bytes 10782720 | tf_op jit(solution)/shard_map/message_forward/pallas_call | solution.py:610
  26.5 2.7 %collective-permute-start.9 = (bf16[128,512]{1,0:T(8,128)(2,1)S(1)}, bf16[128,512]{1,0:T(8,128)(2,1)S(1)}, u32[]{:S(2)}, u32[]{:S(2)}) collective-permute-start(bf16[128,512]{1,0:T(8,128)(2,1)S(1)} %get-tuple-element.121.s0), channel_id=1, source_target_pairs={{0,3},{1,2},{2,1},{3,0},{4,7},{5,6},{6,5},{7,4},{8,11},{9,10},{10,... | collective-permute-start | bytes 393224 | tf_op jit(solution)/shard_map/ppermute | solution.py:628
  30.0 3.8 %collective-permute-done.9.s3 = bf16[128,512]{1,0:T(8,128)(2,1)S(1)} collective-permute-done((bf16[128,512]{1,0:T(8,128)(2,1)S(1)}, bf16[128,512]{1,0:T(8,128)(2,1)S(1)}, u32[]{:S(2)}, u32[]{:S(2)}) %collective-permute-start.9) | collective-permute-done | bytes 131104 | tf_op jit(solution)/shard_map/ppermute | solution.py:628
  41.1 2.7 %collective-permute-done.14.p3 = bf16[128,512]{1,0:T(8,128)(2,1)S(1)} collective-permute-done((bf16[128,512]{1,0:T(8,128)(2,1)S(1)}, bf16[128,512]{1,0:T(8,128)(2,1)S(1)}, u32[]{:S(2)}, u32[]{:S(2)}) %collective-permute-start.14) | collective-permute-done | bytes 131104 | tf_op jit(solution)/shard_map/ppermute | solution.py:628
  46.6 3.6 %collective-permute-start.17 = (bf16[128,512]{1,0:T(8,128)(2,1)S(1)}, bf16[128,512]{1,0:T(8,128)(2,1)S(1)}, u32[]{:S(2)}, u32[]{:S(2)}) collective-permute-start(bf16[128,512]{1,0:T(8,128)(2,1)S(1)} %get-tuple-element.129.rest_0_.c_ref), channel_id=1, source_target_pairs={{0,12},{4,8},{8,4},{12,0},{1,13},{5,9},{9,5},{13,1},{2,14},{6,10},... | collective-permute-start | bytes 393224 | tf_op jit(solution)/shard_map/ppermute | solution.py:628
  51.0 3.9 %collective-permute-done.17.rest_3_ = bf16[128,512]{1,0:T(8,128)(2,1)S(1)} collective-permute-done((bf16[128,512]{1,0:T(8,128)(2,1)S(1)}, bf16[128,512]{1,0:T(8,128)(2,1)S(1)}, u32[]{:S(2)}, u32[]{:S(2)}) %collective-permute-start.17) | collective-permute-done | bytes 131104 | tf_op jit(solution)/shard_map/ppermute | solution.py:628
  54.9 6.2 %collective-permute-done.16.rest_2_ = bf16[128,512]{1,0:T(8,128)(2,1)S(1)} collective-permute-done((bf16[128,512]{1,0:T(8,128)(2,1)S(1)}, bf16[128,512]{1,0:T(8,128)(2,1)S(1)}, u32[]{:S(2)}, u32[]{:S(2)}) %collective-permute-start.16) | collective-permute-done | bytes 131104 | tf_op jit(solution)/shard_map/ppermute | solution.py:628
  61.1 5.0 %update_nodes.1 = (bf16[512,1920]{1,0:T(8,128)(2,1)S(1)}, bf16[512,1920]{1,0:T(8,128)(2,1)S(1)}, bf16[128,512]{1,0:T(8,128)(2,1)S(1)}, bf16[512,1024]{1,0:T(8,12...) custom-call(bf16[896,1920]{1,0:T(8,128)(2,1)S(1)} %get-tuple-element, ...), custom_call_target="tpu_custom_call" | custom-call | flops 20000000000 | bytes 12566528 | tf_op jit(solution)/shard_map/update_nodes/pallas_call | solution.py:610
  66.1 3.0 %collective-permute-start.21 = (bf16[128,512]{1,0:T(8,128)(2,1)S(1)}, bf16[128,512]{1,0:T(8,128)(2,1)S(1)}, u32[]{:S(2)}, u32[]{:S(2)}) collective-permute-start(bf16[128,512]{1,0:T(8,128)(2,1)S(1)} %get-tuple-element.137), channel_id=1, source_target_pairs={{0,8},{4,12},{8,0},{12,4},{1,9},{5,13},{9,1},{13,5},{2,10},{6,14},... | collective-permute-start | bytes 393224 | tf_op jit(solution)/shard_map/ppermute | solution.py:628
  70.5 2.5 %update_edges.1 = (bf16[15,192,128]{2,1,0:T(8,128)(2,1)}, bf16[192,1920]{1,0:T(8,128)(2,1)S(1)}, bf16[512,128]{1,0:T(8,128)(2,1)S(1)}, bf16[512,128]{1,0:T(8,128...) custom-call(bf16[15,192,128]{2,1,0:T(8,128)(2,1)S(1)} %bitcast.30, ...), custom_call_target="tpu_custom_call" | custom-call | bytes 12156928 | tf_op jit(solution)/shard_map/update_edges/pallas_call | solution.py:610
  73.0 5.5 %collective-permute-done.21.rest_2_ = bf16[128,512]{1,0:T(8,128)(2,1)S(1)} collective-permute-done((bf16[128,512]{1,0:T(8,128)(2,1)S(1)}, bf16[128,512]{1,0:T(8,128)(2,1)S(1)}, u32[]{:S(2)}, u32[]{:S(2)}) %collective-permute-start.21) | collective-permute-done | bytes 131104 | tf_op jit(solution)/shard_map/ppermute | solution.py:628
  87.6 3.2 %collective-permute-done.24.t2 = bf16[128,640]{1,0:T(8,128)(2,1)S(1)} collective-permute-done((bf16[128,640]{1,0:T(8,128)(2,1)S(1)}, bf16[128,640]{1,0:T(8,128)(2,1)S(1)}, u32[]{:S(2)}, u32[]{:S(2)}) %collective-permute-start.24) | collective-permute-done | bytes 163872 | tf_op jit(solution)/shard_map/ppermute | solution.py:628
  95.5 2.4 %collective-permute-done.28.t3._ = bf16[128,512]{1,0:T(8,128)(2,1)S(1)} collective-permute-done((bf16[128,512]{1,0:T(8,128)(2,1)S(1)}, bf16[128,512]{1,0:T(8,128)(2,1)S(1)}, u32[]{:S(2)}, u32[]{:S(2)}) %collective-permute-start.28) | collective-permute-done | bytes 131104 | tf_op jit(solution)/shard_map/ppermute | solution.py:628
  99.3 2.9 %message_backward.1 = (f32[128,512]{1,0:T(8,128)S(1)}, bf16[128,512]{1,0:T(8,128)(2,1)S(1)}, f32[1,512]{1,0:T(1,128)S(1)}, bf16[512,1920]{1,0:T(8,128)(2,1)S(1)}...) custom-call(bf16[128,512]{1,0:T(8,128)(2,1)S(1)} %get-tuple-element., ...), custom_call_target="tpu_custom_call" | custom-call | flops 20000000000 | bytes 10864640 | tf_op jit(solution)/shard_map/message_backward/pallas_call | solution.py:610
  102.8 3.0 %collective-permute-start.48 = (bf16[352,512]{1,0:T(8,128)(2,1)S(1)}, bf16[352,512]{1,0:T(8,128)(2,1)S(1)}, u32[]{:S(2)}, u32[]{:S(2)}) collective-permute-start(bf16[352,512]{1,0:T(8,128)(2,1)S(1)} %get-tuple-element.195), channel_id=1, source_target_pairs={{0,4},{4,0},{8,12},{12,8},{1,5},{5,1},{9,13},{13,9},{2,6},{6,2},{1... | collective-permute-start | bytes 1081352 | tf_op jit(solution)/shard_map/ppermute | solution.py:628
  109.3 2.8 %message_edges.1 = (f32[15,192,128]{2,1,0:T(8,128)}, f32[8,256]{1,0:T(8,128)S(1)}) custom-call(bf16[15,192,128]{2,1,0:T(8,128)(2,1)S(1)} %bitcast.31, bf16[512,1920]{1,0:T(8,128)(2,1)S(1)} %get-tuple-element.153.du_ref, bf16[192,1920]{1,0:T(8,128)(2,1)S(1)} %get-tuple-element.154.dq_ref, bf16[15,192,128]{2,1,0:T(8,128)(2,1)S(1)} %bitcast.34, ...), custom_call_target="tpu_custom_call" | custom-call | bytes 7036928 | tf_op jit(solution)/shard_map/message_edges/pallas_call | solution.py:610
  118.5 2.4 %collective-permute-start.34 = (bf16[128,128]{1,0:T(8,128)(2,1)S(1)}, bf16[128,128]{1,0:T(8,128)(2,1)S(1)}, u32[]{:S(2)}, u32[]{:S(2)}) collective-permute-start(bf16[128,128]{1,0:T(8,128)(2,1)S(1)} %get-tuple-element.167), channel_id=1, source_target_pairs={{0,8},{4,12},{8,0},{12,4},{1,9},{5,13},{9,1},{13,5},{2,10},{6,14},... | collective-permute-start | bytes 98312 | tf_op jit(solution)/shard_map/ppermute | solution.py:628
  122.5 4.9 %collective-permute-done.34.rest_2_ = bf16[128,128]{1,0:T(8,128)(2,1)S(1)} collective-permute-done((bf16[128,128]{1,0:T(8,128)(2,1)S(1)}, bf16[128,128]{1,0:T(8,128)(2,1)S(1)}, u32[]{:S(2)}, u32[]{:S(2)}) %collective-permute-start.34) | collective-permute-done | bytes 32800 | tf_op jit(solution)/shard_map/ppermute | solution.py:628
  133.9 4.2 %collective-permute-done.39.got_ref = bf16[352,128]{1,0:T(8,128)(2,1)S(1)} collective-permute-done((bf16[352,128]{1,0:T(8,128)(2,1)S(1)}, bf16[352,128]{1,0:T(8,128)(2,1)S(1)}, u32[]{:S(2)}, u32[]{:S(2)}) %collective-permute-start.39) | collective-permute-done | bytes 90144 | tf_op jit(solution)/shard_map/ppermute | solution.py:628
  143.6 9.7 %collective-permute-done.42.rest_3_ = bf16[288,128]{1,0:T(8,128)(2,1)S(1)} collective-permute-done((bf16[288,128]{1,0:T(8,128)(2,1)S(1)}, bf16[288,128]{1,0:T(8,128)(2,1)S(1)}, u32[]{:S(2)}, u32[]{:S(2)}) %collective-permute-start.42) | collective-permute-done | bytes 73760 | tf_op jit(solution)/shard_map/ppermute | solution.py:628
  (120 shorter events, 64.4 us)
Async XLA Ops:
  2.3 17.9 %collective-permute-start.3 = (bf16[128,2304]{1,0:T(8,128)(2,1)S(1)}, bf16[128,2304]{1,0:T(8,128)(2,1)S(1)}, u32[]{:S(2)}, u32[]{:S(2)}) collective-permute-start(bf16[128,2304]{1,0:T(8,128)(2,1)S(1)} %get-tuple-element.117.full_ref), channel_id=1, source_target_pairs={{0,1},{1,0},{2,3},{3,2},{16,18},{17,19},{18,16},{19,17},{4,5},{5,4... | collective-permute-start | bytes 1769480 | tf_op jit(solution)/shard_map/ppermute | solution.py:709
  8.9 11.0 %collective-permute-start.1 = (bf16[128,512]{1,0:T(8,128)(2,1)}, bf16[128,512]{1,0:T(8,128)(2,1)S(1)}, u32[]{:S(2)}, u32[]{:S(2)}) collective-permute-start(bf16[128,512]{1,0:T(8,128)(2,1)} %bitcast.36), channel_id=1, source_target_pairs={{0,8},{4,12},{8,0},{12,4},{1,9},{5,13},{9,1},{13,5},{2,10},{6,14},... | collective-permute-start | bytes 393224 | tf_op jit(solution)/shard_map/ppermute | solution.py:628
  8.9 11.0 %collective-permute-start = (bf16[128,512]{1,0:T(8,128)(2,1)}, bf16[128,512]{1,0:T(8,128)(2,1)S(1)}, u32[]{:S(2)}, u32[]{:S(2)}) collective-permute-start(bf16[128,512]{1,0:T(8,128)(2,1)} %bitcast.37), channel_id=1, source_target_pairs={{0,4},{4,0},{8,12},{12,8},{1,5},{5,1},{9,13},{13,9},{2,6},{6,2},{1... | collective-permute-start | bytes 393224 | tf_op jit(solution)/shard_map/ppermute | solution.py:628
  9.6 11.3 %collective-permute-start.4 = (bf16[128,1152]{1,0:T(8,128)(2,1)S(1)}, bf16[128,1152]{1,0:T(8,128)(2,1)S(1)}, u32[]{:S(2)}, u32[]{:S(2)}) collective-permute-start(bf16[128,1152]{1,0:T(8,128)(2,1)S(1)} %get-tuple-element.119), channel_id=1, source_target_pairs={{0,3},{1,2},{2,1},{3,0},{4,7},{5,6},{6,5},{7,4},{8,11},{9,10},{10,... | collective-permute-start | bytes 884744 | tf_op jit(solution)/shard_map/ppermute | solution.py:628
  40.6 10.4 %collective-permute-start.18 = (bf16[128,1024]{1,0:T(8,128)(2,1)S(1)}, bf16[128,1024]{1,0:T(8,128)(2,1)S(1)}, u32[]{:S(2)}, u32[]{:S(2)}) collective-permute-start(bf16[128,1024]{1,0:T(8,128)(2,1)S(1)} %collective-permute-done.10._.rest_5_), channel_id=1, source_target_pairs={{0,16},{16,0},{1,17},{17,1},{2,18},{18,2},{3,19},{19,3},{4,20},{20... | collective-permute-start | bytes 786440 | tf_op jit(solution)/shard_map/ppermute | solution.py:628
  40.6 10.4 %collective-permute-start.19 = (bf16[128,512]{1,0:T(8,128)(2,1)S(1)}, bf16[128,512]{1,0:T(8,128)(2,1)S(1)}, u32[]{:S(2)}, u32[]{:S(2)}) collective-permute-start(bf16[128,512]{1,0:T(8,128)(2,1)S(1)} %collective-permute-done.11.__.rest_6_), channel_id=1, source_target_pairs={{0,16},{16,0},{1,17},{17,1},{2,18},{18,2},{3,19},{19,3},{4,20},{20... | collective-permute-start | bytes 393224 | tf_op jit(solution)/shard_map/ppermute | solution.py:628
  50.2 10.8 %collective-permute-start.16 = (bf16[128,512]{1,0:T(8,128)(2,1)S(1)}, bf16[128,512]{1,0:T(8,128)(2,1)S(1)}, u32[]{:S(2)}, u32[]{:S(2)}) collective-permute-start(bf16[128,512]{1,0:T(8,128)(2,1)S(1)} %get-tuple-element.129.rest_0_.c_ref), channel_id=1, source_target_pairs={{0,8},{4,12},{8,0},{12,4},{1,9},{5,13},{9,1},{13,5},{2,10},{6,14},... | collective-permute-start | bytes 393224 | tf_op jit(solution)/shard_map/ppermute | solution.py:628
  50.2 10.8 %collective-permute-start.15 = (bf16[128,512]{1,0:T(8,128)(2,1)S(1)}, bf16[128,512]{1,0:T(8,128)(2,1)S(1)}, u32[]{:S(2)}, u32[]{:S(2)}) collective-permute-start(bf16[128,512]{1,0:T(8,128)(2,1)S(1)} %get-tuple-element.129.rest_0_.c_ref), channel_id=1, source_target_pairs={{0,4},{4,0},{8,12},{12,8},{1,5},{5,1},{9,13},{13,9},{2,6},{6,2},{1... | collective-permute-start | bytes 393224 | tf_op jit(solution)/shard_map/ppermute | solution.py:628
  66.1 12.4 %collective-permute-start.21 = (bf16[128,512]{1,0:T(8,128)(2,1)S(1)}, bf16[128,512]{1,0:T(8,128)(2,1)S(1)}, u32[]{:S(2)}, u32[]{:S(2)}) collective-permute-start(bf16[128,512]{1,0:T(8,128)(2,1)S(1)} %get-tuple-element.137), channel_id=1, source_target_pairs={{0,8},{4,12},{8,0},{12,4},{1,9},{5,13},{9,1},{13,5},{2,10},{6,14},... | collective-permute-start | bytes 393224 | tf_op jit(solution)/shard_map/ppermute | solution.py:628
  80.9 9.9 %collective-permute-start.24 = (bf16[128,640]{1,0:T(8,128)(2,1)S(1)}, bf16[128,640]{1,0:T(8,128)(2,1)S(1)}, u32[]{:S(2)}, u32[]{:S(2)}) collective-permute-start(bf16[128,640]{1,0:T(8,128)(2,1)S(1)} %get-tuple-element.142), channel_id=1, source_target_pairs={{0,2},{1,3},{2,0},{3,1},{4,6},{5,7},{6,4},{7,5},{8,10},{9,11},{10,... | collective-permute-start | bytes 491528 | tf_op jit(solution)/shard_map/ppermute | solution.py:628
  81.1 10.0 %collective-permute-start.25 = (bf16[128,640]{1,0:T(8,128)(2,1)S(1)}, bf16[128,640]{1,0:T(8,128)(2,1)S(1)}, u32[]{:S(2)}, u32[]{:S(2)}) collective-permute-start(bf16[128,640]{1,0:T(8,128)(2,1)S(1)} %get-tuple-element.143), channel_id=1, source_target_pairs={{0,3},{1,2},{2,1},{3,0},{4,7},{5,6},{6,5},{7,4},{8,11},{9,10},{10,... | collective-permute-start | bytes 491528 | tf_op jit(solution)/shard_map/ppermute | solution.py:628
  82.5 11.1 %collective-permute-start.44 = (bf16[512,128]{1,0:T(8,128)(2,1)S(1)}, bf16[512,128]{1,0:T(8,128)(2,1)S(1)}, u32[]{:S(2)}, u32[]{:S(2)}) collective-permute-start(bf16[512,128]{1,0:T(8,128)(2,1)S(1)} %get-tuple-element.189), channel_id=1, source_target_pairs={{0,1},{1,0},{2,3},{3,2},{4,5},{5,4},{6,7},{7,6},{8,9},{9,8},{10,11... | collective-permute-start | bytes 393224 | tf_op jit(solution)/shard_map/ppermute | solution.py:628
  84.4 11.1 %collective-permute-start.45 = (bf16[512,128]{1,0:T(8,128)(2,1)S(1)}, bf16[512,128]{1,0:T(8,128)(2,1)S(1)}, u32[]{:S(2)}, u32[]{:S(2)}) collective-permute-start(bf16[512,128]{1,0:T(8,128)(2,1)S(1)} %get-tuple-element.190), channel_id=1, source_target_pairs={{0,2},{1,3},{2,0},{3,1},{4,6},{5,7},{6,4},{7,5},{8,10},{9,11},{10,... | collective-permute-start | bytes 393224 | tf_op jit(solution)/shard_map/ppermute | solution.py:628
  86.1 9.4 %collective-permute-start.46 = (bf16[512,128]{1,0:T(8,128)(2,1)S(1)}, bf16[512,128]{1,0:T(8,128)(2,1)S(1)}, u32[]{:S(2)}, u32[]{:S(2)}) collective-permute-start(bf16[512,128]{1,0:T(8,128)(2,1)S(1)} %get-tuple-element.191), channel_id=1, source_target_pairs={{0,3},{1,2},{2,1},{3,0},{4,7},{5,6},{6,5},{7,4},{8,11},{9,10},{10,... | collective-permute-start | bytes 393224 | tf_op jit(solution)/shard_map/ppermute | solution.py:628
  102.8 11.4 %collective-permute-start.48 = (bf16[352,512]{1,0:T(8,128)(2,1)S(1)}, bf16[352,512]{1,0:T(8,128)(2,1)S(1)}, u32[]{:S(2)}, u32[]{:S(2)}) collective-permute-start(bf16[352,512]{1,0:T(8,128)(2,1)S(1)} %get-tuple-element.195), channel_id=1, source_target_pairs={{0,4},{4,0},{8,12},{12,8},{1,5},{5,1},{9,13},{13,9},{2,6},{6,2},{1... | collective-permute-start | bytes 1081352 | tf_op jit(solution)/shard_map/ppermute | solution.py:628
  105.8 11.0 %collective-permute-start.29 = (bf16[832,128]{1,0:T(8,128)(2,1)S(1)}, bf16[832,128]{1,0:T(8,128)(2,1)S(1)}, u32[]{:S(2)}, u32[]{:S(2)}) collective-permute-start(bf16[832,128]{1,0:T(8,128)(2,1)S(1)} %get-tuple-element.150), channel_id=1, source_target_pairs={{0,1},{1,0},{2,3},{3,2},{4,5},{5,4},{6,7},{7,6},{8,9},{9,8},{10,11... | collective-permute-start | bytes 638984 | tf_op jit(solution)/shard_map/ppermute | solution.py:628
  106.6 11.0 %collective-permute-start.30 = (bf16[832,128]{1,0:T(8,128)(2,1)S(1)}, bf16[832,128]{1,0:T(8,128)(2,1)S(1)}, u32[]{:S(2)}, u32[]{:S(2)}) collective-permute-start(bf16[832,128]{1,0:T(8,128)(2,1)S(1)} %get-tuple-element.151), channel_id=1, source_target_pairs={{0,2},{1,3},{2,0},{3,1},{4,6},{5,7},{6,4},{7,5},{8,10},{9,11},{10,... | collective-permute-start | bytes 638984 | tf_op jit(solution)/shard_map/ppermute | solution.py:628
  107.9 9.8 %collective-permute-start.31 = (bf16[832,128]{1,0:T(8,128)(2,1)S(1)}, bf16[832,128]{1,0:T(8,128)(2,1)S(1)}, u32[]{:S(2)}, u32[]{:S(2)}) collective-permute-start(bf16[832,128]{1,0:T(8,128)(2,1)S(1)} %get-tuple-element.152), channel_id=1, source_target_pairs={{0,3},{1,2},{2,1},{3,0},{4,7},{5,6},{6,5},{7,4},{8,11},{9,10},{10,... | collective-permute-start | bytes 638984 | tf_op jit(solution)/shard_map/ppermute | solution.py:628
  114.4 13.3 %collective-permute-start.49 = (bf16[176,512]{1,0:T(8,128)(2,1)S(1)}, bf16[176,512]{1,0:T(8,128)(2,1)S(1)}, u32[]{:S(2)}, u32[]{:S(2)}) collective-permute-start(bf16[176,512]{1,0:T(8,128)(2,1)S(1)} %get-tuple-element.197), channel_id=1, source_target_pairs={{0,8},{4,12},{8,0},{12,4},{1,9},{5,13},{9,1},{13,5},{2,10},{6,14},... | collective-permute-start | bytes 540680 | tf_op jit(solution)/shard_map/ppermute | solution.py:628
  127.7 11.4 %collective-permute-start.50 = (bf16[176,512]{1,0:T(8,128)(2,1)S(1)}, bf16[176,512]{1,0:T(8,128)(2,1)S(1)}, u32[]{:S(2)}, u32[]{:S(2)}) collective-permute-start(bf16[176,512]{1,0:T(8,128)(2,1)S(1)} %early_three.1.one_ref), channel_id=1, source_target_pairs={{0,8},{4,12},{8,0},{12,4},{1,9},{5,13},{9,1},{13,5},{2,10},{6,14},... | collective-permute-start | bytes 540680 | tf_op jit(solution)/shard_map/ppermute | solution.py:628
  139.2 15.6 %collective-permute-start.51 = (bf16[352,512]{1,0:T(8,128)(2,1)S(1)}, bf16[352,512]{1,0:T(8,128)(2,1)S(1)}, u32[]{:S(2)}, u32[]{:S(2)}) collective-permute-start(bf16[352,512]{1,0:T(8,128)(2,1)S(1)} %early_four.1.m0), channel_id=1, source_target_pairs={{0,4},{4,0},{8,12},{12,8},{1,5},{5,1},{9,13},{13,9},{2,6},{6,2},{1... | collective-permute-start | bytes 1081352 | tf_op jit(solution)/shard_map/ppermute | solution.py:628
  139.9 13.9 %collective-permute-start.41 = (bf16[640,128]{1,0:T(8,128)(2,1)S(1)}, bf16[640,128]{1,0:T(8,128)(2,1)S(1)}, u32[]{:S(2)}, u32[]{:S(2)}) collective-permute-start(bf16[640,128]{1,0:T(8,128)(2,1)S(1)} %get-tuple-element.176.rest_4_), channel_id=1, source_target_pairs={{0,8},{4,12},{8,0},{12,4},{1,9},{5,13},{9,1},{13,5},{2,10},{6,14},... | collective-permute-start | bytes 491528 | tf_op jit(solution)/shard_map/ppermute | solution.py:628
  142.1 11.2 %collective-permute-start.42 = (bf16[288,128]{1,0:T(8,128)(2,1)S(1)}, bf16[288,128]{1,0:T(8,128)(2,1)S(1)}, u32[]{:S(2)}, u32[]{:S(2)}) collective-permute-start(bf16[288,128]{1,0:T(8,128)(2,1)S(1)} %get-tuple-element.175.rest_0_._), channel_id=1, source_target_pairs={{0,12},{4,8},{8,4},{12,0},{1,13},{5,9},{9,5},{13,1},{2,14},{6,10},... | collective-permute-start | bytes 221192 | tf_op jit(solution)/shard_map/ppermute | solution.py:628
  143.6 10.2 %collective-permute-start.40 = (bf16[288,128]{1,0:T(8,128)(2,1)S(1)}, bf16[288,128]{1,0:T(8,128)(2,1)S(1)}, u32[]{:S(2)}, u32[]{:S(2)}) collective-permute-start(bf16[288,128]{1,0:T(8,128)(2,1)S(1)} %get-tuple-element.175.rest_0_._), channel_id=1, source_target_pairs={{0,4},{4,0},{8,12},{12,8},{1,5},{5,1},{9,13},{13,9},{2,6},{6,2},{1... | collective-permute-start | bytes 221192 | tf_op jit(solution)/shard_map/ppermute | solution.py:628
  (36 other events, 281.2 us)

commit v5 on v4

--- a/solution.py
+++ b/solution.py
@@ -120,7 +120,7 @@
         mix_ref[side : side + total, at] = onehot(idx, total)
 
 
-def node_close(h1_ref, p0, p1, p2, p3, gain_ref, h2_ref, c_ref, out_ref):
+def node_close(h1_ref, p0, p1, p2, p3, gain_ref, _, __, h2_ref, c_ref, out_ref):
     h2 = h1_ref[...] + sum_of((p0, p1, p2, p3))
     h2_ref[...] = h2
     hat, _ = normalize(h2)
@@ -244,7 +244,7 @@
 
 
 def node_forward(
-    s0, s1, s2, s3, nodes_ref, backs_ref, gain_ref, win_ref, wout_ref, _, __,
+    s0, s1, s2, s3, nodes_ref, backs_ref, gain_ref, win_ref, wout_ref,
     s_ref, h1_ref, b_ref, y_ref, slope_ref, part_ref
 ):
     width = nodes_ref.shape[1]
@@ -426,34 +426,32 @@
     out_ref[...] = (one_ref[...].astype(F32) + two_ref[...].astype(F32)).astype(BF16)
 
 
-def join(bit, one, two):
-    own = (lax.axis_index("graph") // bit) % 2
-    return jnp.where(own == 0, one, two), jnp.where(own == 0, two, one)
-
-
-def join_two(bit, one_ref, two_ref, _, out_ref):
-    half = one_ref.shape[0]
-    first, second = join(bit, one_ref[...], two_ref[...])
-    out_ref[:half, :] = first
-    out_ref[half:, :] = second
-
-
-def finish_early(bit, m0, m1, t0, t1, gin_ref, gout_ref, self_ref, edge_ref, other_ref, out_ref):
+def finish_early(near, *refs):
+    parts = 4 if near else 1
+    mine, theirs = refs[:parts], refs[parts : 2 * parts]
+    gin_ref, gout_ref, self_ref, edge_ref, other_ref, out_ref, one_ref, two_ref = refs[2 * parts :]
     width, side = gin_ref.shape[0], edge_ref.shape[0]
     part = (width + side) // 4
 
     def run(one, two):
-        for pair, large, top, low in ((one, gin_ref, self_ref, edge_ref), (two, gout_ref, other_ref, out_ref)):
-            pair = [r[...] for r in pair]
-            if bit:
-                pair = join(bit, *pair)
-            every = jnp.concatenate(pair, axis=0).astype(F32)
-            large[...] = every[:width]
-            small = jnp.concatenate([every[width : width + part, i * 128 : i * 128 + 128] for i in range(4)], axis=0)
+        for pieces, every, large, top, low in (
+            (one, one_ref, gin_ref, self_ref, edge_ref), (two, two_ref, gout_ref, other_ref, out_ref)
+        ):
+            size = pieces[0].shape[0]
+            for k, ref in enumerate(pieces):
+                if near:
+                    owner = lax.axis_index("graph") ^ k
+                    at = pl.multiple_of(((owner % 2) * 2 + owner // 2) * size, 16)
+                    every[pl.ds(at, size), :] = ref[...]
+                else:
+                    every[...] = ref[...]
+            large[...] = every[:width, :].astype(F32)
+            small = every[width : width + part, :].astype(F32)
+            small = jnp.concatenate([small[:, i * 128 : i * 128 + 128] for i in range(4)], axis=0)
             top[...] = small[:width]
             low[...] = small[width:]
 
-    by_core(lambda: run((m0, m1), (t0, t1)), lambda: run((t0, t1), (m0, m1)))
+    by_core(lambda: run(mine, theirs), lambda: run(theirs, mine))
 
 
 def message_backward(
@@ -532,7 +530,8 @@
     by_core(lambda: put(keep_ref, send_ref), lambda: put(send_ref, keep_ref))
 
 
-def node_finish(t0, t1, t2, t3, nodes_ref, dh1_ref, gain_ref, share_ref, late_ref, got_ref, out_ref, pack_ref, long_ref):
+def node_finish(t0, t1, t2, t3, nodes_ref, dh1_ref, gain_ref, share_ref, late_ref, got_ref, *rest):
+    out_ref, pack_ref, long_ref = rest[-3:]
     rows, width = dh1_ref.shape
     low = share_ref.shape[0]
     every = sum_of((t0, t1, t2, t3))
@@ -549,7 +548,7 @@
 
 
 def message_grads(parts, a_ref, *rest):
-    packs, (one_ref, two_ref, out_ref) = rest[:parts], rest[parts:]
+    packs, (one_ref, two_ref), out_ref = rest[:parts], rest[parts : parts + 2], rest[-1]
     rows = a_ref.shape[0] // parts
     width = a_ref.shape[1]
     size = packs[0].shape[0]
@@ -725,12 +724,12 @@
 
     pooled, h1, b, y, slope_f, h2_part = run(
         "node_forward", node_forward, 1,
-        partners(pooled_part, "mp", mp) + [node, backs, gains_n, ffn_in, ffn_out, (cross_later, AFTER), (diag_later, AFTER)],
+        partners(pooled_part, "mp", mp) + [node, backs, gains_n, ffn_in, ffn_out],
         [((rows, hidden), BF16), ((rows, width), F32), ((rows, width), BF16), ((rows, ff), BF16), ((rows, ff), BF16),
          ((rows, width), BF16)],
     )
     h2, c_own, nodes_out = run(
-        "node_close", node_close, 1, [h1] + partners(h2_part, "mp", mp) + [gains_n],
+        "node_close", node_close, 1, [h1] + partners(h2_part, "mp", mp) + [gains_n, (cross_later, AFTER), (diag_later, AFTER)],
         [((rows, width), F32), ((rows, width), BF16), ((rows, width), BF16)],
     )
     c_all = gather_rows(c_own)
@@ -807,33 +806,36 @@
     )
     if near:
         (own,) = run("early_three", sum_two, 1, [stay, go, (term, AFTER)], quarters)
-        go = swap(own, "graph", 2, graph)
+        early_sum = [own, swap(own, "graph", 1, graph), swap(own, "graph", 2, graph)]
+        early_order = [(v, AFTER) for v in early_sum[1:]]
+    else:
+        early_order = []
     none = jnp.zeros((half, shard), BF16)
     grad_nodes, pack, long = run(
         "node_finish", node_finish, 1,
-        partners(term, "mp", mp) + [node, dh1, gains_n, share, late, swap(late, "graph", 1, graph) if near else none],
+        partners(term, "mp", mp) + [node, dh1, gains_n, share, late, swap(late, "graph", 1, graph) if near else none] + early_order,
         [((rows, width), F32), ((2 * rows + width // 16, shard), BF16),
          ((2 * rows + width // 16 + half, shard), BF16)],
     )
     if near:
-        (own,) = run("early_four", functools.partial(join_two, 2), 1, [own, go, (pack, AFTER)], halves)
-        got = swap(own, "graph", 1, graph)
+        early_sum.append(swap(after(early_sum[2], pack), "graph", 1, graph))
         long_two = swap(long, "graph", 2, graph)
         packs = [pack, swap(pack, "graph", 1, graph), long_two, swap(pack, "graph", 3, graph)]
-        early_sum = [own, after(got, *packs[1:])]
+        early_end = [(early_sum[3], AFTER)]
     else:
         early = lax.psum(keep.astype(F32) + got.astype(F32), "graph").astype(BF16)
-        early_sum = [early[: size // 2], early[size // 2 :]]
-        packs, long_two = [pack], jnp.zeros_like(long)
+        early_sum = [early]
+        packs, long_two, early_end = [pack], jnp.zeros_like(long), []
     grad_in, grad_out, grad_us, grad_ue, grad_uo, grad_uout = run(
-        "finish_early", functools.partial(finish_early, 1 if near else 0), 1, early_sum + [swap(v, "dp", 1, cores) for v in early_sum],
+        "finish_early", functools.partial(finish_early, near), 1, early_sum + [swap(v, "dp", 1, cores) for v in early_sum],
         [((width, ff), F32), ((ff, width), F32), ((width, shard), F32), ((side, shard), F32), ((width, shard), F32),
          ((side, shard), F32)],
+        [pltpu.VMEM((size, ff), BF16)] * 2,
     )
     parts = len(packs)
     (part,) = run(
         "message_grads", functools.partial(message_grads, parts), 1,
-        [(a_all, pl.BlockSpec((parts * rows, width), lambda i: (0, 0)))] + packs + [long, long_two],
+        [(a_all, pl.BlockSpec((parts * rows, width), lambda i: (0, 0)))] + packs + [long, long_two] + early_end,
         [((2 * width + half + width // 16, shard), BF16)],
     )
     if not near:

time: 159 us -> 158 us (level)
  waiting for transfers between devices: 64.4 us -> 60.6 us
  starting transfers between devices: 62.8 us -> 65.6 us
    ppermute x52 -> x55, waiting for transfers between devices: 64.4 us -> 60.6 us  [swap(): return lax.ppermute(values, axis, [(i, i ^ bits) for i in range(size)])]
    ppermute x52 -> x55, starting transfers between devices: 59.5 us -> 61.1 us  [swap(): return lax.ppermute(values, axis, [(i, i ^ bits) for i in range(size)])]
    pallas_call x24 -> x23, Pallas kernels: 30.5 us -> 30.5 us  [call(): pl.pallas_call(body, grid=(grid,), in_specs=[s for _, s in ins], out_spec...]
  transfers between devices with their start and end apart: 54 -> 57, of which waited for: 22 -> 28; matrix products, arithmetic and copies ran while one was open for 0% -> 0% of each run, Pallas kernels for 13% -> 13%
where the time goes in v5:
time: 158 us
  starting transfers between devices  65.6 us (42%)
  waiting for transfers between devices  60.6 us (38%)
  Pallas kernels  30.5 us (19%)
    ppermute x55, starting transfers between devices, swap(): return lax.ppermute(values, axis, [(i, i ^ bits) for i in range(size)])  61.1 us
    ppermute x55, waiting for transfers between devices, swap(): return lax.ppermute(values, axis, [(i, i ^ bits) for i in range(size)])  60.6 us
    pallas_call x23, Pallas kernels, call(): pl.pallas_call(body, grid=(grid,), in_specs=[s for _, s in ins], out_spec...  30.5 us
    ppermute x2, starting transfers between devices, across(): return lax.ppermute(values, ('dp', 'mp'), pairs)  4.5 us
  transfers between devices with their start and end apart: 57, of which 28 were waited for; matrix products, arithmetic and copies ran while one was open for 0% of the time, Pallas kernels for 13%

profile of v5, /device:TPU:0, one launch (start us, length us, event | category | flops | bytes accessed | tf_op | source)
XLA Modules:
  0.0 157.7 jit_solution(6615139035308801478)
XLA Ops:
  2.2 3.0 %collective-permute-start.3 = (bf16[128,2304]{1,0:T(8,128)(2,1)S(1)}, bf16[128,2304]{1,0:T(8,128)(2,1)S(1)}, u32[]{:S(2)}, u32[]{:S(2)}) collective-permute-start(bf16[128,2304]{1,0:T(8,128)(2,1)S(1)} %get-tuple-element.117.full_ref), channel_id=1, source_target_pairs={{0,1},{1,0},{2,3},{3,2},{16,18},{17,19},{18,16},{19,17},{4,5},{5,4... | collective-permute-start | bytes 1769480 | tf_op jit(solution)/shard_map/ppermute | solution.py:708
  5.3 3.6 %collective-permute-start.2 = (bf16[128,512]{1,0:T(8,128)(2,1)}, bf16[128,512]{1,0:T(8,128)(2,1)S(1)}, u32[]{:S(2)}, u32[]{:S(2)}) collective-permute-start(bf16[128,512]{1,0:T(8,128)(2,1)} %bitcast.35), channel_id=1, source_target_pairs={{0,12},{4,8},{8,4},{12,0},{1,13},{5,9},{9,5},{13,1},{2,14},{6,10},... | collective-permute-start | bytes 393224 | tf_op jit(solution)/shard_map/ppermute | solution.py:627
  11.1 2.9 %edge_prep.1 = (bf16[896,1920]{1,0:T(8,128)(2,1)S(1)}, s32[1,512]{1,0:T(1,128)S(1)}, f32[2,192,128]{2,1,0:T(8,128)S(1)}, f32[8,512]{1,0:T(8,128)S(1)}, bf16[128,512]{1,0:T(8,128)(2,1)S(1)}) custom-call(bf16[15,192,128]{2,1,0:T(8,128)(2,1)} %bitcast.29, s32[60,1,128]{2,1,0:T(1,128)} %bitcast.44, s32[1,512]{1,0:T(1,128)} %res_ref.1, f32[1,192]{1,0:T(1,128)} %bitcast.48, ...), custom_call_target="tpu_custom_call" | custom-call | bytes 4695552 | tf_op jit(solution)/shard_map/edge_prep/pallas_call | solution.py:609
  14.0 5.9 %collective-permute-done.1.refs_2_ = bf16[128,512]{1,0:T(8,128)(2,1)S(1)} collective-permute-done((bf16[128,512]{1,0:T(8,128)(2,1)}, bf16[128,512]{1,0:T(8,128)(2,1)S(1)}, u32[]{:S(2)}, u32[]{:S(2)}) %collective-permute-start.1) | collective-permute-done | bytes 131104 | tf_op jit(solution)/shard_map/ppermute | solution.py:627
  22.7 3.7 %message_forward.1 = (bf16[512,1920]{1,0:T(8,128)(2,1)S(1)}, bf16[128,512]{1,0:T(8,128)(2,1)S(1)}, bf16[512,1152]{1,0:T(8,128)(2,1)S(1)}, bf16[512,1152]{1,0:T(8,128)(2,1)S(1)}) custom-call(bf16[896,1920]{1,0:T(8,128)(2,1)S(1)} %get-tuple-element.113.mix_ref, s32[1,512]{1,0:T(1,128)S(1)} %get-tuple-element.114.mask_ref, bf16[512,512]{1,0:T(8,128)(2,1)S(1)} %row_prep.1.a_ref, ...), custom_call_target="tpu_custom_call" | custom-call | flops 20000000000 | bytes 10782720 | tf_op jit(solution)/shard_map/message_forward/pallas_call | solution.py:609
  31.4 2.4 %collective-permute-done.9.s3 = bf16[128,512]{1,0:T(8,128)(2,1)S(1)} collective-permute-done((bf16[128,512]{1,0:T(8,128)(2,1)S(1)}, bf16[128,512]{1,0:T(8,128)(2,1)S(1)}, u32[]{:S(2)}, u32[]{:S(2)}) %collective-permute-start.9) | collective-permute-done | bytes 131104 | tf_op jit(solution)/shard_map/ppermute | solution.py:627
  33.8 2.7 %collective-permute-done.8.s2 = bf16[128,512]{1,0:T(8,128)(2,1)S(1)} collective-permute-done((bf16[128,512]{1,0:T(8,128)(2,1)S(1)}, bf16[128,512]{1,0:T(8,128)(2,1)S(1)}, u32[]{:S(2)}, u32[]{:S(2)}) %collective-permute-start.8) | collective-permute-done | bytes 131104 | tf_op jit(solution)/shard_map/ppermute | solution.py:627
  41.4 3.3 %collective-permute-done.12.p3 = bf16[128,512]{1,0:T(8,128)(2,1)S(1)} collective-permute-done((bf16[128,512]{1,0:T(8,128)(2,1)S(1)}, bf16[128,512]{1,0:T(8,128)(2,1)S(1)}, u32[]{:S(2)}, u32[]{:S(2)}) %collective-permute-start.12) | collective-permute-done | bytes 131104 | tf_op jit(solution)/shard_map/ppermute | solution.py:627
  47.2 3.4 %collective-permute-start.17 = (bf16[128,512]{1,0:T(8,128)(2,1)S(1)}, bf16[128,512]{1,0:T(8,128)(2,1)S(1)}, u32[]{:S(2)}, u32[]{:S(2)}) collective-permute-start(bf16[128,512]{1,0:T(8,128)(2,1)S(1)} %get-tuple-element.129.rest_0_.c_ref), channel_id=1, source_target_pairs={{0,12},{4,8},{8,4},{12,0},{1,13},{5,9},{9,5},{13,1},{2,14},{6,10},... | collective-permute-start | bytes 393224 | tf_op jit(solution)/shard_map/ppermute | solution.py:627
  51.6 3.9 %collective-permute-done.17.rest_3_ = bf16[128,512]{1,0:T(8,128)(2,1)S(1)} collective-permute-done((bf16[128,512]{1,0:T(8,128)(2,1)S(1)}, bf16[128,512]{1,0:T(8,128)(2,1)S(1)}, u32[]{:S(2)}, u32[]{:S(2)}) %collective-permute-start.17) | collective-permute-done | bytes 131104 | tf_op jit(solution)/shard_map/ppermute | solution.py:627
  55.5 6.4 %collective-permute-done.16.rest_2_ = bf16[128,512]{1,0:T(8,128)(2,1)S(1)} collective-permute-done((bf16[128,512]{1,0:T(8,128)(2,1)S(1)}, bf16[128,512]{1,0:T(8,128)(2,1)S(1)}, u32[]{:S(2)}, u32[]{:S(2)}) %collective-permute-start.16) | collective-permute-done | bytes 131104 | tf_op jit(solution)/shard_map/ppermute | solution.py:627
  61.9 5.0 %update_nodes.1 = (bf16[512,1920]{1,0:T(8,128)(2,1)S(1)}, bf16[512,1920]{1,0:T(8,128)(2,1)S(1)}, bf16[128,512]{1,0:T(8,128)(2,1)S(1)}, bf16[512,1024]{1,0:T(8,12...) custom-call(bf16[896,1920]{1,0:T(8,128)(2,1)S(1)} %get-tuple-element, ...), custom_call_target="tpu_custom_call" | custom-call | flops 20000000000 | bytes 12566528 | tf_op jit(solution)/shard_map/update_nodes/pallas_call | solution.py:609
  66.9 3.0 %collective-permute-start.21 = (bf16[128,512]{1,0:T(8,128)(2,1)S(1)}, bf16[128,512]{1,0:T(8,128)(2,1)S(1)}, u32[]{:S(2)}, u32[]{:S(2)}) collective-permute-start(bf16[128,512]{1,0:T(8,128)(2,1)S(1)} %get-tuple-element.137), channel_id=1, source_target_pairs={{0,8},{4,12},{8,0},{12,4},{1,9},{5,13},{9,1},{13,5},{2,10},{6,14},... | collective-permute-start | bytes 393224 | tf_op jit(solution)/shard_map/ppermute | solution.py:627
  71.3 2.5 %update_edges.1 = (bf16[15,192,128]{2,1,0:T(8,128)(2,1)}, bf16[192,1920]{1,0:T(8,128)(2,1)S(1)}, bf16[512,128]{1,0:T(8,128)(2,1)S(1)}, bf16[512,128]{1,0:T(8,128...) custom-call(bf16[15,192,128]{2,1,0:T(8,128)(2,1)S(1)} %bitcast.30, ...), custom_call_target="tpu_custom_call" | custom-call | bytes 12156928 | tf_op jit(solution)/shard_map/update_edges/pallas_call | solution.py:609
  73.8 5.8 %collective-permute-done.21.rest_2_ = bf16[128,512]{1,0:T(8,128)(2,1)S(1)} collective-permute-done((bf16[128,512]{1,0:T(8,128)(2,1)S(1)}, bf16[128,512]{1,0:T(8,128)(2,1)S(1)}, u32[]{:S(2)}, u32[]{:S(2)}) %collective-permute-start.21) | collective-permute-done | bytes 131104 | tf_op jit(solution)/shard_map/ppermute | solution.py:627
  92.5 2.0 %collective-permute-start.27 = (bf16[128,512]{1,0:T(8,128)(2,1)S(1)}, bf16[128,512]{1,0:T(8,128)(2,1)S(1)}, u32[]{:S(2)}, u32[]{:S(2)}) collective-permute-start(bf16[128,512]{1,0:T(8,128)(2,1)S(1)} %get-tuple-element.146.t0), channel_id=1, source_target_pairs={{0,2},{1,3},{2,0},{3,1},{4,6},{5,7},{6,4},{7,5},{8,10},{9,11},{10,... | collective-permute-start | bytes 393224 | tf_op jit(solution)/shard_map/ppermute | solution.py:627
  99.5 2.9 %message_backward.1 = (f32[128,512]{1,0:T(8,128)S(1)}, bf16[128,512]{1,0:T(8,128)(2,1)S(1)}, f32[1,512]{1,0:T(1,128)S(1)}, bf16[512,1920]{1,0:T(8,128)(2,1)S(1)}...) custom-call(bf16[128,512]{1,0:T(8,128)(2,1)S(1)} %get-tuple-element., ...), custom_call_target="tpu_custom_call" | custom-call | flops 20000000000 | bytes 10864640 | tf_op jit(solution)/shard_map/message_backward/pallas_call | solution.py:609
  103.0 2.8 %collective-permute-start.44 = (bf16[352,512]{1,0:T(8,128)(2,1)S(1)}, bf16[352,512]{1,0:T(8,128)(2,1)S(1)}, u32[]{:S(2)}, u32[]{:S(2)}) collective-permute-start(bf16[352,512]{1,0:T(8,128)(2,1)S(1)} %get-tuple-element.184), channel_id=1, source_target_pairs={{0,4},{4,0},{8,12},{12,8},{1,5},{5,1},{9,13},{13,9},{2,6},{6,2},{1... | collective-permute-start | bytes 1081352 | tf_op jit(solution)/shard_map/ppermute | solution.py:627
  109.3 2.8 %message_edges.1 = (f32[15,192,128]{2,1,0:T(8,128)}, f32[8,256]{1,0:T(8,128)S(1)}) custom-call(bf16[15,192,128]{2,1,0:T(8,128)(2,1)S(1)} %bitcast.31, bf16[512,1920]{1,0:T(8,128)(2,1)S(1)} %get-tuple-element.153.du_ref, bf16[192,1920]{1,0:T(8,128)(2,1)S(1)} %get-tuple-element.154.dq_ref, bf16[15,192,128]{2,1,0:T(8,128)(2,1)S(1)} %bitcast.34, ...), custom_call_target="tpu_custom_call" | custom-call | bytes 7036928 | tf_op jit(solution)/shard_map/message_edges/pallas_call | solution.py:609
  114.3 2.5 %collective-permute-start.45 = (bf16[176,512]{1,0:T(8,128)(2,1)S(1)}, bf16[176,512]{1,0:T(8,128)(2,1)S(1)}, u32[]{:S(2)}, u32[]{:S(2)}) collective-permute-start(bf16[176,512]{1,0:T(8,128)(2,1)S(1)} %get-tuple-element.186), channel_id=1, source_target_pairs={{0,8},{4,12},{8,0},{12,4},{1,9},{5,13},{9,1},{13,5},{2,10},{6,14},... | collective-permute-start | bytes 540680 | tf_op jit(solution)/shard_map/ppermute | solution.py:627
  118.7 2.5 %collective-permute-start.34 = (bf16[128,128]{1,0:T(8,128)(2,1)S(1)}, bf16[128,128]{1,0:T(8,128)(2,1)S(1)}, u32[]{:S(2)}, u32[]{:S(2)}) collective-permute-start(bf16[128,128]{1,0:T(8,128)(2,1)S(1)} %get-tuple-element.167), channel_id=1, source_target_pairs={{0,8},{4,12},{8,0},{12,4},{1,9},{5,13},{9,1},{13,5},{2,10},{6,14},... | collective-permute-start | bytes 98312 | tf_op jit(solution)/shard_map/ppermute | solution.py:627
  123.9 3.2 %collective-permute-done.34.rest_2_ = bf16[128,128]{1,0:T(8,128)(2,1)S(1)} collective-permute-done((bf16[128,128]{1,0:T(8,128)(2,1)S(1)}, bf16[128,128]{1,0:T(8,128)(2,1)S(1)}, u32[]{:S(2)}, u32[]{:S(2)}) %collective-permute-start.34) | collective-permute-done | bytes 32800 | tf_op jit(solution)/shard_map/ppermute | solution.py:627
  135.0 2.6 %collective-permute-done.38.t3 = bf16[144,512]{1,0:T(8,128)(2,1)S(1)} collective-permute-done((bf16[144,512]{1,0:T(8,128)(2,1)S(1)}, bf16[144,512]{1,0:T(8,128)(2,1)S(1)}, u32[]{:S(2)}, u32[]{:S(2)}) %collective-permute-start.38) | collective-permute-done | bytes 147488 | tf_op jit(solution)/shard_map/ppermute | solution.py:627
  145.1 6.6 %collective-permute-done.50.rest_3_ = bf16[288,128]{1,0:T(8,128)(2,1)S(1)} collective-permute-done((bf16[288,128]{1,0:T(8,128)(2,1)S(1)}, bf16[288,128]{1,0:T(8,128)(2,1)S(1)}, u32[]{:S(2)}, u32[]{:S(2)}) %collective-permute-start.50) | collective-permute-done | bytes 73760 | tf_op jit(solution)/shard_map/ppermute | solution.py:627
  (125 shorter events, 71.4 us)
Async XLA Ops:
  2.2 17.9 %collective-permute-start.3 = (bf16[128,2304]{1,0:T(8,128)(2,1)S(1)}, bf16[128,2304]{1,0:T(8,128)(2,1)S(1)}, u32[]{:S(2)}, u32[]{:S(2)}) collective-permute-start(bf16[128,2304]{1,0:T(8,128)(2,1)S(1)} %get-tuple-element.117.full_ref), channel_id=1, source_target_pairs={{0,1},{1,0},{2,3},{3,2},{16,18},{17,19},{18,16},{19,17},{4,5},{5,4... | collective-permute-start | bytes 1769480 | tf_op jit(solution)/shard_map/ppermute | solution.py:708
  8.9 11.0 %collective-permute-start.1 = (bf16[128,512]{1,0:T(8,128)(2,1)}, bf16[128,512]{1,0:T(8,128)(2,1)S(1)}, u32[]{:S(2)}, u32[]{:S(2)}) collective-permute-start(bf16[128,512]{1,0:T(8,128)(2,1)} %bitcast.36), channel_id=1, source_target_pairs={{0,8},{4,12},{8,0},{12,4},{1,9},{5,13},{9,1},{13,5},{2,10},{6,14},... | collective-permute-start | bytes 393224 | tf_op jit(solution)/shard_map/ppermute | solution.py:627
  8.9 11.0 %collective-permute-start = (bf16[128,512]{1,0:T(8,128)(2,1)}, bf16[128,512]{1,0:T(8,128)(2,1)S(1)}, u32[]{:S(2)}, u32[]{:S(2)}) collective-permute-start(bf16[128,512]{1,0:T(8,128)(2,1)} %bitcast.37), channel_id=1, source_target_pairs={{0,4},{4,0},{8,12},{12,8},{1,5},{5,1},{9,13},{13,9},{2,6},{6,2},{1... | collective-permute-start | bytes 393224 | tf_op jit(solution)/shard_map/ppermute | solution.py:627
  9.6 11.3 %collective-permute-start.4 = (bf16[128,1152]{1,0:T(8,128)(2,1)S(1)}, bf16[128,1152]{1,0:T(8,128)(2,1)S(1)}, u32[]{:S(2)}, u32[]{:S(2)}) collective-permute-start(bf16[128,1152]{1,0:T(8,128)(2,1)S(1)} %get-tuple-element.119), channel_id=1, source_target_pairs={{0,3},{1,2},{2,1},{3,0},{4,7},{5,6},{6,5},{7,4},{8,11},{9,10},{10,... | collective-permute-start | bytes 884744 | tf_op jit(solution)/shard_map/ppermute | solution.py:627
  20.9 20.0 %collective-permute-start.13 = (bf16[128,1024]{1,0:T(8,128)(2,1)S(1)}, bf16[128,1024]{1,0:T(8,128)(2,1)S(1)}, u32[]{:S(2)}, u32[]{:S(2)}) collective-permute-start(bf16[128,1024]{1,0:T(8,128)(2,1)S(1)} %get-tuple-element.125.rest_4_), channel_id=1, source_target_pairs={{0,1},{1,0},{2,3},{3,2},{16,18},{17,19},{18,16},{19,17},{4,5},{5,4... | collective-permute-start | bytes 786440 | tf_op jit(solution)/shard_map/ppermute | solution.py:708
  30.0 11.0 %collective-permute-start.14 = (bf16[128,512]{1,0:T(8,128)(2,1)S(1)}, bf16[128,512]{1,0:T(8,128)(2,1)S(1)}, u32[]{:S(2)}, u32[]{:S(2)}) collective-permute-start(bf16[128,512]{1,0:T(8,128)(2,1)S(1)} %get-tuple-element.126), channel_id=1, source_target_pairs={{0,3},{1,2},{2,1},{3,0},{4,7},{5,6},{6,5},{7,4},{8,11},{9,10},{10,... | collective-permute-start | bytes 393224 | tf_op jit(solution)/shard_map/ppermute | solution.py:627
  40.9 10.7 %collective-permute-start.18 = (bf16[128,1024]{1,0:T(8,128)(2,1)S(1)}, bf16[128,1024]{1,0:T(8,128)(2,1)S(1)}, u32[]{:S(2)}, u32[]{:S(2)}) collective-permute-start(bf16[128,1024]{1,0:T(8,128)(2,1)S(1)} %collective-permute-done.13._.rest_5_), channel_id=1, source_target_pairs={{0,16},{16,0},{1,17},{17,1},{2,18},{18,2},{3,19},{19,3},{4,20},{20... | collective-permute-start | bytes 786440 | tf_op jit(solution)/shard_map/ppermute | solution.py:627
  40.9 10.7 %collective-permute-start.19 = (bf16[128,512]{1,0:T(8,128)(2,1)S(1)}, bf16[128,512]{1,0:T(8,128)(2,1)S(1)}, u32[]{:S(2)}, u32[]{:S(2)}) collective-permute-start(bf16[128,512]{1,0:T(8,128)(2,1)S(1)} %collective-permute-done.14.__.rest_6_), channel_id=1, source_target_pairs={{0,16},{16,0},{1,17},{17,1},{2,18},{18,2},{3,19},{19,3},{4,20},{20... | collective-permute-start | bytes 393224 | tf_op jit(solution)/shard_map/ppermute | solution.py:627
  50.6 11.3 %collective-permute-start.16 = (bf16[128,512]{1,0:T(8,128)(2,1)S(1)}, bf16[128,512]{1,0:T(8,128)(2,1)S(1)}, u32[]{:S(2)}, u32[]{:S(2)}) collective-permute-start(bf16[128,512]{1,0:T(8,128)(2,1)S(1)} %get-tuple-element.129.rest_0_.c_ref), channel_id=1, source_target_pairs={{0,8},{4,12},{8,0},{12,4},{1,9},{5,13},{9,1},{13,5},{2,10},{6,14},... | collective-permute-start | bytes 393224 | tf_op jit(solution)/shard_map/ppermute | solution.py:627
  50.6 11.3 %collective-permute-start.15 = (bf16[128,512]{1,0:T(8,128)(2,1)S(1)}, bf16[128,512]{1,0:T(8,128)(2,1)S(1)}, u32[]{:S(2)}, u32[]{:S(2)}) collective-permute-start(bf16[128,512]{1,0:T(8,128)(2,1)S(1)} %get-tuple-element.129.rest_0_.c_ref), channel_id=1, source_target_pairs={{0,4},{4,0},{8,12},{12,8},{1,5},{5,1},{9,13},{13,9},{2,6},{6,2},{1... | collective-permute-start | bytes 393224 | tf_op jit(solution)/shard_map/ppermute | solution.py:627
  66.9 12.7 %collective-permute-start.21 = (bf16[128,512]{1,0:T(8,128)(2,1)S(1)}, bf16[128,512]{1,0:T(8,128)(2,1)S(1)}, u32[]{:S(2)}, u32[]{:S(2)}) collective-permute-start(bf16[128,512]{1,0:T(8,128)(2,1)S(1)} %get-tuple-element.137), channel_id=1, source_target_pairs={{0,8},{4,12},{8,0},{12,4},{1,9},{5,13},{9,1},{13,5},{2,10},{6,14},... | collective-permute-start | bytes 393224 | tf_op jit(solution)/shard_map/ppermute | solution.py:627
  70.0 9.6 %collective-permute-start.22 = (bf16[128,512]{1,0:T(8,128)(2,1)S(1)}, bf16[128,512]{1,0:T(8,128)(2,1)S(1)}, u32[]{:S(2)}, u32[]{:S(2)}) collective-permute-start(bf16[128,512]{1,0:T(8,128)(2,1)S(1)} %get-tuple-element.138), channel_id=1, source_target_pairs={{0,12},{4,8},{8,4},{12,0},{1,13},{5,9},{9,5},{13,1},{2,14},{6,10},... | collective-permute-start | bytes 393224 | tf_op jit(solution)/shard_map/ppermute | solution.py:627
  83.5 11.1 %collective-permute-start.40 = (bf16[512,128]{1,0:T(8,128)(2,1)S(1)}, bf16[512,128]{1,0:T(8,128)(2,1)S(1)}, u32[]{:S(2)}, u32[]{:S(2)}) collective-permute-start(bf16[512,128]{1,0:T(8,128)(2,1)S(1)} %get-tuple-element.178), channel_id=1, source_target_pairs={{0,1},{1,0},{2,3},{3,2},{4,5},{5,4},{6,7},{7,6},{8,9},{9,8},{10,11... | collective-permute-start | bytes 393224 | tf_op jit(solution)/shard_map/ppermute | solution.py:627
  83.6 11.0 %collective-permute-start.41 = (bf16[512,128]{1,0:T(8,128)(2,1)S(1)}, bf16[512,128]{1,0:T(8,128)(2,1)S(1)}, u32[]{:S(2)}, u32[]{:S(2)}) collective-permute-start(bf16[512,128]{1,0:T(8,128)(2,1)S(1)} %get-tuple-element.179), channel_id=1, source_target_pairs={{0,2},{1,3},{2,0},{3,1},{4,6},{5,7},{6,4},{7,5},{8,10},{9,11},{10,... | collective-permute-start | bytes 393224 | tf_op jit(solution)/shard_map/ppermute | solution.py:627
  103.0 11.1 %collective-permute-start.44 = (bf16[352,512]{1,0:T(8,128)(2,1)S(1)}, bf16[352,512]{1,0:T(8,128)(2,1)S(1)}, u32[]{:S(2)}, u32[]{:S(2)}) collective-permute-start(bf16[352,512]{1,0:T(8,128)(2,1)S(1)} %get-tuple-element.184), channel_id=1, source_target_pairs={{0,4},{4,0},{8,12},{12,8},{1,5},{5,1},{9,13},{13,9},{2,6},{6,2},{1... | collective-permute-start | bytes 1081352 | tf_op jit(solution)/shard_map/ppermute | solution.py:627
  105.8 10.9 %collective-permute-start.29 = (bf16[832,128]{1,0:T(8,128)(2,1)S(1)}, bf16[832,128]{1,0:T(8,128)(2,1)S(1)}, u32[]{:S(2)}, u32[]{:S(2)}) collective-permute-start(bf16[832,128]{1,0:T(8,128)(2,1)S(1)} %get-tuple-element.150), channel_id=1, source_target_pairs={{0,1},{1,0},{2,3},{3,2},{4,5},{5,4},{6,7},{7,6},{8,9},{9,8},{10,11... | collective-permute-start | bytes 638984 | tf_op jit(solution)/shard_map/ppermute | solution.py:627
  106.9 11.0 %collective-permute-start.30 = (bf16[832,128]{1,0:T(8,128)(2,1)S(1)}, bf16[832,128]{1,0:T(8,128)(2,1)S(1)}, u32[]{:S(2)}, u32[]{:S(2)}) collective-permute-start(bf16[832,128]{1,0:T(8,128)(2,1)S(1)} %get-tuple-element.151), channel_id=1, source_target_pairs={{0,2},{1,3},{2,0},{3,1},{4,6},{5,7},{6,4},{7,5},{8,10},{9,11},{10,... | collective-permute-start | bytes 638984 | tf_op jit(solution)/shard_map/ppermute | solution.py:627
  107.7 10.2 %collective-permute-start.31 = (bf16[832,128]{1,0:T(8,128)(2,1)S(1)}, bf16[832,128]{1,0:T(8,128)(2,1)S(1)}, u32[]{:S(2)}, u32[]{:S(2)}) collective-permute-start(bf16[832,128]{1,0:T(8,128)(2,1)S(1)} %get-tuple-element.152), channel_id=1, source_target_pairs={{0,3},{1,2},{2,1},{3,0},{4,7},{5,6},{6,5},{7,4},{8,11},{9,10},{10,... | collective-permute-start | bytes 638984 | tf_op jit(solution)/shard_map/ppermute | solution.py:627
  114.3 14.1 %collective-permute-start.45 = (bf16[176,512]{1,0:T(8,128)(2,1)S(1)}, bf16[176,512]{1,0:T(8,128)(2,1)S(1)}, u32[]{:S(2)}, u32[]{:S(2)}) collective-permute-start(bf16[176,512]{1,0:T(8,128)(2,1)S(1)} %get-tuple-element.186), channel_id=1, source_target_pairs={{0,8},{4,12},{8,0},{12,4},{1,9},{5,13},{9,1},{13,5},{2,10},{6,14},... | collective-permute-start | bytes 540680 | tf_op jit(solution)/shard_map/ppermute | solution.py:627
  118.2 8.9 %collective-permute-start.32 = (bf16[352,128]{1,0:T(8,128)(2,1)S(1)}, bf16[352,128]{1,0:T(8,128)(2,1)S(1)}, u32[]{:S(2)}, u32[]{:S(2)}) collective-permute-start(bf16[352,128]{1,0:T(8,128)(2,1)S(1)} %get-tuple-element.164), channel_id=1, source_target_pairs={{0,16},{16,0},{1,17},{17,1},{2,18},{18,2},{3,19},{19,3},{4,20},{20... | collective-permute-start | bytes 270344 | tf_op jit(solution)/shard_map/ppermute | solution.py:627
  128.4 11.1 %collective-permute-start.47 = (bf16[176,512]{1,0:T(8,128)(2,1)S(1)}, bf16[176,512]{1,0:T(8,128)(2,1)S(1)}, u32[]{:S(2)}, u32[]{:S(2)}) collective-permute-start(bf16[176,512]{1,0:T(8,128)(2,1)S(1)} %early_three.1.refs_0_), channel_id=1, source_target_pairs={{0,8},{4,12},{8,0},{12,4},{1,9},{5,13},{9,1},{13,5},{2,10},{6,14},... | collective-permute-start | bytes 540680 | tf_op jit(solution)/shard_map/ppermute | solution.py:627
  130.0 9.4 %collective-permute-start.46 = (bf16[176,512]{1,0:T(8,128)(2,1)S(1)}, bf16[176,512]{1,0:T(8,128)(2,1)S(1)}, u32[]{:S(2)}, u32[]{:S(2)}) collective-permute-start(bf16[176,512]{1,0:T(8,128)(2,1)S(1)} %early_three.1.refs_0_), channel_id=1, source_target_pairs={{0,4},{4,0},{8,12},{12,8},{1,5},{5,1},{9,13},{13,9},{2,6},{6,2},{1... | collective-permute-start | bytes 540680 | tf_op jit(solution)/shard_map/ppermute | solution.py:627
  140.5 11.2 %collective-permute-start.51 = (bf16[176,512]{1,0:T(8,128)(2,1)S(1)}, bf16[176,512]{1,0:T(8,128)(2,1)S(1)}, u32[]{:S(2)}, u32[]{:S(2)}) collective-permute-start(bf16[176,512]{1,0:T(8,128)(2,1)S(1)} %collective-permute-done.47.rest_1_.refs_2_), channel_id=1, source_target_pairs={{0,4},{4,0},{8,12},{12,8},{1,5},{5,1},{9,13},{13,9},{2,6},{6,2},{1... | collective-permute-start | bytes 540680 | tf_op jit(solution)/shard_map/ppermute | solution.py:627
  141.6 10.1 %collective-permute-start.49 = (bf16[640,128]{1,0:T(8,128)(2,1)S(1)}, bf16[640,128]{1,0:T(8,128)(2,1)S(1)}, u32[]{:S(2)}, u32[]{:S(2)}) collective-permute-start(bf16[640,128]{1,0:T(8,128)(2,1)S(1)} %get-tuple-element.190.rest_4_), channel_id=1, source_target_pairs={{0,8},{4,12},{8,0},{12,4},{1,9},{5,13},{9,1},{13,5},{2,10},{6,14},... | collective-permute-start | bytes 491528 | tf_op jit(solution)/shard_map/ppermute | solution.py:627
  (39 other events, 293.1 us)
